TPU v7x, 32 devices: a whole 2x2x4 slice. The times are simulated.
32 devices in a mesh: rep: 8 (over y, x, core), shard: 4 (over z).
Axes of the slice: x: 2, y: 2, z: 4, core: 2. Of those that a mesh axis runs over, the one named last changes fastest.
Arguments:
- tokens: bfloat16 [8192, 2048], P(('rep', 'shard')), may hold values from -11 to 11, as said below
- cotangent: bfloat16 [8192, 2048], P(('rep', 'shard')), may hold values from -6 to 6
- segment_ids: int32 [8192], P(('rep', 'shard')), may hold values from 0 to 4, as said below
- expert_ids: int32 [8192, 2], P(('rep', 'shard')), may hold values from 0 to 3, all different within a row; in each aligned block of 256 rows (0 to 255, 256 to 511, ...) at most 192 rows name the same one
- norm_gain: float32 [2048], replicated, may hold values from 0.1 to 1.9
- w_query: bfloat16 [2048, 2048], P('shard'), may hold values from -0.125 to 0.125
- w_key: bfloat16 [2048, 2048], P('shard'), may hold values from -0.125 to 0.125
- w_value: bfloat16 [2048, 2048], P('shard'), may hold values from -0.125 to 0.125
- w_output: bfloat16 [2048, 2048], P('shard'), may hold values from -1.5 to 1.5
- query_gain: float32 [128], replicated, may hold values from 0.1 to 1.9
- key_gain: float32 [128], replicated, may hold values from 0.1 to 1.9
- ffn_norm_gain: float32 [2048], replicated, may hold values from 0.1 to 1.9
- w_router: bfloat16 [2048, 4], replicated, may hold values from -0.09375 to 0.09375
- w_gate: bfloat16 [4, 2048, 1024], P(None, 'shard'), may hold values from -0.125 to 0.125
- w_up: bfloat16 [4, 2048, 1024], P(None, 'shard'), may hold values from -0.125 to 0.125
- w_down: bfloat16 [4, 1024, 2048], P(None, 'shard'), may hold values from -0.5 to 0.5
Outputs:
- output: bfloat16 [8192, 2048], P(('rep', 'shard'))
- input_grad: bfloat16 [8192, 2048], P(('rep', 'shard'))
- grad_norm_gain: float32 [2048], replicated
- grad_w_query: float32 [2048, 2048], P('shard')
- grad_w_key: float32 [2048, 2048], P('shard')
- grad_w_value: float32 [2048, 2048], P('shard')
- grad_w_output: float32 [2048, 2048], P('shard')
- grad_query_gain: float32 [128], replicated
- grad_key_gain: float32 [128], replicated
- grad_ffn_norm_gain: float32 [2048], replicated
- grad_w_router: float32 [2048, 4], replicated
- grad_w_gate: float32 [4, 2048, 1024], P(None, 'shard')
- grad_w_up: float32 [4, 2048, 1024], P(None, 'shard')
- grad_w_down: float32 [4, 1024, 2048], P(None, 'shard')
- residual_rms: float32 [3], replicated
Inputs may be any that keep to these rules, and one draw needn't show every extreme that they name: Row scales differ along the tokens. `segment_ids`: in each sequence of 256 tokens the ids are 1, 2, 3, 4 in order, each document one token or more, followed by 1 to 32 padding tokens of id 0. `expert_ids`: A token's 2 experts differ. In each sequence of 256 tokens no expert is chosen by more than 192 tokens, and in some sequence one expert is chosen by exactly 192.
All inputs are finite; a program needn't handle non-finite values.
Results may differ from a plain program's by a relative error of at most 0.02.
Values may be sent and summed in bfloat16 or wider, within the bound.
No kernel may reach another device: no remote copies, remote signals or barrier semaphores. Data moves between devices by JAX's collectives and lax.ppermute only.
A program may use at most 448 MiB of HBM per device.

v0:
```python
import jax
import jax.numpy as jnp
from jax import lax
from jax.sharding import PartitionSpec as P

CAP = 192


epsilon = 1e-06
theta = 10000.0
masked_score = -1e30


def rms_scale(field):
    return lax.rsqrt(jnp.mean(field * field, axis=-1, keepdims=True) + epsilon)


def norm_back(field, scale_part, gain_vec, upstream):
    weighted = upstream * gain_vec
    inner_sum = jnp.sum(weighted * field, axis=-1, keepdims=True)
    return scale_part * weighted - field * scale_part**3 * inner_sum / field.shape[-1]


def rotary_tables(length, dim_size):
    half_size = dim_size // 2
    frequency = theta ** (-2.0 * jnp.arange(half_size, dtype=jnp.float32) / dim_size)
    angles = jnp.arange(length, dtype=jnp.float32)[:, None] * frequency[None, :]
    return (jnp.cos(angles)[:, None, :], jnp.sin(angles)[:, None, :])


def rotate(field, cosine, sine_table):
    half_size = field.shape[-1] // 2
    first_half = field[..., :half_size]
    second_half = field[..., half_size:]
    return jnp.concatenate(
        [
            first_half * cosine - second_half * sine_table,
            second_half * cosine + first_half * sine_table,
        ],
        axis=-1,
    )


def rotate_back(upstream, cosine, sine_table):
    half_size = upstream.shape[-1] // 2
    first_half = upstream[..., :half_size]
    second_half = upstream[..., half_size:]
    return jnp.concatenate(
        [
            first_half * cosine + second_half * sine_table,
            second_half * cosine - first_half * sine_table,
        ],
        axis=-1,
    )


def score_block(query_rot, key_rot, same_document, score_scale):
    raw_scores = (
        jnp.einsum("qhd,khd->hqk", query_rot, key_rot, preferred_element_type=jnp.float32)
        * score_scale
    )
    return jnp.where(same_document, raw_scores, masked_score)


def contract_rows(left_side, right_side):
    return lax.dot_general(
        left_side, right_side, (((0,), (0,)), ((), ())), preferred_element_type=jnp.float32
    )


def body(
    tokens,
    cotangent,
    segment_ids,
    expert_ids,
    norm_gain,
    w_query,
    w_key,
    w_value,
    w_output,
    query_gain,
    key_gain,
    ffn_norm_gain,
    w_router,
    w_gate,
    w_up,
    w_down,
):
    length, model_width = tokens.shape
    head_size = query_gain.shape[0]
    head_count = model_width // head_size
    expert_count = w_gate.shape[0]
    route_count = expert_ids.shape[1]
    capacity = CAP
    score_scale = head_size ** (-0.5)
    stream = tokens.astype(jnp.float32)
    live_rows = (segment_ids > 0).astype(jnp.float32)[:, None]
    full_query, full_key, full_value, full_output = (
        lax.all_gather(w_query, "shard", axis=0, tiled=True),
        lax.all_gather(w_key, "shard", axis=0, tiled=True),
        lax.all_gather(w_value, "shard", axis=0, tiled=True),
        lax.all_gather(w_output, "shard", axis=0, tiled=True),
    )
    first_scale = rms_scale(stream)
    normed = (stream * first_scale * norm_gain).astype(jnp.bfloat16)
    query_raw = jnp.dot(normed, full_query, preferred_element_type=jnp.float32).reshape(
        length, head_count, head_size
    )
    key_raw = jnp.dot(normed, full_key, preferred_element_type=jnp.float32).reshape(
        length, head_count, head_size
    )
    value_heads = (
        jnp.dot(normed, full_value, preferred_element_type=jnp.float32)
        .astype(jnp.bfloat16)
        .reshape(length, head_count, head_size)
    )
    cosine, sine_table = rotary_tables(length, head_size)
    query_scale = rms_scale(query_raw)
    key_scale = rms_scale(key_raw)
    query_rot = rotate(query_raw * query_scale * query_gain, cosine, sine_table).astype(
        jnp.bfloat16
    )
    key_rot = rotate(key_raw * key_scale * key_gain, cosine, sine_table).astype(jnp.bfloat16)
    same_document = (segment_ids[:, None] == segment_ids[None, :])[None]
    scores = score_block(query_rot, key_rot, same_document, score_scale)
    top_score = jnp.max(scores, axis=-1, keepdims=True)
    exponent = jnp.exp(scores - top_score)
    denominator = jnp.sum(exponent, axis=-1, keepdims=True)
    log_total = top_score + jnp.log(denominator)
    weights_soft = (exponent / denominator).astype(jnp.bfloat16)
    mixed_heads = (
        jnp.einsum("hqk,khd->qhd", weights_soft, value_heads, preferred_element_type=jnp.float32)
        .reshape(length, model_width)
        .astype(jnp.bfloat16)
    )
    attention_out = jnp.dot(mixed_heads, full_output, preferred_element_type=jnp.float32)
    hidden = stream + live_rows * attention_out
    second_scale = rms_scale(hidden)
    normed_ffn = (hidden * second_scale * ffn_norm_gain).astype(jnp.bfloat16)
    logits = jnp.dot(normed_ffn, w_router, preferred_element_type=jnp.float32)
    shifted = logits - jnp.max(logits, axis=-1, keepdims=True)
    chances = jnp.exp(shifted) / jnp.sum(jnp.exp(shifted), axis=-1, keepdims=True)
    chosen = expert_ids[:, :, None] == jnp.arange(expert_count)[None, None, :]
    gate_values = jnp.sum(jnp.where(chosen, chances[:, None, :], 0.0), axis=-1)
    flat_pick = chosen.reshape(length * route_count, expert_count).astype(jnp.int32)
    earlier = jnp.cumsum(flat_pick, axis=0) - flat_pick
    position = jnp.sum(earlier * flat_pick, axis=1)
    target = expert_ids.reshape(length * route_count) * capacity + position
    pair_token = jnp.arange(length * route_count, dtype=jnp.int32) // route_count
    slot_token = jnp.zeros((expert_count * capacity,), jnp.int32).at[target].set(pair_token)
    slot_used = jnp.zeros((expert_count * capacity,), jnp.bfloat16).at[target].set(1.0)
    dispatched = (normed_ffn[slot_token] * slot_used[:, None]).reshape(
        expert_count, capacity, model_width
    )
    full_gate, full_up, full_down = (
        lax.all_gather(w_gate, "shard", axis=1, tiled=True),
        lax.all_gather(w_up, "shard", axis=1, tiled=True),
        lax.all_gather(w_down, "shard", axis=1, tiled=True),
    )
    gate_pre = jnp.einsum("ecd,edh->ech", dispatched, full_gate, preferred_element_type=jnp.float32)
    up_pre = jnp.einsum("ecd,edh->ech", dispatched, full_up, preferred_element_type=jnp.float32)
    sigmoid_gate = jax.nn.sigmoid(gate_pre)
    silu_gate = gate_pre * sigmoid_gate
    inner_act = (silu_gate * up_pre).astype(jnp.bfloat16)
    expert_out = jnp.einsum(
        "ech,ehd->ecd", inner_act, full_down, preferred_element_type=jnp.float32
    ).reshape(expert_count * capacity, model_width)
    picked_out = expert_out[target].reshape(length, route_count, model_width)
    moe_out = jnp.sum(gate_values[:, :, None] * picked_out, axis=1)
    result = hidden + live_rows * moe_out
    full_gate, full_up, full_down = (
        lax.all_gather(w_gate, "shard", axis=1, tiled=True),
        lax.all_gather(w_up, "shard", axis=1, tiled=True),
        lax.all_gather(w_down, "shard", axis=1, tiled=True),
    )
    full_query, full_key, full_value, full_output = (
        lax.all_gather(w_query, "shard", axis=0, tiled=True),
        lax.all_gather(w_key, "shard", axis=0, tiled=True),
        lax.all_gather(w_value, "shard", axis=0, tiled=True),
        lax.all_gather(w_output, "shard", axis=0, tiled=True),
    )
    grad_result = cotangent.astype(jnp.float32)
    grad_moe = live_rows * grad_result
    grad_gates = jnp.sum(grad_moe[:, None, :] * picked_out, axis=-1)
    slot_grad = (gate_values[:, :, None] * grad_moe[:, None, :]).reshape(
        length * route_count, model_width
    )
    grad_expert = (
        jnp.zeros((expert_count * capacity, model_width), jnp.float32).at[target].set(slot_grad)
    )
    grad_expert = grad_expert.astype(jnp.bfloat16).reshape(expert_count, capacity, model_width)
    grad_inner = jnp.einsum(
        "ecd,ehd->ech", grad_expert, full_down, preferred_element_type=jnp.float32
    )
    grad_gate_pre = (
        grad_inner * up_pre * sigmoid_gate * (1.0 + gate_pre * (1.0 - sigmoid_gate))
    ).astype(jnp.bfloat16)
    grad_up_pre = (grad_inner * silu_gate).astype(jnp.bfloat16)
    grad_dispatched = jnp.einsum(
        "ech,edh->ecd", grad_gate_pre, full_gate, preferred_element_type=jnp.float32
    )
    grad_dispatched = grad_dispatched + jnp.einsum(
        "ech,edh->ecd", grad_up_pre, full_up, preferred_element_type=jnp.float32
    )
    grad_from_experts = jnp.sum(
        grad_dispatched.reshape(expert_count * capacity, model_width)[target].reshape(
            length, route_count, model_width
        ),
        axis=1,
    )
    grad_chances = jnp.sum(jnp.where(chosen, grad_gates[:, :, None], 0.0), axis=1)
    grad_logits = (
        chances * (grad_chances - jnp.sum(chances * grad_chances, axis=-1, keepdims=True))
    ).astype(jnp.bfloat16)
    grad_router_local = contract_rows(normed_ffn, grad_logits)
    grad_normed_ffn = grad_from_experts + jnp.einsum(
        "te,de->td", grad_logits, w_router, preferred_element_type=jnp.float32
    )
    grad_ffn_local = jnp.sum(grad_normed_ffn * hidden * second_scale, axis=0)
    grad_hidden = grad_result + norm_back(hidden, second_scale, ffn_norm_gain, grad_normed_ffn)
    grad_attention = (live_rows * grad_hidden).astype(jnp.bfloat16)
    grad_mixed = jnp.einsum(
        "td,ed->te", grad_attention, full_output, preferred_element_type=jnp.float32
    )
    grad_mixed = grad_mixed.astype(jnp.bfloat16).reshape(length, head_count, head_size)
    scores_again = score_block(query_rot, key_rot, same_document, score_scale)
    probs_full = jnp.exp(scores_again - log_total)
    grad_values = jnp.einsum(
        "hqk,qhd->khd",
        probs_full.astype(jnp.bfloat16),
        grad_mixed,
        preferred_element_type=jnp.float32,
    ).astype(jnp.bfloat16)
    grad_probs = jnp.einsum(
        "qhd,khd->hqk", grad_mixed, value_heads, preferred_element_type=jnp.float32
    )
    row_dot = jnp.sum(probs_full * grad_probs, axis=-1, keepdims=True)
    grad_scores = (probs_full * (grad_probs - row_dot)).astype(jnp.bfloat16)
    grad_query_rot = (
        jnp.einsum("hqk,khd->qhd", grad_scores, key_rot, preferred_element_type=jnp.float32)
        * score_scale
    )
    grad_key_rot = (
        jnp.einsum("hqk,qhd->khd", grad_scores, query_rot, preferred_element_type=jnp.float32)
        * score_scale
    )
    grad_query_normed = rotate_back(grad_query_rot, cosine, sine_table)
    grad_key_normed = rotate_back(grad_key_rot, cosine, sine_table)
    grad_qgain_local = jnp.sum(grad_query_normed * query_raw * query_scale, axis=(0, 1))
    grad_kgain_local = jnp.sum(grad_key_normed * key_raw * key_scale, axis=(0, 1))
    grad_query_raw = (
        norm_back(query_raw, query_scale, query_gain, grad_query_normed)
        .reshape(length, model_width)
        .astype(jnp.bfloat16)
    )
    grad_key_raw = (
        norm_back(key_raw, key_scale, key_gain, grad_key_normed)
        .reshape(length, model_width)
        .astype(jnp.bfloat16)
    )
    grad_value_raw = grad_values.reshape(length, model_width)
    grad_normed = jnp.einsum(
        "te,de->td", grad_query_raw, full_query, preferred_element_type=jnp.float32
    )
    grad_normed = grad_normed + jnp.einsum(
        "te,de->td", grad_key_raw, full_key, preferred_element_type=jnp.float32
    )
    grad_normed = grad_normed + jnp.einsum(
        "te,de->td", grad_value_raw, full_value, preferred_element_type=jnp.float32
    )
    grad_norm_local = jnp.sum(grad_normed * stream * first_scale, axis=0)
    input_grad = (grad_hidden + norm_back(stream, first_scale, norm_gain, grad_normed)).astype(
        jnp.bfloat16
    )
    grad_down_local = jnp.einsum(
        "ech,ecd->ehd", inner_act, grad_expert, preferred_element_type=jnp.float32
    )
    grad_gate_local = jnp.einsum(
        "ecd,ech->edh", dispatched, grad_gate_pre, preferred_element_type=jnp.float32
    )
    grad_up_local = jnp.einsum(
        "ecd,ech->edh", dispatched, grad_up_pre, preferred_element_type=jnp.float32
    )
    attn_part = lax.psum_scatter(
        jnp.concatenate(
            [
                contract_rows(normed, grad_query_raw),
                contract_rows(normed, grad_key_raw),
                contract_rows(normed, grad_value_raw),
                contract_rows(mixed_heads, grad_attention),
            ],
            axis=1,
        ).astype(jnp.bfloat16),
        "shard",
        scatter_dimension=0,
        tiled=True,
    )
    gate_part, up_part, down_part = (
        lax.psum_scatter(
            grad_gate_local.astype(jnp.bfloat16), "shard", scatter_dimension=1, tiled=True
        ).astype(jnp.float32),
        lax.psum_scatter(
            grad_up_local.astype(jnp.bfloat16), "shard", scatter_dimension=1, tiled=True
        ).astype(jnp.float32),
        lax.psum_scatter(
            grad_down_local.astype(jnp.bfloat16), "shard", scatter_dimension=1, tiled=True
        ).astype(jnp.float32),
    )
    attn_sum, gate_sum, up_sum, down_sum = (
        lax.psum(attn_part, "rep").astype(jnp.float32),
        lax.psum(gate_part.astype(jnp.bfloat16), "rep").astype(jnp.float32),
        lax.psum(up_part.astype(jnp.bfloat16), "rep").astype(jnp.float32),
        lax.psum(down_part.astype(jnp.bfloat16), "rep").astype(jnp.float32),
    )
    square_sums = jnp.stack(
        [
            jnp.sum(live_rows * stream * stream),
            jnp.sum(live_rows * hidden * hidden),
            jnp.sum(live_rows * result * result),
            jnp.sum(live_rows),
        ]
    )
    norm_sum, qgain_sum, kgain_sum, ffn_sum, router_sum, stat_sum = lax.psum(
        (
            grad_norm_local,
            grad_qgain_local,
            grad_kgain_local,
            grad_ffn_local,
            grad_router_local,
            square_sums,
        ),
        ("rep", "shard"),
    )
    residual_rms = jnp.sqrt(stat_sum[:3] / (stat_sum[3] * model_width))
    output = result.astype(jnp.bfloat16)
    return (
        output,
        input_grad,
        norm_sum,
        attn_sum[:, :model_width],
        attn_sum[:, model_width : 2 * model_width],
        attn_sum[:, 2 * model_width : 3 * model_width],
        attn_sum[:, 3 * model_width :],
        qgain_sum,
        kgain_sum,
        ffn_sum,
        router_sum,
        gate_sum,
        up_sum,
        down_sum,
        residual_rms,
    )


def solution(mesh):
    in_specs = (
        P(("rep", "shard"), None),
        P(("rep", "shard"), None),
        P(("rep", "shard")),
        P(("rep", "shard"), None),
        P(),
        P("shard", None),
        P("shard", None),
        P("shard", None),
        P("shard", None),
        P(),
        P(),
        P(),
        P(),
        P(None, "shard", None),
        P(None, "shard", None),
        P(None, "shard", None),
    )
    out_specs = (
        P(("rep", "shard"), None),
        P(("rep", "shard"), None),
        P(),
        P("shard", None),
        P("shard", None),
        P("shard", None),
        P("shard", None),
        P(),
        P(),
        P(),
        P(),
        P(None, "shard", None),
        P(None, "shard", None),
        P(None, "shard", None),
        P(),
    )
    return jax.shard_map(body, mesh=mesh, in_specs=in_specs, out_specs=out_specs, check_vma=False)
```

profile of v0, /device:TPU:0, one launch (start us, length us, event | category | flops | bytes accessed | tf_op | source)
XLA Modules:
  0.0 3222.4 jit_solution(2654529935397855025)
XLA Ops:
  20.3 6.4 mul.743
  35.6 126.4 %all-gather.12.cloned.1.call-done = bf16[2048,2048]{1,0:T(8,128)(2,1)} async-done(((bf16[512,2048]{1,0:T(8,128)(2,1)}), bf16[2048,2048]{1,0:T(8,128)(2,1)}) %all-gather.12.cloned.1.call-update) | async-done | bytes 8388624 | tf_op jit(solution)/shard_map/all_gather | solution.py:100
  169.7 141.7 %all-gather.10.cloned.1.call-done = bf16[2048,2048]{1,0:T(8,128)(2,1)} async-done(((bf16[512,2048]{1,0:T(8,128)(2,1)}), bf16[2048,2048]{1,0:T(8,128)(2,1)}) %all-gather.10.cloned.1.call-update) | async-done | bytes 8388624 | tf_op jit(solution)/shard_map/all_gather | solution.py:99
  330.9 130.0 %all-gather.8.cloned.1.call-done = bf16[2048,2048]{1,0:T(8,128)(2,1)} async-done(((bf16[512,2048]{1,0:T(8,128)(2,1)}), bf16[2048,2048]{1,0:T(8,128)(2,1)}) %all-gather.8.cloned.1.call-update) | async-done | bytes 8388624 | tf_op jit(solution)/shard_map/all_gather | solution.py:101
  469.8 140.4 %all-gather.14.cloned.1.call-done = bf16[2048,2048]{1,0:T(8,128)(2,1)} async-done(((bf16[512,2048]{1,0:T(8,128)(2,1)}), bf16[2048,2048]{1,0:T(8,128)(2,1)}) %all-gather.14.cloned.1.call-update) | async-done | bytes 8388624 | tf_op jit(solution)/shard_map/all_gather | solution.py:102
  618.7 9.1 scatter_custom_fusion.2
  637.4 259.2 %all-gather.18.cloned.1.call-done = bf16[4,2048,1024]{2,1,0:T(8,128)(2,1)} async-done(((bf16[4,512,1024]{2,1,0:T(8,128)(2,1)}), bf16[4,2048,1024]{2,1,0:T(8,128)(2,1)}) %all-gather.18.cloned.1.call-update) | async-done | bytes 16777232 | tf_op jit(solution)/shard_map/all_gather | solution.py:157
  896.7 12.2 fusion.39
  908.9 274.2 %all-gather.16.cloned.1.call-done = bf16[4,2048,1024]{2,1,0:T(8,128)(2,1)} async-done(((bf16[4,512,1024]{2,1,0:T(8,128)(2,1)}), bf16[4,2048,1024]{2,1,0:T(8,128)(2,1)}) %all-gather.16.cloned.1.call-update) | async-done | bytes 16777232 | tf_op jit(solution)/shard_map/all_gather | solution.py:156
  1183.1 12.2 fusion.41
  1195.3 274.4 %all-gather.20.cloned.1.call-done = bf16[4,1024,2048]{2,1,0:T(8,128)(2,1)} async-done(((bf16[4,256,2048]{2,1,0:T(8,128)(2,1)}), bf16[4,1024,2048]{2,1,0:T(8,128)(2,1)}) %all-gather.20.cloned.1.call-update) | async-done | bytes 16777232 | tf_op jit(solution)/shard_map/all_gather | solution.py:158
  1469.7 13.6 multiply_convert_fusion.1
  1483.3 12.7 convolution_convert_fusion
  1496.1 10.2 convolution_convert_fusion.2
  1506.3 10.3 convolution_convert_fusion.1
  1520.8 12.4 fusion.90
  1533.2 8.4 gather_fusion.1
  1547.4 10.9 multiply_reduce_fusion.1
  1558.4 14.9 fusion.91
  1573.2 12.7 convolution_add_fusion
  1585.9 8.4 gather_fusion.2
  1600.3 8.5 reduce_sum.260
  1682.2 24.2 pad_maximum_fusion
  1706.4 68.2 %reduce-scatter.11.cloned.1.call-done = bf16[4,256,2048]{2,1,0:T(8,128)(2,1)} async-done(((bf16[4,1024,2048]{2,1,0:T(8,128)(2,1)}), bf16[4,256,2048]{2,1,0:T(8,128)(2,1)}) %reduce-scatter.11.cloned.1.call-update) | async-done | bytes 4194320 | tf_op jit(solution)/shard_map/reduce_scatter | solution.py:305
  1774.6 283.6 %reduce-scatter.7.cloned.1.call-done = bf16[4,512,1024]{2,1,0:T(8,128)(2,1)} async-done(((bf16[4,2048,1024]{2,1,0:T(8,128)(2,1)}), bf16[4,512,1024]{2,1,0:T(8,128)(2,1)}) %reduce-scatter.7.cloned.1.call-update) | async-done | bytes 4194320 | tf_op jit(solution)/shard_map/reduce_scatter | solution.py:299
  2058.2 283.2 %reduce-scatter.9.cloned.1.call-done = bf16[4,512,1024]{2,1,0:T(8,128)(2,1)} async-done(((bf16[4,2048,1024]{2,1,0:T(8,128)(2,1)}), bf16[4,512,1024]{2,1,0:T(8,128)(2,1)}) %reduce-scatter.9.cloned.1.call-update) | async-done | bytes 4194320 | tf_op jit(solution)/shard_map/reduce_scatter | solution.py:302
  2341.5 555.3 %reduce-scatter.5.cloned.1.call-done = bf16[512,8192]{0,1:T(8,128)(2,1)} async-done(((bf16[2048,8192]{0,1:T(8,128)(2,1)}), bf16[512,8192]{0,1:T(8,128)(2,1)}) %reduce-scatter.5.cloned.1.call-update) | async-done | bytes 8388624 | tf_op jit(solution)/shard_map/reduce_scatter | solution.py:284
  2904.3 6.7 convolution_add_fusion.3
  2919.1 43.9 %all-reduce = (f32[2048]{0:T(1024)}, f32[128]{0:T(128)}, f32[128]{0:T(128)}, f32[2048]{0:T(1024)}, f32[2048,4]{0,1:T(4,128)}, /*index=5*/f32[4]{0:T(128)S(1)}) all-reduce(f32[2048]{0:T(1024)S(1)} %get-tuple-element.109, f32[128]{0:T(128)S(1)} %bitcast_reduce_fusion.1, ...), channel_id=1, replica_groups=mesh['rep'=8,'shard'=4] {'rep','shard'}, use_global_device_ids=true, to_apply=%region_26.27 | all-reduce | flops 12548 | bytes 100384 | tf_op jit(solution)/shard_map/psum | solution.py:323
  2968.0 199.6 %all-reduce.4.cloned.1.call-done = (bf16[512,8192]{0,1:T(8,128)(2,1)}, bf16[4,512,1024]{2,1,0:T(8,128)(2,1)}, bf16[4,512,1024]{2,1,0:T(8,128)(2,1)}, bf16[4,256,2048]{2,1,0:T(8,128)(2,1)}) async-done(((bf16[512,8192]{0,1:T(8,128)(2,1)}, bf16[4,512,1024]{2,1,0:T(8,128)(2,1)}, bf16[4,512,1024]{2,1,0:T(8,128)(2,1)}, bf16[4,256,2048]{2,1,0:T(8,128)(2,1)}), (bf16[512,8192]{0,1:T(8,128)(2,1)}, ...) | async-done | bytes 20971536 | tf_op jit(solution)/shard_map/psum | solution.py:310
  3167.6 10.4 fusion.87
  3199.4 6.8 convert_element_type.141
  (335 shorter events, 214.7 us)
Async XLA Ops:
  7.2 610.2 %copy-start = (bf16[2048,4]{0,1:T(4,128)(2,1)S(1)}, bf16[2048,4]{0,1:T(4,128)(2,1)}, u32[]{:S(2)}) copy-start(bf16[2048,4]{0,1:T(4,128)(2,1)} %param.28) | copy-start | bytes 49156
  7.2 154.8 %all-gather.12.cloned.1.call-start = ((), (), s32[]{:S(2)}) async-start(), calls=%async_computation.6 | async-start | bytes 10485760 | tf_op jit(solution)/shard_map/all_gather | solution.py:100
  7.9 303.5 %all-gather.10.cloned.1.call-start = ((), (), s32[]{:S(2)}) async-start(), calls=%async_computation.5 | async-start | bytes 10485760 | tf_op jit(solution)/shard_map/all_gather | solution.py:99
  8.7 452.2 %all-gather.8.cloned.1.call-start = ((), (), s32[]{:S(2)}) async-start(), calls=%async_computation.4 | async-start | bytes 10485760 | tf_op jit(solution)/shard_map/all_gather | solution.py:101
  9.4 600.8 %all-gather.14.cloned.1.call-start = ((), (), s32[]{:S(2)}) async-start(), calls=%async_computation.7 | async-start | bytes 10485760 | tf_op jit(solution)/shard_map/all_gather | solution.py:102
  10.0 886.7 %all-gather.18.cloned.1.call-start = ((), (), s32[]{:S(2)}) async-start(), calls=%async_computation.9 | async-start | bytes 20971520 | tf_op jit(solution)/shard_map/all_gather | solution.py:157
  10.6 1172.5 %all-gather.16.cloned.1.call-start = ((), (), s32[]{:S(2)}) async-start(), calls=%async_computation.8 | async-start | bytes 20971520 | tf_op jit(solution)/shard_map/all_gather | solution.py:156
  11.2 1458.5 %all-gather.20.cloned.1.call-start = ((), (), s32[]{:S(2)}) async-start(), calls=%async_computation.10 | async-start | bytes 20971520 | tf_op jit(solution)/shard_map/all_gather | solution.py:158
  11.9 1762.7 %reduce-scatter.11.cloned.1.call-start = ((), (), s32[]{:S(2)}) async-start(), calls=%async_computation.14 | async-start | bytes 20971520 | tf_op jit(solution)/shard_map/reduce_scatter | solution.py:305
  20.3 13.7 copy-start.7
  20.3 141.6 %copy-start.44 = (f32[2048]{0:T(1024)S(1)}, f32[2048]{0:T(1024)}, u32[]{:S(2)}) copy-start(f32[2048]{0:T(1024)} %param.20) | copy-start | bytes 24580
  34.9 426.0 %copy-start.63 = (f32[256]{0:T(256)}, f32[256]{0:T(256)S(1)}, u32[]{:S(2)}) copy-start(f32[256]{0:T(256)S(1)} %get-tuple-element.159) | copy-start | bytes 3076
  35.6 289.3 %copy-start.38 = (f32[256,64]{1,0:T(8,128)}, f32[256,64]{1,0:T(8,128)S(1)}, u32[]{:S(2)}) copy-start(f32[256,64]{1,0:T(8,128)S(1)} %get-tuple-element.162) | copy-start | bytes 196612
  35.6 289.3 %copy-start.40 = (f32[256,64]{1,0:T(8,128)}, f32[256,64]{1,0:T(8,128)S(1)}, u32[]{:S(2)}) copy-start(f32[256,64]{1,0:T(8,128)S(1)} %get-tuple-element.163) | copy-start | bytes 196612
  328.3 138.5 %copy-start.51 = (f32[16,256]{1,0:T(8,128)}, f32[16,256]{1,0:T(8,128)S(1)}, u32[]{:S(2)}) copy-start(f32[16,256]{1,0:T(8,128)S(1)} %get-tuple-element.164) | copy-start | bytes 49156
  330.9 136.0 %copy-start.58 = (f32[16,256]{1,0:T(8,128)}, f32[16,256]{1,0:T(8,128)S(1)}, u32[]{:S(2)}) copy-start(f32[16,256]{1,0:T(8,128)S(1)} %fusion.2) | copy-start | bytes 49156
  467.9 142.4 %copy-start.80 = (f32[256]{0:T(256)S(1)}, f32[256]{0:T(256)}, u32[]{:S(2)}) copy-start(f32[256]{0:T(256)} %copy-done.79) | copy-start | bytes 3076
  617.3 15.9 copy-start.2
  1496.0 562.2 %reduce-scatter.7.cloned.1.call-start = ((), (), s32[]{:S(2)}) async-start(), calls=%async_computation.12 | async-start | bytes 20971520 | tf_op jit(solution)/shard_map/reduce_scatter | solution.py:299
  1506.3 835.2 %reduce-scatter.9.cloned.1.call-start = ((), (), s32[]{:S(2)}) async-start(), calls=%async_computation.13 | async-start | bytes 20971520 | tf_op jit(solution)/shard_map/reduce_scatter | solution.py:302
  1516.7 1380.1 %reduce-scatter.5.cloned.1.call-start = ((), (), s32[]{:S(2)}) async-start(), calls=%async_computation.11 | async-start | bytes 41943040 | tf_op jit(solution)/shard_map/reduce_scatter | solution.py:284
  1600.2 8.6 copy-start.71
  1600.2 8.6 copy-start.54
  1600.2 8.6 copy-start.67
  1600.2 8.6 copy-start.77
  1600.2 8.7 copy-start.57
  1600.2 8.7 copy-start.81
  1600.3 8.7 copy-start.84
  1706.4 1461.2 %all-reduce.4.cloned.1.call-start = ((), (), s32[]{:S(2)}) async-start(), calls=%async_computation.15 | async-start | bytes 41943040 | tf_op jit(solution)/shard_map/psum | solution.py:310
  2898.1 12.9 slice-start
  2911.1 8.0 copy-start.72
  2911.1 53.7 %copy-start.96 = (f32[256]{0:T(256)S(1)}, f32[256]{0:T(256)}, u32[]{:S(2)}) copy-start(f32[256]{0:T(256)} %get-tuple-element.158) | copy-start | bytes 3076
  (80 other events, 293.0 us)
Sparse Core Ops, SparseCore 0:
  9.6 152.3 all-gather.11
  163.5 147.8 all-gather.9
  313.0 147.8 all-gather.7
  462.3 147.8 all-gather.13
  611.6 285.0 all-gather.17
  898.1 284.9 all-gather.15
  1184.7 284.9 all-gather.19
  1496.1 278.4 reduce-scatter.10
  1777.1 281.0 reduce-scatter.6
  2060.4 280.9 reduce-scatter.8
  2343.9 552.7 reduce-scatter.4
  2900.9 266.6 all-reduce.3
where the time goes:
time: 3230 us; the launch traced here: 3220 us
  waiting for transfers between devices  2740 us (85%)
  matrix products  201 us (6%)
  other arithmetic  113 us (3%)
  local copies, waits for them, and re-layouts  107 us (3%)
  blocking collectives  43.9 us (1%)
    reduce_scatter x1, waiting for transfers between devices, body(): lax.psum_scatter(jnp.concatenate([contract_rows(normed, grad_query_raw),...  555 us
    reduce_scatter x1, waiting for transfers between devices, body(): lax.psum_scatter(grad_gate_local.astype(jnp.bfloat16), 'shard', scatter_d...  284 us
    reduce_scatter x1, waiting for transfers between devices, body(): lax.psum_scatter(grad_up_local.astype(jnp.bfloat16), 'shard', scatter_dim...  283 us
    all_gather x1, waiting for transfers between devices, body(): lax.all_gather(w_down, 'shard', axis=1, tiled=True)  274 us
    all_gather x1, waiting for transfers between devices, body(): lax.all_gather(w_gate, 'shard', axis=1, tiled=True)  274 us
    all_gather x1, waiting for transfers between devices, body(): lax.all_gather(w_up, 'shard', axis=1, tiled=True)  259 us
    psum x1, waiting for transfers between devices, body(): lax.psum(attn_part, 'rep').astype(jnp.float32)  200 us
    all_gather x1, waiting for transfers between devices, body(): lax.all_gather(w_query, 'shard', axis=0, tiled=True)  142 us
  transfers between devices with their start and end apart: 12, of which 12 were waited for; matrix products, arithmetic and copies ran while one was open for 10% of the time, Pallas kernels for 0%

commit v1 on v0

v1 whole, which is shorter than its diff:
```python
import jax
import jax.numpy as jnp
from jax import lax
from jax.sharding import PartitionSpec as P

EPS = 1e-06
THETA = 10000.0
MASKED = -1e30
F32 = jnp.float32
BF16 = jnp.bfloat16


def rms_scale(field):
    return lax.rsqrt(jnp.mean(field * field, axis=-1, keepdims=True) + EPS)


def norm_back(field, scale, gain, upstream):
    weighted = upstream * gain
    inner = jnp.sum(weighted * field, axis=-1, keepdims=True)
    return scale * weighted - field * scale**3 * inner / field.shape[-1]


def rotary_tables(length, dim):
    half = dim // 2
    frequency = THETA ** (-2.0 * jnp.arange(half, dtype=F32) / dim)
    angles = jnp.arange(length, dtype=F32)[:, None] * frequency[None, :]
    return jnp.cos(angles), jnp.sin(angles)


def rotate(field, cosine, sine):
    half = field.shape[-1] // 2
    first, second = field[..., :half], field[..., half:]
    return jnp.concatenate(
        [first * cosine - second * sine, second * cosine + first * sine], axis=-1
    )


def dot(left, right):
    return jnp.dot(left, right, preferred_element_type=F32)


def dot_nt(left, right):
    return lax.dot_general(left, right, (((1,), (1,)), ((), ())), preferred_element_type=F32)


def dot_tn(left, right):
    return lax.dot_general(left, right, (((0,), (0,)), ((), ())), preferred_element_type=F32)


def gather(piece, axis, dim=0):
    return lax.all_gather(piece, axis, axis=dim, tiled=True)


def scatter_sum(whole, axis):
    return lax.psum_scatter(whole, axis, scatter_dimension=0, tiled=True)


def make_body(reps, shards):
    def body(
        tokens, cotangent, segment_ids, expert_ids, norm_gain, w_query, w_key, w_value, w_output,
        query_gain, key_gain, ffn_norm_gain, w_router, w_gate, w_up, w_down,
    ):
        length, width = tokens.shape
        head_size = query_gain.shape[0]
        head_count = width // head_size
        experts = w_gate.shape[0]
        hidden_total = w_gate.shape[2]
        heads = head_count // reps
        cols = heads * head_size
        parts = reps // experts
        sub = hidden_total // shards // parts
        hid = sub * shards
        rows = width // shards
        total = reps * length
        per_plane = reps // shards
        out_rows = cols // shards
        score_scale = head_size ** (-0.5)

        rep = lax.axis_index("rep")
        expert, part = rep // parts, rep % parts

        def columns(weight):
            return lax.dynamic_slice(weight, (0, rep * cols), (rows, cols))

        def hidden_columns(weight):
            own = lax.dynamic_slice(weight, (expert, 0, 0), (1, rows, hidden_total))
            own = own.reshape(rows, shards, parts, sub)
            return lax.dynamic_slice(own, (0, 0, part, 0), (rows, shards, 1, sub)).reshape(rows, hid)

        w_qkv = gather(jnp.concatenate([columns(w_query), columns(w_key), columns(w_value)], 1), "shard")
        there = [
            (src_rep * shards + src, (src * per_plane + src_rep % per_plane) * shards + src_rep // per_plane)
            for src_rep in range(reps)
            for src in range(shards)
        ]
        back = [(target, source) for source, target in there]
        first_row = (rep % per_plane) * cols + (rep // per_plane) * out_rows
        out_piece = lax.dynamic_slice(w_output, (first_row, 0), (out_rows, width))
        w_out = gather(lax.ppermute(out_piece, ("rep", "shard"), there), "shard")
        w_gu = gather(jnp.concatenate([hidden_columns(w_gate), hidden_columns(w_up)], 1), "shard")
        own_down = lax.dynamic_slice(w_down, (expert, part * sub, 0), (1, sub, width))
        w_dn = gather(own_down.reshape(sub, width), "shard")

        stream = tokens.astype(F32)
        live = (segment_ids > 0).astype(F32)[:, None]
        first_scale = rms_scale(stream)
        normed = (stream * first_scale * norm_gain).astype(BF16)
        grad_moe_own = jnp.where(segment_ids[:, None] > 0, cotangent, jnp.zeros_like(cotangent))

        normed_all = gather(normed, "rep")
        segments = gather(segment_ids, "rep").reshape(reps, length)
        routes = gather(expert_ids, "rep")
        grad_moe = gather(grad_moe_own, "rep")

        qkv = dot(normed_all, w_qkv)
        by_head = (reps, length, heads, head_size)
        query_raw = qkv[:, :cols].reshape(by_head)
        key_raw = qkv[:, cols : 2 * cols].reshape(by_head)
        value = qkv[:, 2 * cols :].astype(BF16).reshape(by_head)
        cosine, sine = rotary_tables(length, head_size)
        cosine, sine = cosine[:, None, :], sine[:, None, :]
        query_scale, key_scale = rms_scale(query_raw), rms_scale(key_raw)
        query = rotate(query_raw * query_scale * query_gain, cosine, sine).astype(BF16)
        key = rotate(key_raw * key_scale * key_gain, cosine, sine).astype(BF16)
        same = (segments[:, :, None] == segments[:, None, :])[:, None]
        scores = jnp.einsum("sqhd,skhd->shqk", query, key, preferred_element_type=F32) * score_scale
        scores = jnp.where(same, scores, MASKED)
        exponent = jnp.exp(scores - jnp.max(scores, axis=-1, keepdims=True))
        soft = exponent / jnp.sum(exponent, axis=-1, keepdims=True)
        soft_low = soft.astype(BF16)
        mixed = jnp.einsum("shqk,skhd->sqhd", soft_low, value, preferred_element_type=F32)
        mixed = mixed.astype(BF16).reshape(total, cols)
        attention_out = scatter_sum(dot(mixed, w_out).astype(BF16), "rep").astype(F32)

        hidden = stream + live * attention_out
        second_scale = rms_scale(hidden)
        normed_ffn = (hidden * second_scale * ffn_norm_gain).astype(BF16)
        ffn_all = gather(normed_ffn, "rep")

        def chances_of(field):
            logits = dot(field, w_router)
            shifted = jnp.exp(logits - jnp.max(logits, axis=-1, keepdims=True))
            return shifted / jnp.sum(shifted, axis=-1, keepdims=True)

        is_own = (jnp.arange(experts) == expert).astype(F32)
        chosen = jnp.any(routes == expert, axis=-1, keepdims=True).astype(F32)
        gate = jnp.sum(chances_of(ffn_all) * is_own, axis=-1, keepdims=True) * chosen
        gate_up = dot(ffn_all, w_gu)
        gate_pre, up_pre = gate_up[:, :hid], gate_up[:, hid:]
        sigmoid = jax.nn.sigmoid(gate_pre)
        silu = gate_pre * sigmoid
        inner = (silu * up_pre).astype(BF16)
        inner_gated = (gate * inner.astype(F32)).astype(BF16)
        grad_inner_raw = dot_nt(grad_moe, w_dn)
        grad_gate_part = jnp.sum(inner.astype(F32) * grad_inner_raw, axis=-1)
        grad_inner = gate * grad_inner_raw
        grad_gp = (grad_inner * up_pre * sigmoid * (1.0 + gate_pre * (1.0 - sigmoid))).astype(BF16)
        grad_up = (grad_inner * silu).astype(BF16)
        grad_gu = jnp.concatenate([grad_gp, grad_up], axis=1)
        moe_out = scatter_sum(dot(inner_gated, w_dn).astype(BF16), "rep").astype(F32)
        grad_ffn = scatter_sum(dot_nt(grad_gu, w_gu).astype(BF16), "rep").astype(F32)
        gate_parts = lax.all_gather(grad_gate_part.reshape(reps, length), "rep")
        gate_parts = lax.dynamic_index_in_dim(gate_parts, rep, 1, False)
        grad_chances = jnp.sum(gate_parts.reshape(experts, parts, length), axis=1).T
        picked = jnp.any(expert_ids[:, :, None] == jnp.arange(experts), axis=1)
        grad_chances = jnp.where(picked, grad_chances, 0.0)
        chances = chances_of(normed_ffn)
        grad_logits = chances * (
            grad_chances - jnp.sum(chances * grad_chances, axis=-1, keepdims=True)
        )
        grad_logits = grad_logits.astype(BF16)
        grad_router = dot_tn(normed_ffn, grad_logits)

        result = hidden + live * moe_out
        grad_result = cotangent.astype(F32)
        grad_normed_ffn = grad_ffn + dot_nt(grad_logits, w_router)
        grad_ffn_gain = jnp.sum(grad_normed_ffn * hidden * second_scale, axis=0)
        grad_hidden = grad_result + norm_back(hidden, second_scale, ffn_norm_gain, grad_normed_ffn)
        grad_attention = gather((live * grad_hidden).astype(BF16), "rep")

        grad_out_w = dot_tn(mixed, grad_attention)
        grad_mixed = dot_nt(grad_attention, w_out).astype(BF16).reshape(by_head)
        grad_value = jnp.einsum("shqk,sqhd->skhd", soft_low, grad_mixed, preferred_element_type=F32)
        grad_value = grad_value.astype(BF16)
        grad_probs = jnp.einsum("sqhd,skhd->shqk", grad_mixed, value, preferred_element_type=F32)
        row_dot = jnp.sum(soft * grad_probs, axis=-1, keepdims=True)
        grad_scores = (soft * (grad_probs - row_dot)).astype(BF16)
        grad_query = jnp.einsum("shqk,skhd->sqhd", grad_scores, key, preferred_element_type=F32)
        grad_key = jnp.einsum("shqk,sqhd->skhd", grad_scores, query, preferred_element_type=F32)
        grad_query = rotate(grad_query * score_scale, cosine, -sine)
        grad_key = rotate(grad_key * score_scale, cosine, -sine)
        grad_qgain = jnp.sum(grad_query * query_raw * query_scale, axis=(0, 1, 2))
        grad_kgain = jnp.sum(grad_key * key_raw * key_scale, axis=(0, 1, 2))
        grad_qkv = jnp.concatenate(
            [
                norm_back(query_raw, query_scale, query_gain, grad_query).reshape(total, cols).astype(BF16),
                norm_back(key_raw, key_scale, key_gain, grad_key).reshape(total, cols).astype(BF16),
                grad_value.reshape(total, cols),
            ],
            axis=1,
        )
        grad_normed = scatter_sum(dot_nt(grad_qkv, w_qkv).astype(BF16), "rep").astype(F32)
        grad_norm_gain = jnp.sum(grad_normed * stream * first_scale, axis=0)
        input_grad = grad_hidden + norm_back(stream, first_scale, norm_gain, grad_normed)

        sum_dn = scatter_sum(dot_tn(inner_gated, grad_moe).astype(BF16), "shard")
        sum_gu = scatter_sum(dot_tn(ffn_all, grad_gu).astype(BF16), "shard")
        sum_out = scatter_sum(grad_out_w.astype(BF16), "shard")
        sum_qkv = scatter_sum(dot_tn(normed_all, grad_qkv).astype(BF16), "shard")
        sum_out = lax.ppermute(sum_out, ("rep", "shard"), back)

        all_dn = gather(sum_dn, "rep").astype(F32).reshape(experts, parts * sub, width)
        all_gu = lax.all_gather(sum_gu, "rep").astype(F32)
        all_gu = all_gu.reshape(experts, parts, rows, 2, shards, sub).transpose(3, 0, 2, 4, 1, 5)
        all_gu = all_gu.reshape(2, experts, rows, hidden_total)
        all_out = gather(sum_out, "rep").astype(F32).reshape(shards, per_plane, out_rows, width)
        all_out = all_out.transpose(1, 0, 2, 3).reshape(rows, width)
        all_qkv = lax.all_gather(sum_qkv, "rep").astype(F32).reshape(reps, rows, 3, cols)
        all_qkv = all_qkv.transpose(2, 1, 0, 3).reshape(3, rows, width)

        square_sums = jnp.stack(
            [
                jnp.sum(live * stream * stream),
                jnp.sum(live * hidden * hidden),
                jnp.sum(live * result * result),
                jnp.sum(live),
            ]
        )
        norm_sum, qgain_sum, kgain_sum, ffn_sum, router_sum, stat_sum = lax.psum(
            (grad_norm_gain, grad_qgain, grad_kgain, grad_ffn_gain, grad_router, square_sums),
            ("rep", "shard"),
        )
        residual_rms = jnp.sqrt(stat_sum[:3] / (stat_sum[3] * width))
        return (
            result.astype(BF16), input_grad.astype(BF16), norm_sum,
            all_qkv[0], all_qkv[1], all_qkv[2], all_out,
            qgain_sum, kgain_sum, ffn_sum, router_sum,
            all_gu[0], all_gu[1], all_dn, residual_rms,
        )

    return body


def solution(mesh):
    by_token, by_shard, inner_shard = P(("rep", "shard"), None), P("shard", None), P(None, "shard", None)
    in_specs = (
        by_token, by_token, P(("rep", "shard")), by_token, P(),
        by_shard, by_shard, by_shard, by_shard, P(), P(), P(), P(),
        inner_shard, inner_shard, inner_shard,
    )
    out_specs = (
        by_token, by_token, P(), by_shard, by_shard, by_shard, by_shard, P(), P(), P(), P(),
        inner_shard, inner_shard, inner_shard, P(),
    )
    body = make_body(mesh.shape["rep"], mesh.shape["shard"])
    return jax.shard_map(body, mesh=mesh, in_specs=in_specs, out_specs=out_specs, check_vma=False)
```

time: 3230 us -> 1320 us (0.41)
  waiting for transfers between devices: 2740 us -> 778 us
  local copies, waits for them, and re-layouts: 107 us -> 233 us
  other arithmetic: 113 us -> 56.7 us
  matrix products: 201 us -> 152 us
    all_gather x7 -> x12, waiting for transfers between devices: 1350 us -> 420 us  [the longest x10 372 us: gather(): return lax.all_gather(piece, axis, axis=dim, tiled=True)]
    reduce_scatter x4 -> x8, waiting for transfers between devices: 1190 us -> 357 us  [scatter_sum(): return lax.psum_scatter(whole, axis, scatter_dimension=0, tiled=True)]
    psum x1 -> x0, waiting for transfers between devices: 200 us -> none  [body(): lax.psum(attn_part, 'rep').astype(jnp.float32)]
    slice x3 -> x10, local copies, waits for them, and re-layouts: 11.2 us -> 72 us  [the longest x2 24.6 us: body(): all_gu[1]]
    dot_general x30 -> x21, matrix products: 201 us -> 146 us  [the longest x5 49.4 us: dot_nt(): lax.dot_general(left, right, (((1,), (1,)), ((), ())), preferred_element_...]
    all_gather x0 -> x3, blocking collectives: none -> 32.8 us  [the longest x2 23.6 us: gather(): return lax.all_gather(piece, axis, axis=dim, tiled=True)]
  transfers between devices with their start and end apart: 12 -> 22, of which waited for: 12 -> 17; matrix products, arithmetic and copies ran while one was open for 10% -> 24% of each run, Pallas kernels for 0% -> 0%
where the time goes in v1:
time: 1320 us; the launch traced here: 1310 us
  waiting for transfers between devices  778 us (59%)
  local copies, waits for them, and re-layouts  233 us (18%)
  matrix products  152 us (12%)
  blocking collectives  73.7 us (6%)
  other arithmetic  56.7 us (4%)
  between operations  16 us (1%)
    all_gather x10, waiting for transfers between devices, gather(): return lax.all_gather(piece, axis, axis=dim, tiled=True)  372 us
    reduce_scatter x8, waiting for transfers between devices, scatter_sum(): return lax.psum_scatter(whole, axis, scatter_dimension=0, tiled=True)  357 us
    unnamed x127, local copies, waits for them, and re-layouts  56.8 us
    dot_general x5, matrix products, dot_nt(): lax.dot_general(left, right, (((1,), (1,)), ((), ())), preferred_element_...  49.4 us
    all_gather x1, waiting for transfers between devices, body(): all_gu = lax.all_gather(sum_gu, 'rep').astype(F32)  46.8 us
    dot_general x6, matrix products, dot(): return jnp.dot(left, right, preferred_element_type=F32)  44.8 us
    dot_general x5, matrix products, dot_tn(): lax.dot_general(left, right, (((0,), (0,)), ((), ())), preferred_element_...  41.1 us
    psum x1, blocking collectives, body(): lax.psum((grad_norm_gain, grad_qgain, grad_kgain, grad_ffn_gain, grad_rou...  40.9 us
  transfers between devices with their start and end apart: 22, of which 17 were waited for; matrix products, arithmetic and copies ran while one was open for 24% of the time, Pallas kernels for 0%

profile of v1, /device:TPU:0, one launch (start us, length us, event | category | flops | bytes accessed | tf_op | source)
XLA Modules:
  0.0 1312.8 jit_solution(3289610690287515567)
XLA Ops:
  16.1 14.6 %all-gather.3 = s32[8,1,256]{2,1,0:T(1,128)S(1)} all-gather(s32[1,1,256]{2,1,0:T(1,128)S(1)} %bitcast.196), channel_id=1, replica_groups=mesh['rep'=8,'shard'=4] {'rep'}, dimensions={0}, use_global_device_ids=true | all-gather | bytes 9216 | tf_op jit(solution)/shard_map/all_gather | solution.py:51
  32.5 56.2 %all-gather.19.cloned.1.call-done = bf16[2048,768]{1,0:T(8,128)(2,1)} async-done(((bf16[512,768]{1,0:T(8,128)(2,1)}), bf16[2048,768]{1,0:T(8,128)(2,1)}) %all-gather.19.cloned.1.call-update) | async-done | bytes 3145744 | tf_op jit(solution)/shard_map/all_gather | solution.py:51
  88.7 57.2 %all-gather.17.cloned.1.call-done = bf16[2048,2048]{1,0:T(8,128)(2,1)} async-done(((bf16[256,2048]{1,0:T(8,128)(2,1)}), bf16[2048,2048]{1,0:T(8,128)(2,1)}) %all-gather.17.cloned.1.call-update) | async-done | bytes 8388624 | tf_op jit(solution)/shard_map/all_gather | solution.py:51
  145.9 10.0 fusion.70
  210.0 70.7 %reduce-scatter.9.cloned.1.call-done = bf16[256,2048]{1,0:T(8,128)(2,1)} async-done(((bf16[2048,2048]{1,0:T(8,128)(2,1)}), bf16[256,2048]{1,0:T(8,128)(2,1)}) %reduce-scatter.9.cloned.1.call-update) | async-done | bytes 1048592 | tf_op jit(solution)/shard_map/reduce_scatter | solution.py:55
  306.2 32.6 %all-gather.23.cloned.1.call-done = bf16[2048,2048]{1,0:T(8,128)(2,1)} async-done(((bf16[256,2048]{1,0:T(8,128)(2,1)}), bf16[2048,2048]{1,0:T(8,128)(2,1)}) %all-gather.23.cloned.1.call-update) | async-done | bytes 8388624 | tf_op jit(solution)/shard_map/all_gather | solution.py:51
  344.6 77.1 %all-gather.25.cloned.1.call-done = bf16[2048,1024]{0,1:T(8,128)(2,1)} async-done(((bf16[512,1024]{0,1:T(8,128)(2,1)}), bf16[2048,1024]{0,1:T(8,128)(2,1)}) %all-gather.25.cloned.1.call-update) | async-done | bytes 4194320 | tf_op jit(solution)/shard_map/all_gather | solution.py:51
  421.7 14.5 %fusion.71 = f32[2048,1024]{0,1:T(8,128)} fusion(bf16[2048,2048]{1,0:T(8,128)(2,1)} %all-gather.23.cloned.1.call-done, bf16[2048,1024]{0,1:T(8,128)(2,1)} %all-gather.25.cloned.1.call-done), kind=kOutput, calls=%fused_computation.185 | convolution fusion | flops 8589934592 | bytes 20971520 | tf_op jit(solution)/shard_map/dot_general | solution.py:39
  436.2 32.2 %all-gather.35.cloned.1.call-done = bf16[1,512,2048]{2,1,0:T(8,128)(2,1)} async-done(((bf16[1,128,2048]{2,1,0:T(8,128)(2,1)}), bf16[1,512,2048]{2,1,0:T(8,128)(2,1)}) %all-gather.35.cloned.1.call-update) | async-done | bytes 2097168 | tf_op jit(solution)/shard_map/all_gather | solution.py:51
  468.4 55.8 %all-gather.27.cloned.1.call-done = bf16[2048,2048]{1,0:T(8,128)(2,1)} async-done(((bf16[256,2048]{1,0:T(8,128)(2,1)}), bf16[2048,2048]{1,0:T(8,128)(2,1)}) %all-gather.27.cloned.1.call-update) | async-done | bytes 8388624 | tf_op jit(solution)/shard_map/all_gather | solution.py:51
  524.2 12.6 multiply_convert_fusion.2
  545.4 14.3 %convolution_convert_fusion.1 = bf16[2048,2048]{1,0:T(8,128)(2,1)} fusion(bf16[2048,1024]{0,1:T(8,128)(2,1)} %all-gather.25.cloned.1.call-done, bf16[2048,512]{0,1:T(8,128)(2,1)} %get-tuple-element.103, bf16[2048,512]{0,1:T(8,128)(2,1)} %get-tuple-element.102), kind=kOutput, calls=%fused_computation.2 | convolution fusion | flops 8602517504 | bytes 16777216 | tf_op jit(solution)/shard_map/dot_general | solution.py:43
  570.8 45.6 %reduce-scatter.11.cloned.1.call-done = bf16[256,2048]{1,0:T(8,128)(2,1)} async-done(((bf16[2048,2048]{1,0:T(8,128)(2,1)}), bf16[256,2048]{1,0:T(8,128)(2,1)}) %reduce-scatter.11.cloned.1.call-update) | async-done | bytes 1048592 | tf_op jit(solution)/shard_map/reduce_scatter | solution.py:55
  616.4 75.2 %reduce-scatter.13.cloned.1.call-done = bf16[256,2048]{1,0:T(8,128)(2,1)} async-done(((bf16[2048,2048]{1,0:T(8,128)(2,1)}), bf16[256,2048]{1,0:T(8,128)(2,1)}) %reduce-scatter.13.cloned.1.call-update) | async-done | bytes 1048592 | tf_op jit(solution)/shard_map/reduce_scatter | solution.py:55
  699.0 9.8 convolution_convert_fusion.6
  710.4 13.3 %convolution_convert_fusion.4 = bf16[2048,1024]{1,0:T(8,128)(2,1)} fusion(bf16[2048,2048]{1,0:T(8,128)(2,1)} %all-gather.23.cloned.1.call-done, bf16[2048,512]{0,1:T(8,128)(2,1)} %get-tuple-element.103, bf16[2048,512]{0,1:T(8,128)(2,1)S(1)} %copy-done.55), kind=kOutput, calls=%fused_computation.28 | convolution fusion | flops 8600420352 | bytes 16777216 | tf_op jit(solution)/shard_map/dot_general | solution.py:47
  728.3 25.2 %all-gather.29.cloned.1.call-done = bf16[2048,2048]{1,0:T(8,128)(2,1)} async-done(((bf16[256,2048]{1,0:T(8,128)(2,1)}), bf16[2048,2048]{1,0:T(8,128)(2,1)}) %all-gather.29.cloned.1.call-update) | async-done | bytes 8388624 | tf_op jit(solution)/shard_map/all_gather | solution.py:51
  816.0 10.5 convolution_convert_fusion.5
  827.2 52.1 %reduce-scatter.21.cloned.1.call-done = bf16[512,1024]{1,0:T(8,128)(2,1)} async-done(((bf16[2048,1024]{1,0:T(8,128)(2,1)}), bf16[512,1024]{1,0:T(8,128)(2,1)}) %reduce-scatter.21.cloned.1.call-update) | async-done | bytes 1048592 | tf_op jit(solution)/shard_map/reduce_scatter | solution.py:55
  879.3 29.9 %reduce-scatter.19.cloned.1.call-done = bf16[64,2048]{1,0:T(8,128)(2,1)} async-done(((bf16[256,2048]{1,0:T(8,128)(2,1)}), bf16[64,2048]{1,0:T(8,128)(2,1)}) %reduce-scatter.19.cloned.1.call-update) | async-done | bytes 262160 | tf_op jit(solution)/shard_map/reduce_scatter | solution.py:55
  911.5 11.0 convolution_convert_fusion
  922.6 60.4 %reduce-scatter.17.cloned.1.call-done = bf16[512,768]{1,0:T(8,128)(2,1)} async-done(((bf16[2048,768]{1,0:T(8,128)(2,1)}), bf16[512,768]{1,0:T(8,128)(2,1)}) %reduce-scatter.17.cloned.1.call-update) | async-done | bytes 786448 | tf_op jit(solution)/shard_map/reduce_scatter | solution.py:55
  983.3 35.9 %all-gather.33.cloned.1.call-done = bf16[1024,2048]{1,0:T(8,128)(2,1)} async-done(((bf16[128,2048]{1,0:T(8,128)(2,1)}), bf16[1024,2048]{1,0:T(8,128)(2,1)}) %all-gather.33.cloned.1.call-update) | async-done | bytes 4194320 | tf_op jit(solution)/shard_map/all_gather | solution.py:51
  1028.5 46.8 %all-gather.39.cloned.1.call-done = bf16[4096,1024]{1,0:T(8,128)(2,1)} async-done(((bf16[512,1024]{1,0:T(8,128)(2,1)}), bf16[4096,1024]{1,0:T(8,128)(2,1)}) %all-gather.39.cloned.1.call-update) | async-done | bytes 8388624 | tf_op jit(solution)/shard_map/all_gather | solution.py:213
  1075.4 16.6 %reshape.304 = f32[4,2,512,2,4,128]{5,4,3,2,1,0:T(4,128)} reshape(bf16[4096,1024]{1,0:T(8,128)(2,1)} %all-gather.39.cloned.1.call-done) | data formatting | bytes 25165824 | tf_op jit(solution)/shard_map/transpose | solution.py:214
  1101.1 12.2 copy.241
  1113.3 12.2 squeeze.21
  1125.5 15.5 %copy.242 = f32[1,4,512,4,2,128]{5,4,3,2,1,0:T(2,128)} copy(f32[1,4,512,4,2,128]{5,3,0,2,4,1:T(4,128)} %get-tuple-element.100) | data formatting | bytes 16777216 | tf_op jit(solution)/shard_map/slice | solution.py:238
  1140.9 11.5 squeeze.22
  1157.0 23.4 %reduce-scatter.15.cloned.1.call-done = bf16[256,2048]{1,0:T(8,128)(2,1)} async-done(((bf16[2048,2048]{1,0:T(8,128)(2,1)}), bf16[256,2048]{1,0:T(8,128)(2,1)}) %reduce-scatter.15.cloned.1.call-update) | async-done | bytes 1048592 | tf_op jit(solution)/shard_map/reduce_scatter | solution.py:55
  1182.3 40.9 %all-reduce = (f32[2048]{0:T(1024)}, f32[128]{0:T(128)}, f32[128]{0:T(128)}, f32[2048]{0:T(1024)}, f32[2048,4]{0,1:T(4,128)}, /*index=5*/f32[4]{0:T(128)S(1)}) all-reduce(f32[2048]{0:T(1024)S(1)} %get-tuple-element.81, f32[128]{0:T(128)S(1)} %bitcast_reduce_fusion.1, ...), channel_id=1, replica_groups=mesh['rep'=8,'shard'=4] {'rep','shard'}, use_global_device_ids=true, to_apply=%region_26.27 | all-reduce | flops 12548 | bytes 100384 | tf_op jit(solution)/shard_map/psum | solution.py:229
  1238.3 21.9 %copy.272 = f32[96,8,8,512]{3,2,1,0:T(8,128)} copy(f32[96,8,8,512]{3,1,2,0:T(8,128)} %bitcast.168) | data formatting | bytes 25165824
  (279 shorter events, 279.4 us)
Async XLA Ops:
  7.2 81.5 %all-gather.19.cloned.1.call-start = ((), (), s32[]{:S(2)}) async-start(), calls=%async_computation.9 | async-start | bytes 3932160 | tf_op jit(solution)/shard_map/all_gather | solution.py:51
  10.9 135.0 %all-gather.17.cloned.1.call-start = ((), (), s32[]{:S(2)}) async-start(), calls=%async_computation.8 | async-start | bytes 9437184 | tf_op jit(solution)/shard_map/all_gather | solution.py:51
  13.1 188.8 %all-gather.21.cloned.1.call-start = ((), (), s32[]{:S(2)}) async-start(), calls=%async_computation.10 | async-start | bytes 1310720 | tf_op jit(solution)/shard_map/all_gather | solution.py:51
  14.2 17.6 %collective-permute-start = (bf16[64,2048]{1,0:T(8,128)(2,1)S(1)}, bf16[64,2048]{1,0:T(8,128)(2,1)S(1)}, u32[]{:S(2)}, u32[]{:S(2)}) collective-permute-start(bf16[64,2048]{1,0:T(8,128)(2,1)S(1)} %constant_dynamic-slice_fusion.5), channel_id=1, source_target_pairs={{0,0},{1,8},{2,16},{3,24},{4,4},{5,12},{6,20},{7,28},{8,1},{9,9},{... | collective-permute-start | bytes 786440 | tf_op jit(solution)/shard_map/ppermute | solution.py:99
  32.5 248.3 %reduce-scatter.9.cloned.1.call-start = ((), (), s32[]{:S(2)}) async-start(), calls=%async_computation.11 | async-start | bytes 9437184 | tf_op jit(solution)/shard_map/reduce_scatter | solution.py:55
  209.4 73.3 %copy-start.44 = (f32[2048]{0:T(1024)S(1)}, f32[2048]{0:T(1024)}, u32[]{:S(2)}) copy-start(f32[2048]{0:T(1024)} %param.27) | copy-start | bytes 24580
  209.4 129.4 %all-gather.23.cloned.1.call-start = ((), (), s32[]{:S(2)}) async-start(), calls=%async_computation.12 | async-start | bytes 9437184 | tf_op jit(solution)/shard_map/all_gather | solution.py:51
  284.2 137.5 %all-gather.25.cloned.1.call-start = ((), (), s32[]{:S(2)}) async-start(), calls=%async_computation.13 | async-start | bytes 5242880 | tf_op jit(solution)/shard_map/all_gather | solution.py:51
  293.9 174.5 %all-gather.35.cloned.1.call-start = ((), (), s32[]{:S(2)}) async-start(), calls=%async_computation.25 | async-start | bytes 2621440 | tf_op jit(solution)/shard_map/all_gather | solution.py:51
  295.9 43.0 %copy-start.43 = (bf16[2048,4]{0,1:T(4,128)(2,1)S(1)}, bf16[2048,4]{0,1:T(4,128)(2,1)}, u32[]{:S(2)}) copy-start(bf16[2048,4]{0,1:T(4,128)(2,1)} %param.28) | copy-start | bytes 49156
  295.9 228.3 %all-gather.27.cloned.1.call-start = ((), (), s32[]{:S(2)}) async-start(), calls=%async_computation.15 | async-start | bytes 9437184 | tf_op jit(solution)/shard_map/all_gather | solution.py:51
  297.1 319.3 %reduce-scatter.11.cloned.1.call-start = ((), (), s32[]{:S(2)}) async-start(), calls=%async_computation.14 | async-start | bytes 9437184 | tf_op jit(solution)/shard_map/reduce_scatter | solution.py:55
  544.9 146.6 %reduce-scatter.13.cloned.1.call-start = ((), (), s32[]{:S(2)}) async-start(), calls=%async_computation.16 | async-start | bytes 9437184 | tf_op jit(solution)/shard_map/reduce_scatter | solution.py:55
  559.7 193.8 %all-gather.29.cloned.1.call-start = ((), (), s32[]{:S(2)}) async-start(), calls=%async_computation.17 | async-start | bytes 9437184 | tf_op jit(solution)/shard_map/all_gather | solution.py:51
  570.8 125.5 %copy-start.19 = (bf16[256,2048]{1,0:T(8,128)(2,1)S(1)}, bf16[256,2048]{1,0:T(8,128)(2,1)}, u32[]{:S(2)}) copy-start(bf16[256,2048]{1,0:T(8,128)(2,1)} %param.17) | copy-start | bytes 3145732
  699.0 127.6 %reduce-scatter.23.cloned.1.call-start = ((), (), s32[]{:S(2)}) async-start(), calls=%async_computation.23 | async-start | bytes 2621440 | tf_op jit(solution)/shard_map/reduce_scatter | solution.py:55
  708.9 170.3 %reduce-scatter.21.cloned.1.call-start = ((), (), s32[]{:S(2)}) async-start(), calls=%async_computation.22 | async-start | bytes 5242880 | tf_op jit(solution)/shard_map/reduce_scatter | solution.py:55
  723.8 185.4 %reduce-scatter.19.cloned.1.call-start = ((), (), s32[]{:S(2)}) async-start(), calls=%async_computation.20 | async-start | bytes 1310720 | tf_op jit(solution)/shard_map/reduce_scatter | solution.py:55
  723.8 29.7 %copy-start.31 = (bf16[256,2048]{1,0:T(8,128)(2,1)S(1)}, bf16[256,2048]{1,0:T(8,128)(2,1)}, u32[]{:S(2)}) copy-start(bf16[256,2048]{1,0:T(8,128)(2,1)} %all-gather.21.cloned.1.call-done) | copy-start | bytes 3145732
  792.1 191.0 %reduce-scatter.17.cloned.1.call-start = ((), (), s32[]{:S(2)}) async-start(), calls=%async_computation.19 | async-start | bytes 3932160 | tf_op jit(solution)/shard_map/reduce_scatter | solution.py:55
  826.5 85.0 %copy-start.37 = (bf16[256,8,2,128]{3,1,2,0:T(8,128)(2,1)S(1)}, bf16[256,8,2,128]{3,1,2,0:T(8,128)(2,1)}, u32[]{:S(2)}) copy-start(bf16[256,8,2,128]{3,1,2,0:T(8,128)(2,1)} %copy-done.36) | copy-start | bytes 3145732
  826.5 192.7 %all-gather.33.cloned.1.call-start = ((), (), s32[]{:S(2)}) async-start(), calls=%async_computation.24 | async-start | bytes 4718592 | tf_op jit(solution)/shard_map/all_gather | solution.py:51
  827.1 248.2 %all-gather.39.cloned.1.call-start = ((), (), s32[]{:S(2)}) async-start(), calls=%async_computation.27 | async-start | bytes 9437184 | tf_op jit(solution)/shard_map/all_gather | solution.py:213
  879.2 273.3 %all-gather.31.cloned.1.call-start = ((), (), s32[]{:S(2)}) async-start(), calls=%async_computation.21 | async-start | bytes 2359296 | tf_op jit(solution)/shard_map/all_gather | solution.py:51
  909.1 1.6 collective-permute-start.1
  911.5 268.9 %reduce-scatter.15.cloned.1.call-start = ((), (), s32[]{:S(2)}) async-start(), calls=%async_computation.18 | async-start | bytes 9437184 | tf_op jit(solution)/shard_map/reduce_scatter | solution.py:55
  922.5 60.5 %copy-start.10 = (bf16[256,2048]{1,0:T(8,128)(2,1)S(1)}, bf16[256,2048]{1,0:T(8,128)(2,1)}, u32[]{:S(2)}) copy-start(bf16[256,2048]{1,0:T(8,128)(2,1)} %multiply_convert_fusion.5) | copy-start | bytes 3145732
  922.6 306.1 %all-gather.37.cloned.1.call-start = ((), (), s32[]{:S(2)}) async-start(), calls=%async_computation.26 | async-start | bytes 7077888 | tf_op jit(solution)/shard_map/all_gather | solution.py:218
  1154.6 25.7 %copy-start.3 = (bf16[256,2048]{1,0:T(8,128)(2,1)S(1)}, bf16[256,2048]{1,0:T(8,128)(2,1)}, u32[]{:S(2)}) copy-start(bf16[256,2048]{1,0:T(8,128)(2,1)} %param.16) | copy-start | bytes 3145732
  1154.6 25.7 %copy-start.42 = (f32[2048]{0:T(1024)S(1)}, f32[2048]{0:T(1024)}, u32[]{:S(2)}) copy-start(f32[2048]{0:T(1024)} %param.20) | copy-start | bytes 24580
  1157.0 68.0 %copy-start.15 = (f32[256,2048]{1,0:T(8,128)S(1)}, f32[256,2048]{1,0:T(8,128)}, u32[]{:S(2)}) copy-start(f32[256,2048]{1,0:T(8,128)} %get-tuple-element.97) | copy-start | bytes 6291460
  1157.0 68.0 %copy-start.52 = (f32[256]{0:T(256)S(1)}, f32[256]{0:T(256)}, u32[]{:S(2)}) copy-start(f32[256]{0:T(256)} %get-tuple-element.130) | copy-start | bytes 3076
  (48 other events, 222.8 us)
Sparse Core Ops, SparseCore 0:
  11.0 77.6 all-gather.18
  91.2 54.6 all-gather.16
  148.0 27.9 all-gather.20
  209.5 71.2 reduce-scatter.8
  284.3 54.4 all-gather.22
  340.9 80.7 all-gather.24
  423.9 44.4 all-gather.34
  471.0 53.0 all-gather.26
  545.0 71.2 reduce-scatter.10
  620.2 71.2 reduce-scatter.12
  699.1 54.3 all-gather.28
  756.3 43.8 reduce-scatter.22
  803.1 76.0 reduce-scatter.20
  881.5 27.6 reduce-scatter.18
  911.9 71.1 reduce-scatter.16
  984.8 34.3 all-gather.32
  1020.9 54.3 all-gather.38
  1077.7 27.8 all-gather.30
  1109.1 71.2 reduce-scatter.14
  1182.3 46.3 all-gather.36

commit v2 on v1

v2 whole, which is shorter than its diff:
```python
import functools

import jax
import jax.numpy as jnp
from jax import lax
from jax.experimental import pallas as pl
from jax.experimental.pallas import tpu as pltpu
from jax.sharding import PartitionSpec as P

EPS = 1e-06
THETA = 10000.0
MASKED = -1e30
F32 = jnp.float32
BF16 = jnp.bfloat16


def rms_scale(field):
    return lax.rsqrt(jnp.mean(field * field, axis=-1, keepdims=True) + EPS)


def norm_back(field, scale, gain, upstream):
    weighted = upstream * gain
    inner = jnp.sum(weighted * field, axis=-1, keepdims=True)
    return scale * weighted - field * scale**3 * inner / field.shape[-1]


def rotary_tables(length, dim):
    half = dim // 2
    frequency = THETA ** (-2.0 * jnp.arange(half, dtype=F32) / dim)
    angles = jnp.arange(length, dtype=F32)[:, None] * frequency[None, :]
    return jnp.cos(angles), jnp.sin(angles)


def rotate(field, cosine, sine):
    half = field.shape[-1] // 2
    first, second = field[..., :half], field[..., half:]
    return jnp.concatenate(
        [first * cosine - second * sine, second * cosine + first * sine], axis=-1
    )


def dot(left, right):
    return jnp.dot(left, right, preferred_element_type=F32)


def dot_nt(left, right):
    return lax.dot_general(left, right, (((1,), (1,)), ((), ())), preferred_element_type=F32)


def dot_tn(left, right):
    return lax.dot_general(left, right, (((0,), (0,)), ((), ())), preferred_element_type=F32)


def after(value, *events):
    return lax.optimization_barrier((value, *events))[0]


def total_over_all(value, sizes):
    for axis, size in sizes:
        bit = 1
        while bit < size:
            value = value + lax.ppermute(value, axis, [(i, i ^ bit) for i in range(size)])
            bit *= 2
    return value


def gather(piece, axis, dim=0):
    return lax.all_gather(piece, axis, axis=dim, tiled=True)


def scatter_sum(whole, axis):
    return lax.psum_scatter(whole, axis, scatter_dimension=0, tiled=True)


SCALE = 1.0
IDS = 16


def params(mib=24):
    return pltpu.CompilerParams(vmem_limit_bytes=mib * 2**20)


def whole(array):
    return pl.BlockSpec(array.shape, lambda i: (0,) * len(array.shape), pipeline_mode=pl.Buffered(1))


def cost(flops, arrays):
    moved = sum(a.size * a.dtype.itemsize for a in arrays)
    return pl.CostEstimate(flops=int(flops * SCALE), bytes_accessed=int(moved * SCALE), transcendentals=0)


def turned(rows):
    rows = jnp.concatenate([rows, jnp.zeros((128 - rows.shape[0], rows.shape[1]), F32)])
    return rows.T


def spin(field, cosine, sine):
    return field * cosine + pltpu.roll(field, field.shape[-1] // 2, 1) * sine


def head_state(raw, ids, gains, cosine, sine, cols, lane, score_scale):
    size = gains.shape[-1]
    query_raw = raw[:, lane : lane + size]
    key_raw = raw[:, cols + lane : cols + lane + size]
    value = raw[:, 2 * cols + lane : 2 * cols + lane + size].astype(BF16)
    query_scale, key_scale = rms_scale(query_raw), rms_scale(key_raw)
    query = spin(query_raw * query_scale * gains[0:1], cosine, sine).astype(BF16)
    key = spin(key_raw * key_scale * gains[1:2], cosine, sine).astype(BF16)
    scores = dot_nt(query, key) * score_scale
    scores = jnp.where(turned(ids)[:, 0:1] == ids[0:1], scores, MASKED)
    exponent = jnp.exp(scores - jnp.max(scores, axis=-1, keepdims=True))
    soft = exponent / jnp.sum(exponent, axis=-1, keepdims=True)
    return query_raw, key_raw, value, query_scale, key_scale, query, key, soft


def attend_kernel(length, score_scale, blk0, blk1, w_qkv, gains, cosine, sine, raw_ref, mixed_ref):
    size = gains.shape[-1]
    cols = w_qkv.shape[1] // 3
    raw = dot(jnp.concatenate([blk0[:length], blk1[:length]]), w_qkv[...])
    raw_ref[...] = raw
    for i, blk in enumerate((blk0, blk1)):
        ids = blk[length : length + IDS, :length].astype(F32)
        mine = raw[i * length : (i + 1) * length]
        for lane in range(0, cols, size):
            state = head_state(mine, ids, gains[...], cosine[...], sine[...], cols, lane, score_scale)
            value, soft = state[2], state[7]
            mixed = dot(soft.astype(BF16), value).astype(BF16)
            mixed_ref[i * length : (i + 1) * length, lane : lane + size] = mixed


def attend(pair, w_qkv, gains, cosine, sine, length, score_scale):
    width, cols = w_qkv.shape[0], w_qkv.shape[1] // 3
    ins = (*pair, w_qkv, gains, cosine, sine)
    specs = [whole(a) for a in ins]
    outs = (
        jax.ShapeDtypeStruct((2 * length, 3 * cols), F32),
        jax.ShapeDtypeStruct((2 * length, cols), BF16),
    )
    return pl.pallas_call(
        functools.partial(attend_kernel, length, score_scale),
        grid=(1,),
        in_specs=specs,
        out_specs=tuple(whole(a) for a in outs),
        out_shape=outs,
        compiler_params=params(),
        cost_estimate=cost(12 * length * width * cols, ins + outs),
        name="attend",
    )(*ins)


def attend_back_kernel(
    length, score_scale, da0, da1, blk0, blk1, raw_ref, w_qkv, w_out, gains, cosine, sine,
    out0, out1, grad_ref, gain_ref,
):
    cols = w_out.shape[0]
    size = gains.shape[-1]
    grad_mixed_all = dot_nt(jnp.concatenate([da0[...], da1[...]]), w_out[...]).astype(BF16)
    qgain = jnp.zeros((1, size), F32)
    kgain = jnp.zeros((1, size), F32)
    for i, (blk, out) in enumerate(((blk0, out0), (blk1, out1))):
        ids = blk[...].astype(F32)
        span = slice(i * length, (i + 1) * length)
        mine = raw_ref[span]
        for lane in range(0, cols, size):
            query_raw, key_raw, value, query_scale, key_scale, query, key, soft = head_state(
                mine, ids, gains[...], cosine[...], sine[...], cols, lane, score_scale
            )
            grad_mixed = grad_mixed_all[span, lane : lane + size]
            grad_value = dot_tn(soft.astype(BF16), grad_mixed).astype(BF16)
            grad_probs = dot_nt(grad_mixed, value)
            row_dot = jnp.sum(soft * grad_probs, axis=-1, keepdims=True)
            grad_scores = (soft * (grad_probs - row_dot)).astype(BF16)
            grad_query = spin(dot(grad_scores, key) * score_scale, cosine[...], -sine[...])
            grad_key = spin(dot_tn(grad_scores, query) * score_scale, cosine[...], -sine[...])
            qgain += jnp.sum(grad_query * query_raw * query_scale, axis=0, keepdims=True)
            kgain += jnp.sum(grad_key * key_raw * key_scale, axis=0, keepdims=True)
            grad_ref[span, lane : lane + size] = norm_back(
                query_raw, query_scale, gains[0:1], grad_query
            ).astype(BF16)
            grad_ref[span, cols + lane : cols + lane + size] = norm_back(
                key_raw, key_scale, gains[1:2], grad_key
            ).astype(BF16)
            grad_ref[span, 2 * cols + lane : 2 * cols + lane + size] = grad_value
        out[...] = dot_nt(grad_ref[span], w_qkv[...]).astype(BF16)
    gain_ref[...] = jnp.concatenate([qgain, kgain, jnp.zeros((6, size), F32)])


def attend_back(pair, ids, raw, w_qkv, w_out, gains, cosine, sine, length, score_scale):
    width, cols = w_qkv.shape[0], w_out.shape[0]
    ins = (*pair, *ids, raw, w_qkv, w_out, gains, cosine, sine)
    outs = (
        jax.ShapeDtypeStruct((length, width), BF16),
        jax.ShapeDtypeStruct((length, width), BF16),
        jax.ShapeDtypeStruct((2 * length, 3 * cols), BF16),
        jax.ShapeDtypeStruct((8, gains.shape[-1]), F32),
    )
    specs = [whole(a) for a in ins]
    for i in (2, 3):
        specs[i] = pl.BlockSpec((IDS, length), lambda i: (length // IDS, 0))
    return pl.pallas_call(
        functools.partial(attend_back_kernel, length, score_scale),
        grid=(1,),
        in_specs=specs,
        out_specs=tuple(whole(a) for a in outs),
        out_shape=outs,
        compiler_params=params(),
        cost_estimate=cost(24 * length * width * cols, ins + outs),
        name="attend_back",
    )(*ins)


def expert_in_kernel(
    length, experts, place, b0, b1, ids0, ids1, w_router, w_gu, gated_ref, inner_ref, factor_ref
):
    hid = w_gu.shape[1] // 2
    expert = place[1]
    field = joined((b0, b1))
    logits = dot(field, w_router[...])
    lane = lax.broadcasted_iota(jnp.int32, logits.shape, 1)
    logits = jnp.where(lane < experts, logits, MASKED)
    chances = jnp.exp(logits - jnp.max(logits, axis=-1, keepdims=True))
    chance = jnp.sum(jnp.where(lane == expert, chances, 0.0), axis=-1, keepdims=True)
    chance = chance / jnp.sum(chances, axis=-1, keepdims=True)
    routes = jnp.concatenate([turned(ids0[...].astype(F32)), turned(ids1[...].astype(F32))])
    wanted = expert.astype(F32)
    chosen = jnp.logical_or(routes[:, 1:2] == wanted, routes[:, 2:3] == wanted)
    gate = jnp.where(chosen, chance, 0.0)
    gate_up = dot(field, w_gu[...])
    gate_pre, up_pre = gate_up[:, :hid], gate_up[:, hid:]
    sigmoid = jax.nn.sigmoid(gate_pre)
    silu = gate_pre * sigmoid
    inner = (silu * up_pre).astype(BF16)
    inner_ref[...] = inner
    gated_ref[...] = (gate * inner.astype(F32)).astype(BF16)
    factor_ref[:, :hid] = gate * up_pre * sigmoid * (1.0 + gate_pre * (1.0 - sigmoid))
    factor_ref[:, hid:] = gate * silu


def expert_in(place, fields, ids, w_router, w_gu, length, experts):
    width, hid = fields[0].shape[1], w_gu.shape[1] // 2
    ins = (place, *fields, *ids, w_router, w_gu)
    outs = (
        jax.ShapeDtypeStruct((2 * length, hid), BF16),
        jax.ShapeDtypeStruct((2 * length, hid), BF16),
        jax.ShapeDtypeStruct((2 * length, 2 * hid), F32),
    )
    specs = [whole(a) for a in ins]
    specs[0] = pl.BlockSpec(memory_space=pltpu.SMEM)
    for i in (3, 4):
        specs[i] = pl.BlockSpec((IDS, length), lambda i: (length // IDS, 0))
    return pl.pallas_call(
        functools.partial(expert_in_kernel, length, experts),
        grid=(1,),
        in_specs=specs,
        out_specs=tuple(whole(a) for a in outs),
        out_shape=outs,
        compiler_params=params(28),
        cost_estimate=cost(8 * length * width * hid, ins + outs),
        name="expert_in",
    )(*ins)


def expert_back_kernel(length, place, c0, c1, inner, factor, w_gu, w_dn, out0, out1, grad_ref):
    hid = w_dn.shape[0]
    rep = place[0]
    grad_inner = dot_nt(joined((c0, c1)), w_dn[...])
    grad_gate = jnp.sum(inner[...].astype(F32) * grad_inner, axis=-1, keepdims=True)
    grad_ref[:, :hid] = (grad_inner * factor[:, :hid]).astype(BF16)
    grad_ref[:, hid:] = (grad_inner * factor[:, hid:]).astype(BF16)
    partial = dot_nt(grad_ref[...], w_gu[...]).astype(BF16)
    grad_gate = jnp.broadcast_to(grad_gate, (2 * length, 128)).T
    extra = out0.shape[0] - length
    row = lax.broadcasted_iota(jnp.int32, (extra, length), 0)
    for i, out in enumerate((out0, out1)):
        out[:length] = partial[i * length : (i + 1) * length]
        whole_grad = grad_gate[:extra, i * length : (i + 1) * length]
        high = whole_grad.astype(BF16).astype(F32)
        parts = jnp.where(row == 2 * rep, high, jnp.where(row == 2 * rep + 1, whole_grad - high, 0.0))
        out[length:, :length] = parts.astype(BF16)
        out[length:, length:] = jnp.zeros((extra, out.shape[1] - length), BF16)


def expert_back(place, grads, inner, factor, w_gu, w_dn, length, reps):
    width, hid = w_dn.shape[1], w_dn.shape[0]
    ins = (place, *grads, inner, factor, w_gu, w_dn)
    tall = length + max(2 * reps, IDS)
    outs = (
        jax.ShapeDtypeStruct((tall, width), BF16),
        jax.ShapeDtypeStruct((tall, width), BF16),
        jax.ShapeDtypeStruct((2 * length, 2 * hid), BF16),
    )
    specs = [whole(a) for a in ins]
    specs[0] = pl.BlockSpec(memory_space=pltpu.SMEM)
    return pl.pallas_call(
        functools.partial(expert_back_kernel, length),
        grid=(1,),
        in_specs=specs,
        out_specs=tuple(whole(a) for a in outs),
        out_shape=outs,
        compiler_params=params(30),
        cost_estimate=cost(12 * length * width * hid, ins + outs),
        name="expert_back",
    )(*ins)


def mix_out_kernel(length, mixed, w_out, out0, out1):
    both = dot(mixed[...], w_out[...]).astype(BF16)
    out0[...] = both[:length]
    out1[...] = both[length:]


def mix_out(mixed, w_out, length, name):
    out = jax.ShapeDtypeStruct((length, w_out.shape[1]), BF16)
    ins = (mixed, w_out)
    return pl.pallas_call(
        functools.partial(mix_out_kernel, length),
        grid=(1,),
        in_specs=[whole(a) for a in ins],
        out_specs=(whole(out), whole(out)),
        out_shape=(out, out),
        compiler_params=params(16),
        cost_estimate=cost(4 * length * w_out.size, (*ins, out, out)),
        name=name,
    )(*ins)


def joined(refs):
    return jnp.concatenate([ref[...] for ref in refs])


def weight_grad_kernel(count, *refs):
    refs[-1][...] = dot_tn(joined(refs[:count]), joined(refs[count:-1])).astype(BF16)


def weight_grad(left, right, tile, wide, name):
    out = jax.ShapeDtypeStruct((left[0].shape[1], right[0].shape[1]), BF16)
    ins = (*left, *right)
    rows_step, cols_step = int(tile < out.shape[0]), int(wide < out.shape[1])
    return pl.pallas_call(
        functools.partial(weight_grad_kernel, len(left)),
        grid=(out.shape[0] // tile if rows_step else out.shape[1] // wide,),
        in_specs=[pl.BlockSpec((a.shape[0], tile), lambda i: (0, i * rows_step)) for a in left]
        + [pl.BlockSpec((a.shape[0], wide), lambda i: (0, i * cols_step)) for a in right],
        out_specs=pl.BlockSpec((tile, wide), lambda i: (i * rows_step, i * cols_step)),
        out_shape=out,
        compiler_params=params(),
        cost_estimate=cost(2 * left[0].shape[0] * len(left) * out.size, (*ins, out)),
        name=name,
    )(*ins)


def attention_grad_kernel(count, out_rows, *refs):
    left, right, (extra, weight, out, gain) = refs[:count], refs[count:-4], refs[-4:]
    tile, columns = left[0].shape[1], right[0].shape[1]
    cols = out.shape[1] - columns
    grad = dot_tn(joined(left), joined(right))
    out[:, :columns] = grad.astype(BF16)
    gain[...] = jnp.sum(grad * weight[...].astype(F32), axis=-1, keepdims=True)
    chunks = extra.shape[1] // cols
    for k in range(tile // out_rows):
        place = pl.program_id(0) * (tile // out_rows) + k
        row = pl.multiple_of(lax.div(place, chunks) * out_rows, out_rows)
        lane = pl.multiple_of(lax.rem(place, chunks) * cols, cols)
        out[k * out_rows : (k + 1) * out_rows, columns:] = extra[pl.ds(row, out_rows), pl.ds(lane, cols)]


def attention_grad(left, right, extra, weight, length, shards, tile):
    width, columns, cols = left[0].shape[1], right[0].shape[1], extra.shape[0]
    outs = (jax.ShapeDtypeStruct((width, columns + cols), BF16), jax.ShapeDtypeStruct((width, 1), F32))
    return pl.pallas_call(
        functools.partial(attention_grad_kernel, len(left), cols // shards),
        grid=(width // tile,),
        in_specs=[pl.BlockSpec((length, tile), lambda i: (0, i)) for _ in left]
        + [pl.BlockSpec(a.shape, lambda i: (0, 0)) for a in (*right, extra)]
        + [pl.BlockSpec((tile, columns), lambda i: (i, 0))],
        out_specs=(
            pl.BlockSpec((tile, columns + cols), lambda i: (i, 0)),
            pl.BlockSpec((tile, 1), lambda i: (i, 0)),
        ),
        out_shape=outs,
        compiler_params=params(),
        cost_estimate=cost(2 * length * len(left) * width * columns, (*left, *right, *outs)),
        name="attention_grad",
    )(*left, *right, extra, weight)


def own_columns_kernel(place, query, key, value, out):
    cols = query.shape[1]
    for i, ref in enumerate((query, key, value)):
        out[:, i * cols : (i + 1) * cols] = ref[...]


def own_columns(weights, rep, cols):
    rows = weights[0].shape[0]
    return pl.pallas_call(
        own_columns_kernel,
        grid_spec=pltpu.PrefetchScalarGridSpec(
            num_scalar_prefetch=1,
            grid=(1,),
            in_specs=[pl.BlockSpec((rows, cols), lambda i, place: (0, place[0]))] * len(weights),
            out_specs=pl.BlockSpec((rows, len(weights) * cols), lambda i, place: (0, 0)),
        ),
        out_shape=jax.ShapeDtypeStruct((rows, len(weights) * cols), BF16),
        compiler_params=params(),
        name="own_columns",
    )(rep.reshape(1), *weights)


def own_expert_kernel(place, gate, up, down, gu, dn):
    step = pl.program_id(0)
    sub = gate.shape[2]
    for i, ref in enumerate((gate, up)):
        gu[:, pl.ds(pl.multiple_of(i * gu.shape[1] // 2 + step * sub, 128), sub)] = ref[0]

    @pl.when(step == 0)
    def _():
        dn[...] = down[0]


def own_expert(gate, up, down, table, parts, sub):
    _, rows, wide = gate.shape
    width = down.shape[2]
    hid = wide // parts
    spec = pl.BlockSpec((1, rows, sub), lambda z, place: (place[0], 0, z * parts + place[1]))
    return pl.pallas_call(
        own_expert_kernel,
        grid_spec=pltpu.PrefetchScalarGridSpec(
            num_scalar_prefetch=1,
            grid=(hid // sub,),
            in_specs=[spec, spec, pl.BlockSpec((1, sub, width), lambda z, place: (place[0], place[1], 0))],
            out_specs=(
                pl.BlockSpec((rows, 2 * hid), lambda z, place: (0, 0)),
                pl.BlockSpec((sub, width), lambda z, place: (0, 0)),
            ),
        ),
        out_shape=(jax.ShapeDtypeStruct((rows, 2 * hid), BF16), jax.ShapeDtypeStruct((sub, width), BF16)),
        compiler_params=params(),
        name="own_expert",
    )(table, gate, up, down)


def place_out_kernel(rows, place, *refs):
    out = refs[-1]
    cols = refs[0].shape[1]
    for m, source in enumerate(refs[:-1]):
        row = pl.multiple_of(place[m] * rows, rows)
        for c in range(out.shape[1] // cols):
            out[pl.ds(row, rows), c * cols : (c + 1) * cols] = source[c * rows : (c + 1) * rows].astype(F32)


def place_out(pieces, table, rows, shape):
    return pl.pallas_call(
        functools.partial(place_out_kernel, rows),
        grid_spec=pltpu.PrefetchScalarGridSpec(
            num_scalar_prefetch=1,
            grid=(1,),
            in_specs=[pl.BlockSpec((a.shape[0], a.shape[1] // 4), lambda i, place: (0, 3)) for a in pieces],
            out_specs=pl.BlockSpec(shape, lambda i, place: (0, 0)),
        ),
        out_shape=jax.ShapeDtypeStruct(shape, F32),
        compiler_params=params(),
        cost_estimate=cost(0, [jax.ShapeDtypeStruct((2, *shape), F32)]),
        name="place_out",
    )(table, *pieces)


def place_units_kernel(parts, shards, place, *refs):
    sources, (out_gate, out_up) = refs[:-2], refs[-2:]
    sub = sources[0].shape[1] // 2 // shards
    for m, source in enumerate(sources):
        expert, part = place[2 * m], place[2 * m + 1]
        for i, out in enumerate((out_gate, out_up)):
            for z in range(shards):
                lane = pl.multiple_of((z * parts + part) * sub, 128)
                at = (i * shards + z) * sub
                out[expert, :, pl.ds(lane, sub)] = source[:, at : at + sub].astype(F32)


def place_units(pieces, table, parts, shards, shape, tile):
    wide = pieces[0].shape[1]
    return pl.pallas_call(
        functools.partial(place_units_kernel, parts, shards),
        grid_spec=pltpu.PrefetchScalarGridSpec(
            num_scalar_prefetch=1,
            grid=(shape[1] // tile,),
            in_specs=[pl.BlockSpec((tile, wide), lambda t, place: (t, 0)) for _ in pieces],
            out_specs=[pl.BlockSpec((shape[0], tile, shape[2]), lambda t, place: (0, t, 0))] * 2,
        ),
        out_shape=[jax.ShapeDtypeStruct(shape, F32)] * 2,
        compiler_params=params(),
        cost_estimate=cost(0, [jax.ShapeDtypeStruct((4, *shape), F32)]),
        name="place_units",
    )(table, *pieces)


def place_down_kernel(place, *refs):
    sub = refs[0].shape[0]
    for m, source in enumerate(refs[:-1]):
        refs[-1][pl.ds(pl.multiple_of(place[m] * sub, sub), sub), :] = source[...].astype(F32)


def place_down(pieces, table, rows, sub, width):
    wide = pieces[0].shape[1]
    return pl.pallas_call(
        place_down_kernel,
        grid_spec=pltpu.PrefetchScalarGridSpec(
            num_scalar_prefetch=1,
            grid=(width // wide,),
            in_specs=[pl.BlockSpec((sub, wide), lambda c, place: (rows // sub + c, 0)) for _ in pieces],
            out_specs=pl.BlockSpec((len(pieces) * sub, wide), lambda c, place: (0, c)),
        ),
        out_shape=jax.ShapeDtypeStruct((len(pieces) * sub, width), F32),
        compiler_params=params(),
        cost_estimate=cost(0, [jax.ShapeDtypeStruct((len(pieces) * sub, 2 * width), F32)]),
        name="place_down",
    )(table, *pieces)


def place_heads_kernel(place, *refs):
    sources, outs = refs[:-3], refs[-3:]
    cols = sources[0].shape[1] // 4
    for m, source in enumerate(sources):
        lane = pl.multiple_of(place[m] * cols, cols)
        for i, out in enumerate(outs):
            out[:, pl.ds(lane, cols)] = source[:, i * cols : (i + 1) * cols].astype(F32)


def place_heads(pieces, table, tile):
    rows, wide = pieces[0].shape
    width = len(pieces) * wide // 4
    return pl.pallas_call(
        place_heads_kernel,
        grid_spec=pltpu.PrefetchScalarGridSpec(
            num_scalar_prefetch=1,
            grid=(rows // tile,),
            in_specs=[pl.BlockSpec((tile, wide), lambda t, place: (t, 0)) for _ in pieces],
            out_specs=[pl.BlockSpec((tile, width), lambda t, place: (t, 0))] * 3,
        ),
        out_shape=[jax.ShapeDtypeStruct((rows, width), F32)] * 3,
        compiler_params=params(),
        cost_estimate=cost(0, [jax.ShapeDtypeStruct((6, rows, width), F32)]),
        name="place_heads",
    )(table, *pieces)


def place_hidden_kernel(parts, shards, sub, source, *outs):
    hid = shards * sub
    for i, out in enumerate(outs):
        for z in range(shards):
            for p in range(parts):
                lane = i * hid + z * sub
                out[0, :, (z * parts + p) * sub : (z * parts + p + 1) * sub] = source[
                    p, :, lane : lane + sub
                ].astype(F32)


def place_hidden(source, experts, shards, tile):
    reps, rows, wide = source.shape
    parts = reps // experts
    full = parts * wide // 2
    return pl.pallas_call(
        functools.partial(place_hidden_kernel, parts, shards, wide // 2 // shards),
        grid=(experts, rows // tile),
        in_specs=[pl.BlockSpec((parts, tile, wide), lambda e, t: (e, t, 0))],
        out_specs=[pl.BlockSpec((1, tile, full), lambda e, t: (e, t, 0)) for _ in range(2)],
        out_shape=[jax.ShapeDtypeStruct((experts, rows, full), F32) for _ in range(2)],
        compiler_params=params(),
        name="place_hidden",
    )(source)


class Ring:
    def __init__(self, reps):
        self.reps = reps
        self.links = [m for m in range(2, reps, 2)]
        self.links.sort(key=lambda m: (bin(m).count("1"), m))

    def swap(self, piece, bit):
        return lax.ppermute(piece, "rep", [(i, i ^ bit) for i in range(self.reps)])

    @staticmethod
    def hops(m):
        return 1 << (m.bit_length() - 1), m & -m

    def gather(self, block):
        half = max(block.shape[0] // 32 * 16, 8)
        held = {0: block}
        for m in self.links:
            high, low = self.hops(m)
            if high == low:
                held[m] = self.swap(block, m)
            else:
                held[m] = jnp.concatenate(
                    [self.swap(held[m ^ high][:half], high), self.swap(held[m ^ low][half:], low)]
                )
        for m in [0] + self.links:
            held[m ^ 1] = self.swap(held[m], 1)
        return [held[m] for m in range(self.reps)]

    def summing(self):
        return RingSum(self)


class RingSum:
    def __init__(self, ring):
        self.ring = ring
        self.held = {}
        self.core = {}

    def feed(self, m, own, other):
        self.half = max(own.shape[0] // 32 * 16, 8)
        got = self.core[m] = self.ring.swap(other, 1)
        parts = (slice(None, self.half), slice(self.half, None))
        self.held[m] = [own[part].astype(F32) + got[part].astype(F32) for part in parts]

    def far(self, *gate):
        events = []
        for m in reversed(self.ring.links):
            high, low = self.ring.hops(m)
            if high == low:
                continue
            for part, bit in ((0, high), (1, low)):
                piece = self.held[m][part].astype(BF16)
                got = self.ring.swap(after(piece, *gate) if gate else piece, bit)
                self.held[m ^ bit][part] = self.held[m ^ bit][part] + got.astype(F32)
                events.append(got)
        return events

    def near(self, m, *gate):
        piece = jnp.concatenate(self.held[m]).astype(BF16)
        got = self.ring.swap(after(piece, *gate) if gate else piece, m)
        for part, rows in ((0, slice(None, self.half)), (1, slice(self.half, None))):
            self.held[0][part] = self.held[0][part] + got[rows].astype(F32)
        return got

    def total(self):
        return jnp.concatenate(self.held[0])


def make_body(reps, shards):
    ring = Ring(reps)

    def body(
        tokens, cotangent, segment_ids, expert_ids, norm_gain, w_query, w_key, w_value, w_output,
        query_gain, key_gain, ffn_norm_gain, w_router, w_gate, w_up, w_down,
    ):
        length, width = tokens.shape
        head_size = query_gain.shape[0]
        head_count = width // head_size
        experts = w_gate.shape[0]
        hidden_total = w_gate.shape[2]
        heads = head_count // reps
        cols = heads * head_size
        parts = reps // experts
        sub = hidden_total // shards // parts
        hid = sub * shards
        rows = width // shards
        total = reps * length
        per_plane = reps // shards
        out_rows = cols // shards
        score_scale = head_size ** (-0.5)

        rep = lax.axis_index("rep")
        expert, part = lax.div(rep, parts), lax.rem(rep, parts)

        def hidden_columns(weight):
            own = lax.dynamic_slice(weight, (expert, 0, 0), (1, rows, hidden_total))
            own = own.reshape(rows, shards, parts, sub)
            return lax.dynamic_slice(own, (0, 0, part, 0), (rows, shards, 1, sub)).reshape(rows, hid)

        there = [
            (src_rep * shards + src, (src * per_plane + src_rep % per_plane) * shards + src_rep // per_plane)
            for src_rep in range(reps)
            for src in range(shards)
        ]
        back = [(target, source) for source, target in there]
        first_row = lax.rem(rep, per_plane) * cols + lax.div(rep, per_plane) * out_rows
        out_piece = lax.dynamic_slice(w_output, (first_row, 0), (out_rows, width))
        out_piece = lax.ppermute(out_piece, ("rep", "shard"), there)
        w_qkv = gather(own_columns((w_query, w_key, w_value), rep, cols), "shard")

        stream = tokens.astype(F32)
        live = (segment_ids > 0).astype(F32)[:, None]
        first_scale = rms_scale(stream)
        normed = (stream * first_scale * norm_gain).astype(BF16)
        ids = jnp.concatenate([segment_ids[None], expert_ids.T]).astype(BF16)
        ids = jnp.pad(ids, ((0, IDS - ids.shape[0]), (0, width - length)))
        blocks = ring.gather(jnp.concatenate([normed, ids]))
        pairs = range(0, reps, 2)

        unit = jnp.stack([expert, part]).astype(jnp.int32)
        if sub % 128 == 0:
            own_gu, own_dn = own_expert(w_gate, w_up, w_down, unit, parts, sub)
        else:
            own_gu = jnp.concatenate([hidden_columns(w_gate), hidden_columns(w_up)], 1)
            own_dn = lax.dynamic_slice(w_down, (expert, part * sub, 0), (1, sub, width))[0]
        grad_moe_own = jnp.where(segment_ids[:, None] > 0, cotangent, jnp.zeros_like(cotangent))
        grad_moe = ring.gather(after(grad_moe_own, blocks[2], blocks[4]))
        arrived = [grad_moe[m] for m in ring.links]
        w_out = gather(after(out_piece, w_qkv, grad_moe[2], grad_moe[4]), "shard")
        w_gu = gather(after(own_gu, w_out), "shard")

        cosine, sine = rotary_tables(length, head_size)
        cosine = jnp.concatenate([cosine, cosine], axis=1)
        sine = jnp.concatenate([-sine, sine], axis=1)
        gains = after(jnp.stack([query_gain, key_gain]), own_gu, own_dn, *arrived)
        order = sorted(pairs, key=lambda m: (-bin(m).count("1"), m))
        singles = [m for m in ring.links if m & (m - 1) == 0]
        attended = {
            m: attend(blocks[m : m + 2], w_qkv, gains, cosine, sine, length, score_scale) for m in order
        }
        summed = ring.summing()
        for m in order:
            mixed = after(attended[m][1], attended[order[-1]][1]) if m != order[-1] else attended[m][1]
            summed.feed(m, *mix_out(mixed, w_out, length, "mix_out"))
        summed.far()
        near = [summed.near(m) for m in singles]
        attention_out = summed.total()
        w_dn = gather(after(own_dn, *near), "shard")

        hidden = stream + live * attention_out
        second_scale = rms_scale(hidden)
        normed_ffn = (hidden * second_scale * ffn_norm_gain).astype(BF16)
        ffn_all = ring.gather(normed_ffn)

        place = jnp.stack([rep, expert]).astype(jnp.int32)
        router = jnp.pad(w_router, ((0, 0), (0, 128 - experts)))
        entered = {m: expert_in(place, ffn_all[m : m + 2], blocks[m : m + 2], router, w_gu, length, experts) for m in order}
        inner_gated = [entered[m][0] for m in pairs]
        part_dn = weight_grad(inner_gated, grad_moe, hid, 512, "down_grad")
        sum_dn = scatter_sum(part_dn, "shard")
        stepped = {}
        summed = ring.summing()
        for i, m in enumerate(order):
            gate = [summed.core[order[i - 2]]] if i >= 2 else [part_dn]
            if i == len(order) - 1:
                gate += summed.far()
            stepped[m] = expert_back(
                after(place, *gate), grad_moe[m : m + 2], entered[m][1], entered[m][2], w_gu, w_dn, length, reps
            )
            summed.feed(m, *stepped[m][:2])
        near = [summed.near(m) for m in singles]
        grad_gu = [stepped[m][2] for m in pairs]
        grad_gu[0] = after(grad_gu[0], summed.core[order[-1]])
        part_gu = weight_grad(ffn_all, grad_gu, 256, 2 * hid, "up_grad")
        sum_gu = scatter_sum(after(part_gu, sum_dn, *near), "shard")
        grad_ffn = summed.total()
        grad_ffn = after(grad_ffn, part_gu)
        grad_gate = grad_ffn[length : length + 2 * reps, :length]
        grad_gate = jnp.sum(grad_gate.reshape(experts, parts * 2, length), axis=1)
        grad_ffn = grad_ffn[:length]

        logits = dot(normed_ffn, w_router)
        shifted = jnp.exp(logits - jnp.max(logits, axis=-1, keepdims=True))
        chances = shifted / jnp.sum(shifted, axis=-1, keepdims=True)
        picked = jnp.any(expert_ids[:, :, None] == jnp.arange(experts), axis=1)
        grad_chances = jnp.where(picked, grad_gate.T, 0.0)
        grad_logits = chances * (
            grad_chances - jnp.sum(chances * grad_chances, axis=-1, keepdims=True)
        )
        grad_logits = grad_logits.astype(BF16)
        grad_router = dot_tn(normed_ffn, grad_logits)

        grad_result = cotangent.astype(F32)
        grad_normed_ffn = grad_ffn + dot_nt(grad_logits, w_router)
        grad_ffn_gain = jnp.sum(grad_normed_ffn * hidden * second_scale, axis=0)
        grad_hidden = grad_result + norm_back(hidden, second_scale, ffn_norm_gain, grad_normed_ffn)
        grad_attention = ring.gather((live * grad_hidden).astype(BF16))

        moe_sum = ring.summing()
        for m in order:
            moe_sum.feed(m, *mix_out(after(entered[m][0], grad_attention[0]), w_dn, length, "mix_back"))
        backs = {}
        summed = ring.summing()
        backward = list(reversed(order))
        for i, m in enumerate(backward):
            gate = [moe_sum.core[order[min(i, len(order) - 1)]]]
            if i == len(order) - 1:
                gate += moe_sum.far()
            backs[m] = attend_back(
                grad_attention[m : m + 2], blocks[m : m + 2], attended[m][0],
                w_qkv, w_out, after(gains, *gate), cosine, sine, length, score_scale,
            )
            summed.feed(m, *backs[m][:2])
        mixed = [attended[m][1] for m in pairs]
        part_out = weight_grad(mixed, grad_attention, cols, 1024, "out_grad")
        grad_qkv = [backs[m][2] for m in pairs]
        grad_qkv[0] = after(grad_qkv[0], summed.core[backward[-1]])
        part_attention, grad_norm_gain = attention_grad(blocks, grad_qkv, part_out, w_qkv, length, shards, 256)
        grad_norm_gain = grad_norm_gain.reshape(-1) / norm_gain
        moe_last = [moe_sum.near(m) for m in singles]
        far = summed.far(*moe_last)
        normed_last = [summed.near(m) for m in singles]
        moe_out = moe_sum.total()
        grad_normed = summed.total()
        grad_gains = sum(backs[m][3] for m in pairs)
        grad_qgain, grad_kgain = grad_gains[0], grad_gains[1]
        input_grad = grad_hidden + norm_back(stream, first_scale, norm_gain, grad_normed)

        result = hidden + live * moe_out

        sum_attention = scatter_sum(after(part_attention, sum_gu, *moe_last), "shard")
        chops = [sum_dn[:, c : c + 2 * hid] for c in range(0, width, 2 * hid)]
        pieces = ring.gather(after(jnp.concatenate([sum_gu] + chops), *far))

        device = rep ^ jnp.arange(reps, dtype=jnp.int32)
        shapes = ((experts, rows, hidden_total),) * 2 + ((experts, parts * sub, width),)
        all_dn = place_down(pieces, device, rows, sub, width).reshape(shapes[2])
        if sub % 128 == 0:
            units = jnp.stack([lax.div(device, parts), lax.rem(device, parts)], axis=1).reshape(-1)
            all_gate, all_up = place_units(pieces, units, parts, shards, shapes[0], 64)
        else:
            all_gate, all_up = place_hidden(lax.all_gather(sum_gu, "rep"), experts, shards, rows // 4)
        sum_attention = after(sum_attention, *[pieces[m] for m in ring.links], *normed_last)
        sum_out = lax.ppermute(sum_attention[:, 3 * cols :], ("rep", "shard"), back)
        pieces = ring.gather(jnp.concatenate([sum_attention[:, : 3 * cols], sum_out], axis=1))
        all_qkv = place_heads(pieces, device, 64)
        row_block = lax.rem(device, per_plane) * shards + lax.div(device, per_plane)
        all_out = place_out(pieces, row_block, out_rows, (rows, width))

        square_sums = jnp.stack(
            [
                jnp.sum(live * stream * stream),
                jnp.sum(live * hidden * hidden),
                jnp.sum(live * result * result),
                jnp.sum(live),
            ]
        )
        small = [grad_norm_gain, grad_ffn_gain, grad_qgain, grad_kgain, grad_router.T.reshape(-1)]
        small.append(jnp.pad(square_sums, (0, 124)))
        small = total_over_all(
            jnp.concatenate([part.reshape(-1, 128) for part in small]), (("rep", reps), ("shard", shards))
        ).reshape(-1)
        norm_sum, ffn_sum = small[:width], small[width : 2 * width]
        small = small[2 * width :]
        qgain_sum, kgain_sum = small[:head_size], small[head_size : 2 * head_size]
        router_sum = small[2 * head_size : 2 * head_size + experts * width].reshape(experts, width).T
        stat_sum = small[2 * head_size + experts * width :]
        residual_rms = jnp.sqrt(stat_sum[:3] / (stat_sum[3] * width))
        return (
            result.astype(BF16), input_grad.astype(BF16), norm_sum,
            all_qkv[0], all_qkv[1], all_qkv[2], all_out,
            qgain_sum, kgain_sum, ffn_sum, router_sum,
            all_gate, all_up, all_dn, residual_rms,
        )

    return body


def solution(mesh):
    by_token, by_shard, inner_shard = P(("rep", "shard"), None), P("shard", None), P(None, "shard", None)
    in_specs = (
        by_token, by_token, P(("rep", "shard")), by_token, P(),
        by_shard, by_shard, by_shard, by_shard, P(), P(), P(), P(),
        inner_shard, inner_shard, inner_shard,
    )
    out_specs = (
        by_token, by_token, P(), by_shard, by_shard, by_shard, by_shard, P(), P(), P(), P(),
        inner_shard, inner_shard, inner_shard, P(),
    )
    body = make_body(mesh.shape["rep"], mesh.shape["shard"])
    return jax.shard_map(body, mesh=mesh, in_specs=in_specs, out_specs=out_specs, check_vma=False)
```

time: 1320 us -> 714 us (0.54)
  waiting for transfers between devices: 778 us -> 288 us
  Pallas kernels: 0 us -> 168 us
  matrix products: 152 us -> 4.04 us
  local copies, waits for them, and re-layouts: 233 us -> 115 us
  blocking collectives: 73.7 us -> 0 us
  starting transfers between devices: 3.67 us -> 69.4 us
    all_gather x10 -> x4, waiting for transfers between devices: 372 us -> 7.35 us  [gather(): return lax.all_gather(piece, axis, axis=dim, tiled=True)]
    reduce_scatter x8 -> x3, waiting for transfers between devices: 357 us -> 0.02 us  [scatter_sum(): return lax.psum_scatter(whole, axis, scatter_dimension=0, tiled=True)]
    ppermute x2 -> x87, waiting for transfers between devices: 0.01 us -> 280 us  [the longest x80 258 us: swap(): return lax.ppermute(piece, 'rep', [(i, i ^ bit) for i in range(self.reps)])]
    pallas_call x0 -> x34, Pallas kernels: none -> 168 us  [the longest x4 31.7 us: attend_back(): pl.pallas_call(functools.partial(attend_back_kernel, length, score_scale)...]
    ppermute x2 -> x87, starting transfers between devices: 2.27 us -> 68.1 us  [the longest x80 63.3 us: swap(): return lax.ppermute(piece, 'rep', [(i, i ^ bit) for i in range(self.reps)])]
    slice x9 -> x22, local copies, waits for them, and re-layouts: 71.4 us -> 16.8 us  [the longest x6 7.85 us: gather(): held[m ^ high][:half]]
    all_gather x2 -> x0, waiting for transfers between devices: 47.7 us -> none  [the longest x1 46.8 us: body(): all_gu = lax.all_gather(sum_gu, 'rep').astype(F32)]
    dot_general x5 -> x1, matrix products: 49.4 us -> 3.39 us  [dot_nt(): lax.dot_general(left, right, (((1,), (1,)), ((), ())), preferred_element_...]
  transfers between devices with their start and end apart: 22 -> 94, of which waited for: 17 -> 30; matrix products, arithmetic and copies ran while one was open for 24% -> 12% of each run, Pallas kernels for 0% -> 21%
where the time goes in v2:
time: 714 us; the launch traced here: 708 us
  waiting for transfers between devices  288 us (40%)
  Pallas kernels  168 us (24%)
  local copies, waits for them, and re-layouts  115 us (16%)
  starting transfers between devices  69.4 us (10%)
  other arithmetic  47.3 us (7%)
  between operations  16.9 us (2%)
    ppermute x80, waiting for transfers between devices, swap(): return lax.ppermute(piece, 'rep', [(i, i ^ bit) for i in range(self.reps)])  258 us
    unnamed x331, local copies, waits for them, and re-layouts  88.7 us
    ppermute x80, starting transfers between devices, swap(): return lax.ppermute(piece, 'rep', [(i, i ^ bit) for i in range(self.reps)])  63.3 us
    pallas_call x4, Pallas kernels, attend_back(): pl.pallas_call(functools.partial(attend_back_kernel, length, score_scale)...  31.7 us
    pallas_call x3, Pallas kernels, weight_grad(): pl.pallas_call(functools.partial(weight_grad_kernel, len(left)), grid=(ou...  22.5 us
    ppermute x5, waiting for transfers between devices, total_over_all(): lax.ppermute(value, axis, [(i, i ^ bit) for i in range(size)])  22.2 us
    pallas_call x4, Pallas kernels, expert_back(): pl.pallas_call(functools.partial(expert_back_kernel, length), grid=(1,),...  21.6 us
    pallas_call x4, Pallas kernels, attend(): pl.pallas_call(functools.partial(attend_kernel, length, score_scale), gri...  21 us
  transfers between devices with their start and end apart: 94, of which 30 were waited for; matrix products, arithmetic and copies ran while one was open for 12% of the time, Pallas kernels for 21%

profile of v2, /device:TPU:0, one launch (start us, length us, event | category | flops | bytes accessed | tf_op | source)
XLA Modules:
  0.0 707.9 jit_solution(5564382953053968856)
XLA Ops:
  22.2 21.4 %collective-permute-done.1.blk0.ids0.refs_2_ = bf16[272,2048]{1,0:T(8,128)(2,1)} collective-permute-done((bf16[272,2048]{1,0:T(8,128)(2,1)S(1)}, bf16[272,2048]{1,0:T(8,128)(2,1)}, u32[]{:S(2)}, u32[]{:S(2)}) %collective-permute-start.1) | collective-permute-done | bytes 1114144 | tf_op jit(solution)/shard_map/ppermute | solution.py:579
  52.4 32.8 %collective-permute-done.11 = bf16[128,2048]{1,0:T(8,128)(2,1)} collective-permute-done((bf16[128,2048]{1,0:T(8,128)(2,1)}, bf16[128,2048]{1,0:T(8,128)(2,1)}, u32[]{:S(2)}, u32[]{:S(2)}) %collective-permute-start.11) | collective-permute-done | bytes 524320 | tf_op jit(solution)/shard_map/ppermute | solution.py:579
  87.2 7.3 %all-gather.5.cloned.1.call-done.w_qkv.refs_13_ = bf16[2048,768]{1,0:T(8,128)(2,1)} async-done(((bf16[512,768]{1,0:T(8,128)(2,1)}), bf16[2048,768]{1,0:T(8,128)(2,1)}) %all-gather.5.cloned.1.call-update) | async-done | bytes 3145744 | tf_op jit(solution)/shard_map/all_gather | solution.py:68
  124.5 5.4 attend.6
  140.8 5.4 attend.5
  156.9 5.2 attend.7
  168.6 10.8 %collective-permute-done.19 = bf16[128,2048]{1,0:T(8,128)(2,1)S(1)} collective-permute-done((bf16[128,2048]{1,0:T(8,128)(2,1)S(1)}, bf16[128,2048]{1,0:T(8,128)(2,1)S(1)}, u32[]{:S(2)}, u32[]{:S(2)}) %collective-permute-start.19) | collective-permute-done | bytes 524320 | tf_op jit(solution)/shard_map/ppermute | solution.py:579
  180.5 20.7 %collective-permute-done.16 = bf16[256,2048]{1,0:T(8,128)(2,1)S(1)} collective-permute-done((bf16[256,2048]{1,0:T(8,128)(2,1)S(1)}, bf16[256,2048]{1,0:T(8,128)(2,1)S(1)}, u32[]{:S(2)}, u32[]{:S(2)}) %collective-permute-start.16) | collective-permute-done | bytes 1048608 | tf_op jit(solution)/shard_map/ppermute | solution.py:579
  207.8 21.9 %collective-permute-done.22.b0.refs_2_ = bf16[256,2048]{1,0:T(8,128)(2,1)S(1)} collective-permute-done((bf16[256,2048]{1,0:T(8,128)(2,1)S(1)}, bf16[256,2048]{1,0:T(8,128)(2,1)S(1)}, u32[]{:S(2)}, u32[]{:S(2)}) %collective-permute-start.22) | collective-permute-done | bytes 1048608 | tf_op jit(solution)/shard_map/ppermute | solution.py:579
  234.9 7.0 collective-permute-done.26
  281.5 7.1 down_grad.1
  297.1 6.1 expert_back.5
  312.3 5.2 expert_back.4
  327.3 6.2 collective-permute-done.35
  346.9 12.2 %up_grad.1 = bf16[2048,1024]{1,0:T(8,128)(2,1)S(1)} custom-call(bf16[256,2048]{1,0:T(8,128)(2,1)S(1)} %multiply_convert_fusion.1.b0.refs_0_, bf16[256,2048]{1,0:T(8,128)(2,1)} %collective-permute-done.21.b1.refs_1_, bf16[256,2048]{1,0:T(8,128)(2,1)S(1)} %copy-done.19, bf16[256,2048]{1,0:T(8,128)(2,1)S(1)} %copy-done.39, bf16[256,2048]{1,0:T(8,128)(2,1)S(1)} %copy-done.22, ...), custom_call_target="tpu_custom_call" | custom-call | flops 8589934592 | bytes 16777216 | tf_op jit(solution)/shard_map/up_grad/pallas_call | solution.py:339
  361.1 9.8 %collective-permute-done.40 = bf16[272,2048]{1,0:T(8,128)(2,1)} collective-permute-done((bf16[272,2048]{1,0:T(8,128)(2,1)}, bf16[272,2048]{1,0:T(8,128)(2,1)}, u32[]{:S(2)}, u32[]{:S(2)}) %collective-permute-start.40) | collective-permute-done | bytes 1114144 | tf_op jit(solution)/shard_map/ppermute | solution.py:579
  389.6 18.6 %collective-permute-done.51.da0.refs_6_ = bf16[256,2048]{1,0:T(8,128)(2,1)S(1)} collective-permute-done((bf16[256,2048]{1,0:T(8,128)(2,1)S(1)}, bf16[256,2048]{1,0:T(8,128)(2,1)S(1)}, u32[]{:S(2)}, u32[]{:S(2)}) %collective-permute-start.51) | collective-permute-done | bytes 1048608 | tf_op jit(solution)/shard_map/ppermute | solution.py:579
  413.9 7.6 %attend_back.4 = (bf16[256,2048]{1,0:T(8,128)(2,1)S(1)}, bf16[256,2048]{1,0:T(8,128)(2,1)S(1)}, bf16[512,768]{1,0:T(8,128)(2,1)S(1)}, f32[8,128]{1,0:T(8,128)S(1)}) custom-call(bf16[256,2048]{1,0:T(8,128)(2,1)S(1)} %get-tuple-element.227.da0.refs_4_, bf16[256,2048]{1,0:T(8,128)(2,1)S(1)} %collective-permute-done.49.da1.refs_5_, ...), custom_call_target="tpu_custom_call" | custom-call | flops 3221225472 | bytes 13243392 | tf_op jit(solution)/shard_map/attend_back/pallas_call | solution.py:200
  424.0 13.0 %collective-permute-done.56 = bf16[128,2048]{1,0:T(8,128)(2,1)S(1)} collective-permute-done((bf16[128,2048]{1,0:T(8,128)(2,1)S(1)}, bf16[128,2048]{1,0:T(8,128)(2,1)S(1)}, u32[]{:S(2)}, u32[]{:S(2)}) %collective-permute-start.56) | collective-permute-done | bytes 524320 | tf_op jit(solution)/shard_map/ppermute | solution.py:579
  441.2 7.2 %attend_back.6 = (bf16[256,2048]{1,0:T(8,128)(2,1)S(1)}, bf16[256,2048]{1,0:T(8,128)(2,1)S(1)}, bf16[512,768]{1,0:T(8,128)(2,1)S(1)}, f32[8,128]{1,0:T(8,128)S(1)}) custom-call(bf16[256,2048]{1,0:T(8,128)(2,1)S(1)} %constant_dynamic-update-slice_fusion.6.da0.refs_10_, bf16[256,2048]{1,0:T(8,128)(2,1)S(1)} %collective-permute-done.57.da1.refs_11_, ...), custom_call_target="tpu_custom_call" | custom-call | flops 3221225472 | bytes 13243392 | tf_op jit(solution)/shard_map/attend_back/pallas_call | solution.py:200
  450.3 8.6 %attend_back.5 = (bf16[256,2048]{1,0:T(8,128)(2,1)S(1)}, bf16[256,2048]{1,0:T(8,128)(2,1)}, bf16[512,768]{1,0:T(8,128)(2,1)S(1)}, f32[8,128]{1,0:T(8,128)S(1)}) custom-call(bf16[256,2048]{1,0:T(8,128)(2,1)S(1)} %collective-permute-done.51.da0.refs_6_, bf16[256,2048]{1,0:T(8,128)(2,1)S(1)} %collective-permute-done.52.da1.refs_7_, ...), custom_call_target="tpu_custom_call" | custom-call | flops 3221225472 | bytes 13243392 | tf_op jit(solution)/shard_map/attend_back/pallas_call | solution.py:200
  459.9 8.3 %attend_back.7 = (bf16[256,2048]{1,0:T(8,128)(2,1)S(1)}, bf16[256,2048]{1,0:T(8,128)(2,1)}, bf16[512,768]{1,0:T(8,128)(2,1)S(1)}, f32[8,128]{1,0:T(8,128)S(1)}) custom-call(bf16[256,2048]{1,0:T(8,128)(2,1)S(1)} %collective-permute-done.55.da0.refs_8_, bf16[256,2048]{1,0:T(8,128)(2,1)S(1)} %collective-permute-done.61.da1.refs_9_, ...), custom_call_target="tpu_custom_call" | custom-call | flops 3221225472 | bytes 13243392 | tf_op jit(solution)/shard_map/attend_back/pallas_call | solution.py:200
  473.4 10.5 %attention_grad.1 = (bf16[2048,1024]{1,0:T(8,128)(2,1)S(1)}, f32[2048,1]{1,0:T(8,128)S(1)}) custom-call(bf16[272,2048]{1,0:T(8,128)(2,1)S(1)} %pad_maximum_fusion.2.blk0.ids0.refs_0_, bf16[272,2048]{1,0:T(8,128)(2,1)} %collective-permute-done.blk1.ids1.refs_1_, bf16[272,2048]{1,0:T(8,128)(2,1)} %collective-permute-done.1.blk0.ids0.refs_2_, ...), custom_call_target="tpu_custom_call" | custom-call | flops 6442450944 | bytes 16261120 | tf_op jit(solution)/shard_map/attention_grad/pallas_call | solution.py:370
  491.7 12.1 %collective-permute-done.59 = bf16[128,2048]{1,0:T(8,128)(2,1)S(1)} collective-permute-done((bf16[128,2048]{1,0:T(8,128)(2,1)S(1)}, bf16[128,2048]{1,0:T(8,128)(2,1)S(1)}, u32[]{:S(2)}, u32[]{:S(2)}) %collective-permute-start.59) | collective-permute-done | bytes 524320 | tf_op jit(solution)/shard_map/ppermute | solution.py:579
  515.2 26.8 %collective-permute-done.70.refs_2_ = bf16[768,1024]{1,0:T(8,128)(2,1)} collective-permute-done((bf16[768,1024]{1,0:T(8,128)(2,1)S(1)}, bf16[768,1024]{1,0:T(8,128)(2,1)}, u32[]{:S(2)}, u32[]{:S(2)}) %collective-permute-start.70) | collective-permute-done | bytes 1572896 | tf_op jit(solution)/shard_map/ppermute | solution.py:579
  551.5 30.3 %collective-permute-done.72 = bf16[384,1024]{1,0:T(8,128)(2,1)} collective-permute-done((bf16[384,1024]{1,0:T(8,128)(2,1)}, bf16[384,1024]{1,0:T(8,128)(2,1)}, u32[]{:S(2)}, u32[]{:S(2)}) %collective-permute-start.72) | collective-permute-done | bytes 786464 | tf_op jit(solution)/shard_map/ppermute | solution.py:579
  590.6 19.9 %collective-permute-start.76 = (bf16[512,1024]{1,0:T(8,128)(2,1)S(1)}, bf16[512,1024]{1,0:T(8,128)(2,1)}, u32[]{:S(2)}, u32[]{:S(2)}) collective-permute-start(bf16[512,1024]{1,0:T(8,128)(2,1)S(1)} %pad_maximum_fusion.11.refs_0_), channel_id=1, source_target_pairs={{0,8},{4,12},{8,0},{12,4},{16,24},{20,28},{24,16},{28,20},{1,9},{5... | collective-permute-start | bytes 3145736 | tf_op jit(solution)/shard_map/ppermute | solution.py:579
  618.2 16.2 %collective-permute-done.66 = f32[99,128]{1,0:T(8,128)S(1)} collective-permute-done((f32[99,128]{1,0:T(8,128)S(1)}, f32[99,128]{1,0:T(8,128)S(1)}, u32[]{:S(2)}, u32[]{:S(2)}) %collective-permute-start.66) | collective-permute-done | bytes 50720 | tf_op jit(solution)/shard_map/ppermute | solution.py:62
  645.1 7.3 %collective-permute-done.80 = bf16[256,1024]{1,0:T(8,128)(2,1)S(1)} collective-permute-done((bf16[256,1024]{1,0:T(8,128)(2,1)}, bf16[256,1024]{1,0:T(8,128)(2,1)S(1)}, u32[]{:S(2)}, u32[]{:S(2)}) %collective-permute-start.80) | collective-permute-done | bytes 524320 | tf_op jit(solution)/shard_map/ppermute | solution.py:579
  669.1 5.7 place_down.1
  674.7 10.8 %place_units.1 = (f32[4,512,1024]{2,1,0:T(8,128)}, f32[4,512,1024]{2,1,0:T(8,128)}) custom-call(s32[16]{0:T(128)S(1)} %reshape.160.place, bf16[768,1024]{1,0:T(8,128)(2,1)S(1)} %pad_maximum_fusion.1.refs_0_, bf16[768,1024]{1,0:T(8,128)(2,1)} %collective-permute-done.83.refs_1_, bf16[768,1024]{1,0:T(8,128)(2,1)} %collective-permute-done.70.refs_2_, ...), custom_call_target="tpu_custom_call" | custom-call | bytes 33554432 | tf_op jit(solution)/shard_map/place_units/pallas_call | solution.py:481
  685.6 9.7 %place_heads.1 = (f32[512,2048]{1,0:T(8,128)}, f32[512,2048]{1,0:T(8,128)}, f32[512,2048]{1,0:T(8,128)}) custom-call(s32[8]{0:T(128)S(1)} %iota_xor_fusion.1.place, bf16[512,1024]{1,0:T(8,128)(2,1)S(1)} %pad_maximum_fusion.11.refs_0_, bf16[512,1024]{1,0:T(8,128)(2,1)} %collective-permute-done.75.refs_1_, bf16[512,1024]{1,0:T(8,128)(2,1)} %collective-permute-done.76.refs_2_, ...), custom_call_target="tpu_custom_call" | custom-call | bytes 25165824 | tf_op jit(solution)/shard_map/place_heads/pallas_call | solution.py:531
  (640 shorter events, 293.9 us)
Async XLA Ops:
  7.2 87.3 %all-gather.5.cloned.1.call-start = ((), (), s32[]{:S(2)}) async-start(), calls=%async_computation.3 | async-start | bytes 3932160 | tf_op jit(solution)/shard_map/all_gather | solution.py:68
  13.2 118.5 %all-gather.7.cloned.1.call-start = ((), (), s32[]{:S(2)}) async-start(), calls=%async_computation.4 | async-start | bytes 1310720 | tf_op jit(solution)/shard_map/all_gather | solution.py:68
  44.9 42.2 %collective-permute-start.3 = (bf16[256,2048]{1,0:T(8,128)(2,1)}, bf16[256,2048]{1,0:T(8,128)(2,1)}, u32[]{:S(2)}, u32[]{:S(2)}) collective-permute-start(bf16[256,2048]{1,0:T(8,128)(2,1)} %broadcast_select_fusion.refs_4_.c0), channel_id=1, source_target_pairs={{0,8},{4,12},{8,0},{12,4},{16,24},{20,28},{24,16},{28,20},{1,9},{5... | collective-permute-start | bytes 3145736 | tf_op jit(solution)/shard_map/ppermute | solution.py:579
  45.3 41.9 %collective-permute-start.4 = (bf16[256,2048]{1,0:T(8,128)(2,1)}, bf16[256,2048]{1,0:T(8,128)(2,1)}, u32[]{:S(2)}, u32[]{:S(2)}) collective-permute-start(bf16[256,2048]{1,0:T(8,128)(2,1)} %broadcast_select_fusion.refs_4_.c0), channel_id=1, source_target_pairs={{0,16},{4,20},{8,24},{12,28},{16,0},{20,4},{24,8},{28,12},{1,17},{... | collective-permute-start | bytes 3145736 | tf_op jit(solution)/shard_map/ppermute | solution.py:579
  48.8 36.4 %collective-permute-start.11 = (bf16[128,2048]{1,0:T(8,128)(2,1)}, bf16[128,2048]{1,0:T(8,128)(2,1)}, u32[]{:S(2)}, u32[]{:S(2)}) collective-permute-start(bf16[128,2048]{1,0:T(8,128)(2,1)} %slice.459), channel_id=1, source_target_pairs={{0,16},{4,20},{8,24},{12,28},{16,0},{20,4},{24,8},{28,12},{1,17},{... | collective-permute-start | bytes 1572872 | tf_op jit(solution)/shard_map/ppermute | solution.py:579
  50.1 44.5 %collective-permute-start.12 = (bf16[144,2048]{1,0:T(8,128)(2,1)}, bf16[144,2048]{1,0:T(8,128)(2,1)}, u32[]{:S(2)}, u32[]{:S(2)}) collective-permute-start(bf16[144,2048]{1,0:T(8,128)(2,1)} %slice.460), channel_id=1, source_target_pairs={{0,8},{4,12},{8,0},{12,4},{16,24},{20,28},{24,16},{28,20},{1,9},{5... | collective-permute-start | bytes 1769480 | tf_op jit(solution)/shard_map/ppermute | solution.py:579
  51.7 35.4 %collective-permute-start.7 = (bf16[64,2048]{1,0:T(8,128)(2,1)S(1)}, bf16[64,2048]{1,0:T(8,128)(2,1)S(1)}, u32[]{:S(2)}, u32[]{:S(2)}) collective-permute-start(bf16[64,2048]{1,0:T(8,128)(2,1)S(1)} %constant_dynamic-slice_fusion), channel_id=1, source_target_pairs={{0,0},{1,8},{2,16},{3,24},{4,4},{5,12},{6,20},{7,28},{8,1},{9,9},{... | collective-permute-start | bytes 786440 | tf_op jit(solution)/shard_map/ppermute | solution.py:679
  85.2 29.3 %collective-permute-start = (bf16[272,2048]{1,0:T(8,128)(2,1)S(1)}, bf16[272,2048]{1,0:T(8,128)(2,1)}, u32[]{:S(2)}, u32[]{:S(2)}) collective-permute-start(bf16[272,2048]{1,0:T(8,128)(2,1)S(1)} %pad_maximum_fusion.2.blk0.ids0.refs_0_), channel_id=1, source_target_pairs={{0,4},{4,0},{8,12},{12,8},{16,20},{20,16},{24,28},{28,24},{1,5},{5... | collective-permute-start | bytes 3342344 | tf_op jit(solution)/shard_map/ppermute | solution.py:579
  94.5 157.9 %all-gather.9.cloned.1.call-start = ((), (), s32[]{:S(2)}) async-start(), calls=%async_computation.5 | async-start | bytes 5242880 | tf_op jit(solution)/shard_map/all_gather | solution.py:68
  108.2 28.9 %collective-permute-start.9 = (bf16[272,2048]{1,0:T(8,128)(2,1)}, bf16[272,2048]{1,0:T(8,128)(2,1)}, u32[]{:S(2)}, u32[]{:S(2)}) collective-permute-start(bf16[272,2048]{1,0:T(8,128)(2,1)} %collective-permute-done.1.blk0.ids0.refs_2_), channel_id=1, source_target_pairs={{0,4},{4,0},{8,12},{12,8},{16,20},{20,16},{24,28},{28,24},{1,5},{5... | collective-permute-start | bytes 3342344 | tf_op jit(solution)/shard_map/ppermute | solution.py:579
  149.7 140.9 %all-gather.11.cloned.1.call-start = ((), (), s32[]{:S(2)}) async-start(), calls=%async_computation.6 | async-start | bytes 2621440 | tf_op jit(solution)/shard_map/all_gather | solution.py:68
  168.2 33.0 %collective-permute-start.16 = (bf16[256,2048]{1,0:T(8,128)(2,1)S(1)}, bf16[256,2048]{1,0:T(8,128)(2,1)S(1)}, u32[]{:S(2)}, u32[]{:S(2)}) collective-permute-start(bf16[256,2048]{1,0:T(8,128)(2,1)S(1)} %pad_maximum_fusion.5), channel_id=1, source_target_pairs={{0,8},{4,12},{8,0},{12,4},{16,24},{20,28},{24,16},{28,20},{1,9},{5... | collective-permute-start | bytes 3145736 | tf_op jit(solution)/shard_map/ppermute | solution.py:579
  234.1 136.8 %reduce-scatter.4.cloned.1.call-start = ((), (), s32[]{:S(2)}) async-start(), calls=%async_computation.7 | async-start | bytes 2621440 | tf_op jit(solution)/shard_map/reduce_scatter | solution.py:72
  247.9 33.5 %collective-permute-start.29 = (bf16[256,2048]{1,0:T(8,128)(2,1)}, bf16[256,2048]{1,0:T(8,128)(2,1)}, u32[]{:S(2)}, u32[]{:S(2)}) collective-permute-start(bf16[256,2048]{1,0:T(8,128)(2,1)} %broadcast_select_fusion.refs_4_.c0), channel_id=1, source_target_pairs={{0,4},{4,0},{8,12},{12,8},{16,20},{20,16},{24,28},{28,24},{1,5},{5... | collective-permute-start | bytes 3145736 | tf_op jit(solution)/shard_map/ppermute | solution.py:579
  248.9 32.5 %collective-permute-start.30 = (bf16[256,2048]{1,0:T(8,128)(2,1)}, bf16[256,2048]{1,0:T(8,128)(2,1)}, u32[]{:S(2)}, u32[]{:S(2)}) collective-permute-start(bf16[256,2048]{1,0:T(8,128)(2,1)} %collective-permute-done.3.refs_6_.c0), channel_id=1, source_target_pairs={{0,4},{4,0},{8,12},{12,8},{16,20},{20,16},{24,28},{28,24},{1,5},{5... | collective-permute-start | bytes 3145736 | tf_op jit(solution)/shard_map/ppermute | solution.py:579
  250.4 31.0 %collective-permute-start.31 = (bf16[256,2048]{1,0:T(8,128)(2,1)}, bf16[256,2048]{1,0:T(8,128)(2,1)}, u32[]{:S(2)}, u32[]{:S(2)}) collective-permute-start(bf16[256,2048]{1,0:T(8,128)(2,1)} %collective-permute-done.4.refs_8_.c0), channel_id=1, source_target_pairs={{0,4},{4,0},{8,12},{12,8},{16,20},{20,16},{24,28},{28,24},{1,5},{5... | collective-permute-start | bytes 3145736 | tf_op jit(solution)/shard_map/ppermute | solution.py:579
  251.4 30.0 %collective-permute-start.32 = (bf16[256,2048]{1,0:T(8,128)(2,1)}, bf16[256,2048]{1,0:T(8,128)(2,1)}, u32[]{:S(2)}, u32[]{:S(2)}) collective-permute-start(bf16[256,2048]{1,0:T(8,128)(2,1)} %constant_dynamic-update-slice_fusion.refs_10_.c0), channel_id=1, source_target_pairs={{0,4},{4,0},{8,12},{12,8},{16,20},{20,16},{24,28},{28,24},{1,5},{5... | collective-permute-start | bytes 3145736 | tf_op jit(solution)/shard_map/ppermute | solution.py:579
  305.3 182.5 %reduce-scatter.6.cloned.1.call-start = ((), (), s32[]{:S(2)}) async-start(), calls=%async_computation.8 | async-start | bytes 5242880 | tf_op jit(solution)/shard_map/reduce_scatter | solution.py:72
  371.0 215.0 %reduce-scatter.8.cloned.1.call-start = ((), (), s32[]{:S(2)}) async-start(), calls=%async_computation.9 | async-start | bytes 5242880 | tf_op jit(solution)/shard_map/reduce_scatter | solution.py:72
  388.0 33.6 %collective-permute-start.46 = (bf16[256,2048]{1,0:T(8,128)(2,1)S(1)}, bf16[256,2048]{1,0:T(8,128)(2,1)S(1)}, u32[]{:S(2)}, u32[]{:S(2)}) collective-permute-start(bf16[256,2048]{1,0:T(8,128)(2,1)S(1)} %get-tuple-element.178), channel_id=1, source_target_pairs={{0,4},{4,0},{8,12},{12,8},{16,20},{20,16},{24,28},{28,24},{1,5},{5... | collective-permute-start | bytes 3145736 | tf_op jit(solution)/shard_map/ppermute | solution.py:579
  438.3 48.6 %collective-permute-start.48 = (bf16[256,2048]{1,0:T(8,128)(2,1)S(1)}, bf16[256,2048]{1,0:T(8,128)(2,1)S(1)}, u32[]{:S(2)}, u32[]{:S(2)}) collective-permute-start(bf16[256,2048]{1,0:T(8,128)(2,1)S(1)} %pad_maximum_fusion.8), channel_id=1, source_target_pairs={{0,16},{4,20},{8,24},{12,28},{16,0},{20,4},{24,8},{28,12},{1,17},{... | collective-permute-start | bytes 3145736 | tf_op jit(solution)/shard_map/ppermute | solution.py:579
  448.8 39.0 %collective-permute-start.45 = (bf16[256,2048]{1,0:T(8,128)(2,1)S(1)}, bf16[256,2048]{1,0:T(8,128)(2,1)}, u32[]{:S(2)}, u32[]{:S(2)}) collective-permute-start(bf16[256,2048]{1,0:T(8,128)(2,1)S(1)} %pad_maximum_fusion.7), channel_id=1, source_target_pairs={{0,8},{4,12},{8,0},{12,4},{16,24},{20,28},{24,16},{28,20},{1,9},{5... | collective-permute-start | bytes 3145736 | tf_op jit(solution)/shard_map/ppermute | solution.py:579
  504.6 37.4 %collective-permute-start.70 = (bf16[768,1024]{1,0:T(8,128)(2,1)S(1)}, bf16[768,1024]{1,0:T(8,128)(2,1)}, u32[]{:S(2)}, u32[]{:S(2)}) collective-permute-start(bf16[768,1024]{1,0:T(8,128)(2,1)S(1)} %pad_maximum_fusion.1.refs_0_), channel_id=1, source_target_pairs={{0,8},{4,12},{8,0},{12,4},{16,24},{20,28},{24,16},{28,20},{1,9},{5... | collective-permute-start | bytes 4718600 | tf_op jit(solution)/shard_map/ppermute | solution.py:579
  505.5 82.1 %collective-permute-start.50 = (bf16[256,2048]{1,0:T(8,128)(2,1)}, bf16[256,2048]{1,0:T(8,128)(2,1)}, u32[]{:S(2)}, u32[]{:S(2)}) collective-permute-start(bf16[256,2048]{1,0:T(8,128)(2,1)} %copy-done.95), channel_id=1, source_target_pairs={{0,4},{4,0},{8,12},{12,8},{16,20},{20,16},{24,28},{28,24},{1,5},{5... | collective-permute-start | bytes 3145736 | tf_op jit(solution)/shard_map/ppermute | solution.py:579
  505.6 39.6 %collective-permute-start.71 = (bf16[768,1024]{1,0:T(8,128)(2,1)S(1)}, bf16[768,1024]{1,0:T(8,128)(2,1)}, u32[]{:S(2)}, u32[]{:S(2)}) collective-permute-start(bf16[768,1024]{1,0:T(8,128)(2,1)S(1)} %pad_maximum_fusion.1.refs_0_), channel_id=1, source_target_pairs={{0,16},{4,20},{8,24},{12,28},{16,0},{20,4},{24,8},{28,12},{1,17},{... | collective-permute-start | bytes 4718600 | tf_op jit(solution)/shard_map/ppermute | solution.py:579
  510.0 76.0 %collective-permute-start.60 = (bf16[256,2048]{1,0:T(8,128)(2,1)}, bf16[256,2048]{1,0:T(8,128)(2,1)}, u32[]{:S(2)}, u32[]{:S(2)}) collective-permute-start(bf16[256,2048]{1,0:T(8,128)(2,1)} %pad_maximum_fusion.9), channel_id=1, source_target_pairs={{0,8},{4,12},{8,0},{12,4},{16,24},{20,28},{24,16},{28,20},{1,9},{5... | collective-permute-start | bytes 3145736 | tf_op jit(solution)/shard_map/ppermute | solution.py:579
  514.3 71.7 %collective-permute-start.64 = (bf16[256,2048]{1,0:T(8,128)(2,1)}, bf16[256,2048]{1,0:T(8,128)(2,1)}, u32[]{:S(2)}, u32[]{:S(2)}) collective-permute-start(bf16[256,2048]{1,0:T(8,128)(2,1)} %pad_maximum_fusion.10), channel_id=1, source_target_pairs={{0,16},{4,20},{8,24},{12,28},{16,0},{20,4},{24,8},{28,12},{1,17},{... | collective-permute-start | bytes 3145736 | tf_op jit(solution)/shard_map/ppermute | solution.py:579
  544.1 37.7 %collective-permute-start.72 = (bf16[384,1024]{1,0:T(8,128)(2,1)}, bf16[384,1024]{1,0:T(8,128)(2,1)}, u32[]{:S(2)}, u32[]{:S(2)}) collective-permute-start(bf16[384,1024]{1,0:T(8,128)(2,1)} %slice.514), channel_id=1, source_target_pairs={{0,16},{4,20},{8,24},{12,28},{16,0},{20,4},{24,8},{28,12},{1,17},{... | collective-permute-start | bytes 2359304 | tf_op jit(solution)/shard_map/ppermute | solution.py:579
  547.3 36.6 %collective-permute-start.73 = (bf16[384,1024]{1,0:T(8,128)(2,1)}, bf16[384,1024]{1,0:T(8,128)(2,1)}, u32[]{:S(2)}, u32[]{:S(2)}) collective-permute-start(bf16[384,1024]{1,0:T(8,128)(2,1)} %slice.515), channel_id=1, source_target_pairs={{0,8},{4,12},{8,0},{12,4},{16,24},{20,28},{24,16},{28,20},{1,9},{5... | collective-permute-start | bytes 2359304 | tf_op jit(solution)/shard_map/ppermute | solution.py:579
  590.6 43.8 %collective-permute-start.76 = (bf16[512,1024]{1,0:T(8,128)(2,1)S(1)}, bf16[512,1024]{1,0:T(8,128)(2,1)}, u32[]{:S(2)}, u32[]{:S(2)}) collective-permute-start(bf16[512,1024]{1,0:T(8,128)(2,1)S(1)} %pad_maximum_fusion.11.refs_0_), channel_id=1, source_target_pairs={{0,8},{4,12},{8,0},{12,4},{16,24},{20,28},{24,16},{28,20},{1,9},{5... | collective-permute-start | bytes 3145736 | tf_op jit(solution)/shard_map/ppermute | solution.py:579
  617.7 43.3 %collective-permute-start.83 = (bf16[768,1024]{1,0:T(8,128)(2,1)S(1)}, bf16[768,1024]{1,0:T(8,128)(2,1)}, u32[]{:S(2)}, u32[]{:S(2)}) collective-permute-start(bf16[768,1024]{1,0:T(8,128)(2,1)S(1)} %pad_maximum_fusion.1.refs_0_), channel_id=1, source_target_pairs={{0,4},{4,0},{8,12},{12,8},{16,20},{20,16},{24,28},{28,24},{1,5},{5... | collective-permute-start | bytes 4718600 | tf_op jit(solution)/shard_map/ppermute | solution.py:579
  617.8 43.7 %collective-permute-start.84 = (bf16[768,1024]{1,0:T(8,128)(2,1)}, bf16[768,1024]{1,0:T(8,128)(2,1)}, u32[]{:S(2)}, u32[]{:S(2)}) collective-permute-start(bf16[768,1024]{1,0:T(8,128)(2,1)} %collective-permute-done.70.refs_2_), channel_id=1, source_target_pairs={{0,4},{4,0},{8,12},{12,8},{16,20},{20,16},{24,28},{28,24},{1,5},{5... | collective-permute-start | bytes 4718600 | tf_op jit(solution)/shard_map/ppermute | solution.py:579
  (226 other events, 2158.1 us)
Sparse Core Ops, SparseCore 0:
  13.3 81.1 all-gather.4
  96.6 27.9 all-gather.6
  149.8 81.1 all-gather.8
  234.2 45.9 all-gather.10
  305.4 43.5 reduce-scatter.3
  371.1 76.3 reduce-scatter.5
  488.0 76.2 reduce-scatter.7

commit v3 on v2

--- a/solution.py
+++ b/solution.py
@@ -72,7 +72,6 @@
     return lax.psum_scatter(whole, axis, scatter_dimension=0, tiled=True)
 
 
-SCALE = 1.0
 IDS = 16
 
 
@@ -86,7 +85,7 @@
 
 def cost(flops, arrays):
     moved = sum(a.size * a.dtype.itemsize for a in arrays)
-    return pl.CostEstimate(flops=int(flops * SCALE), bytes_accessed=int(moved * SCALE), transcendentals=0)
+    return pl.CostEstimate(flops=flops, bytes_accessed=moved, transcendentals=0)
 
 
 def turned(rows):
@@ -454,7 +453,7 @@
         grid_spec=pltpu.PrefetchScalarGridSpec(
             num_scalar_prefetch=1,
             grid=(1,),
-            in_specs=[pl.BlockSpec((a.shape[0], a.shape[1] // 4), lambda i, place: (0, 3)) for a in pieces],
+            in_specs=[pl.BlockSpec(a.shape, lambda i, place: (0, 0)) for a in pieces],
             out_specs=pl.BlockSpec(shape, lambda i, place: (0, 0)),
         ),
         out_shape=jax.ShapeDtypeStruct(shape, F32),
@@ -516,31 +515,24 @@
     )(table, *pieces)
 
 
-def place_heads_kernel(place, *refs):
-    sources, outs = refs[:-3], refs[-3:]
-    cols = sources[0].shape[1] // 4
-    for m, source in enumerate(sources):
-        lane = pl.multiple_of(place[m] * cols, cols)
-        for i, out in enumerate(outs):
-            out[:, pl.ds(lane, cols)] = source[:, i * cols : (i + 1) * cols].astype(F32)
-
-
-def place_heads(pieces, table, tile):
-    rows, wide = pieces[0].shape
-    width = len(pieces) * wide // 4
-    return pl.pallas_call(
-        place_heads_kernel,
-        grid_spec=pltpu.PrefetchScalarGridSpec(
-            num_scalar_prefetch=1,
-            grid=(rows // tile,),
-            in_specs=[pl.BlockSpec((tile, wide), lambda t, place: (t, 0)) for _ in pieces],
-            out_specs=[pl.BlockSpec((tile, width), lambda t, place: (t, 0))] * 3,
-        ),
-        out_shape=[jax.ShapeDtypeStruct((rows, width), F32)] * 3,
-        compiler_params=params(),
-        cost_estimate=cost(0, [jax.ShapeDtypeStruct((6, rows, width), F32)]),
-        name="place_heads",
-    )(table, *pieces)
+def place_columns_kernel(source, *outs):
+    cols = outs[0].shape[1]
+    for i, out in enumerate(outs):
+        out[...] = source[0, :, i * cols : (i + 1) * cols].astype(F32)
+
+
+def place_columns(source, rows, count):
+    reps, _, wide = source.shape
+    cols = wide // count
+    return pl.pallas_call(
+        place_columns_kernel,
+        grid=(reps,),
+        in_specs=[pl.BlockSpec((1, rows, wide), lambda r: (r, 0, 0))],
+        out_specs=[pl.BlockSpec((rows, cols), lambda r: (0, r)) for _ in range(count)],
+        out_shape=[jax.ShapeDtypeStruct((rows, reps * cols), F32) for _ in range(count)],
+        compiler_params=params(),
+        name="place_columns",
+    )(source)
 
 
 def place_hidden_kernel(parts, shards, sub, source, *outs):
@@ -574,6 +566,7 @@
         self.reps = reps
         self.links = [m for m in range(2, reps, 2)]
         self.links.sort(key=lambda m: (bin(m).count("1"), m))
+        self.singles = [m for m in self.links if m & (m - 1) == 0]
 
     def swap(self, piece, bit):
         return lax.ppermute(piece, "rep", [(i, i ^ bit) for i in range(self.reps)])
@@ -582,23 +575,51 @@
     def hops(m):
         return 1 << (m.bit_length() - 1), m & -m
 
+    def gathering(self, block):
+        return RingGather(self, block)
+
     def gather(self, block):
-        half = max(block.shape[0] // 32 * 16, 8)
-        held = {0: block}
-        for m in self.links:
-            high, low = self.hops(m)
-            if high == low:
-                held[m] = self.swap(block, m)
-            else:
-                held[m] = jnp.concatenate(
-                    [self.swap(held[m ^ high][:half], high), self.swap(held[m ^ low][half:], low)]
-                )
+        whole_set = RingGather(self, block)
+        whole_set.near()
+        whole_set.far()
         for m in [0] + self.links:
-            held[m ^ 1] = self.swap(held[m], 1)
-        return [held[m] for m in range(self.reps)]
+            whole_set.core(m)
+        return whole_set.blocks()
 
     def summing(self):
         return RingSum(self)
+
+
+class RingGather:
+    def __init__(self, ring, block):
+        self.ring = ring
+        self.half = max(block.shape[0] // 32 * 16, 8)
+        self.held = {0: block}
+
+    def near(self, *gate):
+        block = after(self.held[0], *gate) if gate else self.held[0]
+        for m in self.ring.singles:
+            self.held[m] = self.ring.swap(block, m)
+
+    def far(self, *gate):
+        for m in self.ring.links:
+            high, low = self.ring.hops(m)
+            if high == low:
+                continue
+            first, second = self.held[m ^ high][: self.half], self.held[m ^ low][self.half :]
+            if gate:
+                first, second = after((first, second), *gate)
+            self.held[m] = jnp.concatenate([self.ring.swap(first, high), self.ring.swap(second, low)])
+
+    def core(self, m, *gate):
+        block = after(self.held[m], *gate) if gate else self.held[m]
+        self.held[m ^ 1] = self.ring.swap(block, 1)
+
+    def pair(self, m):
+        return [self.held[m], self.held[m ^ 1]]
+
+    def blocks(self):
+        return [self.held[m] for m in range(self.ring.reps)]
 
 
 class RingSum:
@@ -685,7 +706,8 @@
         normed = (stream * first_scale * norm_gain).astype(BF16)
         ids = jnp.concatenate([segment_ids[None], expert_ids.T]).astype(BF16)
         ids = jnp.pad(ids, ((0, IDS - ids.shape[0]), (0, width - length)))
-        blocks = ring.gather(jnp.concatenate([normed, ids]))
+        first = ring.gathering(jnp.concatenate([normed, ids]))
+        first.near()
         pairs = range(0, reps, 2)
 
         unit = jnp.stack([expert, part]).astype(jnp.int32)
@@ -695,23 +717,35 @@
             own_gu = jnp.concatenate([hidden_columns(w_gate), hidden_columns(w_up)], 1)
             own_dn = lax.dynamic_slice(w_down, (expert, part * sub, 0), (1, sub, width))[0]
         grad_moe_own = jnp.where(segment_ids[:, None] > 0, cotangent, jnp.zeros_like(cotangent))
-        grad_moe = ring.gather(after(grad_moe_own, blocks[2], blocks[4]))
-        arrived = [grad_moe[m] for m in ring.links]
-        w_out = gather(after(out_piece, w_qkv, grad_moe[2], grad_moe[4]), "shard")
-        w_gu = gather(after(own_gu, w_out), "shard")
+        router = jnp.pad(w_router, ((0, 0), (0, 128 - experts)))
+        first.far(own_gu, own_dn, router)
+        for m in [0] + ring.links:
+            first.core(m)
+        blocks = first.blocks()
+        w_out = gather(after(out_piece, w_qkv), "shard")
+        second = ring.gathering(grad_moe_own)
+        second.near(blocks[ring.links[-1]])
 
         cosine, sine = rotary_tables(length, head_size)
         cosine = jnp.concatenate([cosine, cosine], axis=1)
         sine = jnp.concatenate([-sine, sine], axis=1)
-        gains = after(jnp.stack([query_gain, key_gain]), own_gu, own_dn, *arrived)
+        gains = jnp.stack([query_gain, key_gain])
         order = sorted(pairs, key=lambda m: (-bin(m).count("1"), m))
-        singles = [m for m in ring.links if m & (m - 1) == 0]
+        singles = ring.singles
         attended = {
             m: attend(blocks[m : m + 2], w_qkv, gains, cosine, sine, length, score_scale) for m in order
         }
+        second.far(*[attended[m][1] for m in order])
+        for m in [0] + ring.links:
+            second.core(m)
+        grad_moe = second.blocks()
+        w_gu = gather(after(own_gu, w_out, *[attended[m][1] for m in order]), "shard")
         summed = ring.summing()
-        for m in order:
-            mixed = after(attended[m][1], attended[order[-1]][1]) if m != order[-1] else attended[m][1]
+        for i, m in enumerate(order):
+            gate = [attended[k][1] for k in order if k != m] if i == 0 else []
+            gate += [grad_moe[ring.links[-1]]] if i == 1 else []
+            gate += grad_moe if i == 2 else []
+            mixed = after(attended[m][1], *gate) if gate else attended[m][1]
             summed.feed(m, *mix_out(mixed, w_out, length, "mix_out"))
         summed.far()
         near = [summed.near(m) for m in singles]
@@ -724,7 +758,6 @@
         ffn_all = ring.gather(normed_ffn)
 
         place = jnp.stack([rep, expert]).astype(jnp.int32)
-        router = jnp.pad(w_router, ((0, 0), (0, 128 - experts)))
         entered = {m: expert_in(place, ffn_all[m : m + 2], blocks[m : m + 2], router, w_gu, length, experts) for m in order}
         inner_gated = [entered[m][0] for m in pairs]
         part_dn = weight_grad(inner_gated, grad_moe, hid, 512, "down_grad")
@@ -801,7 +834,12 @@
 
         sum_attention = scatter_sum(after(part_attention, sum_gu, *moe_last), "shard")
         chops = [sum_dn[:, c : c + 2 * hid] for c in range(0, width, 2 * hid)]
-        pieces = ring.gather(after(jnp.concatenate([sum_gu] + chops), *far))
+        expert_grads = ring.gathering(jnp.concatenate([sum_gu] + chops))
+        expert_grads.near(*far)
+        expert_grads.far()
+        for m in [0] + ring.links:
+            expert_grads.core(m)
+        pieces = expert_grads.blocks()
 
         device = rep ^ jnp.arange(reps, dtype=jnp.int32)
         shapes = ((experts, rows, hidden_total),) * 2 + ((experts, parts * sub, width),)
@@ -811,13 +849,6 @@
             all_gate, all_up = place_units(pieces, units, parts, shards, shapes[0], 64)
         else:
             all_gate, all_up = place_hidden(lax.all_gather(sum_gu, "rep"), experts, shards, rows // 4)
-        sum_attention = after(sum_attention, *[pieces[m] for m in ring.links], *normed_last)
-        sum_out = lax.ppermute(sum_attention[:, 3 * cols :], ("rep", "shard"), back)
-        pieces = ring.gather(jnp.concatenate([sum_attention[:, : 3 * cols], sum_out], axis=1))
-        all_qkv = place_heads(pieces, device, 64)
-        row_block = lax.rem(device, per_plane) * shards + lax.div(device, per_plane)
-        all_out = place_out(pieces, row_block, out_rows, (rows, width))
-
         square_sums = jnp.stack(
             [
                 jnp.sum(live * stream * stream),
@@ -828,9 +859,29 @@
         )
         small = [grad_norm_gain, grad_ffn_gain, grad_qgain, grad_kgain, grad_router.T.reshape(-1)]
         small.append(jnp.pad(square_sums, (0, 124)))
-        small = total_over_all(
-            jnp.concatenate([part.reshape(-1, 128) for part in small]), (("rep", reps), ("shard", shards))
-        ).reshape(-1)
+        small = jnp.concatenate([part.reshape(-1, 128) for part in small])
+        count = small.size
+        small = total_over_all(small, (("shard", shards),)).reshape(-1)
+        wide = 3 * cols
+        lines = -(-count // wide)
+        small = jnp.pad(small, (0, lines * wide - count)).reshape(lines, wide)
+        high = lax.reduce_precision(small, 8, 7)
+        low = (small - high).astype(BF16)
+        filler = jnp.zeros((-2 * lines % 16, wide), BF16)
+        extra = jnp.concatenate([high.astype(BF16), low, filler])
+        sum_attention = after(sum_attention, *[expert_grads.held[m] for m in singles], *normed_last, extra)
+        last = lax.all_gather(jnp.concatenate([sum_attention[:, :wide], extra]), "rep")
+        all_qkv = place_columns(last, rows, 3)
+        small = last[:, rows : rows + lines].astype(F32) + last[:, rows + lines : rows + 2 * lines].astype(F32)
+        small = jnp.sum(small, axis=0).reshape(-1)
+        row_block = lax.rem(device, per_plane) * shards + lax.div(device, per_plane)
+        out_piece = after(sum_attention[:, wide:], expert_grads.held[ring.links[-1]])
+        out_set = ring.gathering(lax.ppermute(out_piece, ("rep", "shard"), back))
+        out_set.near()
+        out_set.far(all_gate, all_dn)
+        for m in [0] + ring.links:
+            out_set.core(m)
+        all_out = place_out(out_set.blocks(), row_block, out_rows, (rows, width))
         norm_sum, ffn_sum = small[:width], small[width : 2 * width]
         small = small[2 * width :]
         qgain_sum, kgain_sum = small[:head_size], small[head_size : 2 * head_size]

time: 714 us -> 670 us (0.938)
  waiting for transfers between devices: 288 us -> 248 us
  local copies, waits for them, and re-layouts: 115 us -> 92.8 us
  starting transfers between devices: 69.4 us -> 89.8 us
    ppermute x80, waiting for transfers between devices: 258 us -> 218 us  [swap(): return lax.ppermute(piece, 'rep', [(i, i ^ bit) for i in range(self.reps)])]
    ppermute x80, starting transfers between devices: 63.3 us -> 82.9 us  [swap(): return lax.ppermute(piece, 'rep', [(i, i ^ bit) for i in range(self.reps)])]
    unnamed x331 -> x271, local copies, waits for them, and re-layouts: 88.7 us -> 73.1 us
    all_gather x4, waiting for transfers between devices: 7.35 us -> 20 us  [gather(): return lax.all_gather(piece, axis, axis=dim, tiled=True)]
    ppermute x5 -> x2, waiting for transfers between devices: 22.2 us -> 9.92 us  [total_over_all(): lax.ppermute(value, axis, [(i, i ^ bit) for i in range(size)])]
  transfers between devices with their start and end apart: 94 -> 92, of which waited for: 30 -> 35; matrix products, arithmetic and copies ran while one was open for 12% -> 10% of each run, Pallas kernels for 21% -> 23%
where the time goes in v3:
time: 670 us; the launch traced here: 665 us
  waiting for transfers between devices  248 us (37%)
  Pallas kernels  165 us (25%)
  local copies, waits for them, and re-layouts  92.8 us (14%)
  starting transfers between devices  89.8 us (13%)
  other arithmetic  49.2 us (7%)
  between operations  16.7 us (2%)
    ppermute x80, waiting for transfers between devices, swap(): return lax.ppermute(piece, 'rep', [(i, i ^ bit) for i in range(self.reps)])  218 us
    ppermute x80, starting transfers between devices, swap(): return lax.ppermute(piece, 'rep', [(i, i ^ bit) for i in range(self.reps)])  82.9 us
    unnamed x271, local copies, waits for them, and re-layouts  73.1 us
    pallas_call x4, Pallas kernels, attend_back(): pl.pallas_call(functools.partial(attend_back_kernel, length, score_scale)...  31.3 us
    pallas_call x4, Pallas kernels, attend(): pl.pallas_call(functools.partial(attend_kernel, length, score_scale), gri...  23.1 us
    pallas_call x3, Pallas kernels, weight_grad(): pl.pallas_call(functools.partial(weight_grad_kernel, len(left)), grid=(ou...  22.5 us
    pallas_call x4, Pallas kernels, expert_back(): pl.pallas_call(functools.partial(expert_back_kernel, length), grid=(1,),...  21.5 us
    all_gather x4, waiting for transfers between devices, gather(): return lax.all_gather(piece, axis, axis=dim, tiled=True)  20 us
  transfers between devices with their start and end apart: 92, of which 35 were waited for; matrix products, arithmetic and copies ran while one was open for 10% of the time, Pallas kernels for 23%

profile of v3, /device:TPU:0, one launch (start us, length us, event | category | flops | bytes accessed | tf_op | source)
XLA Modules:
  0.0 664.8 jit_solution(7682695300560473351)
XLA Ops:
  30.4 12.9 %collective-permute-done.5.blk0.ids0.refs_4_ = bf16[272,2048]{1,0:T(8,128)(2,1)} collective-permute-done((bf16[272,2048]{1,0:T(8,128)(2,1)}, bf16[272,2048]{1,0:T(8,128)(2,1)}, u32[]{:S(2)}, u32[]{:S(2)}) %collective-permute-start.5) | collective-permute-done | bytes 1114144 | tf_op jit(solution)/shard_map/ppermute | solution.py:572
  52.6 7.0 %collective-permute-done.6 = bf16[128,2048]{1,0:T(8,128)(2,1)S(1)} collective-permute-done((bf16[128,2048]{1,0:T(8,128)(2,1)}, bf16[128,2048]{1,0:T(8,128)(2,1)S(1)}, u32[]{:S(2)}, u32[]{:S(2)}) %collective-permute-start.6) | collective-permute-done | bytes 524320 | tf_op jit(solution)/shard_map/ppermute | solution.py:572
  65.6 5.3 collective-permute-start.9
  71.5 20.0 %all-gather.7.cloned.1.call-done.w_qkv.refs_13_ = bf16[2048,768]{1,0:T(8,128)(2,1)} async-done(((bf16[512,768]{1,0:T(8,128)(2,1)}), bf16[2048,768]{1,0:T(8,128)(2,1)}) %all-gather.7.cloned.1.call-update) | async-done | bytes 3145744 | tf_op jit(solution)/shard_map/all_gather | solution.py:68
  101.5 5.5 attend.6
  108.2 5.5 attend.5
  113.7 6.0 attend.7
  120.9 6.1 attend.4
  135.7 7.6 %collective-permute-done.12 = bf16[128,2048]{1,0:T(8,128)(2,1)S(1)} collective-permute-done((bf16[128,2048]{1,0:T(8,128)(2,1)}, bf16[128,2048]{1,0:T(8,128)(2,1)S(1)}, u32[]{:S(2)}, u32[]{:S(2)}) %collective-permute-start.12) | collective-permute-done | bytes 524320 | tf_op jit(solution)/shard_map/ppermute | solution.py:572
  155.8 8.8 %collective-permute-done.16 = bf16[128,2048]{1,0:T(8,128)(2,1)S(1)} collective-permute-done((bf16[128,2048]{1,0:T(8,128)(2,1)S(1)}, bf16[128,2048]{1,0:T(8,128)(2,1)S(1)}, u32[]{:S(2)}, u32[]{:S(2)}) %collective-permute-start.16) | collective-permute-done | bytes 524320 | tf_op jit(solution)/shard_map/ppermute | solution.py:572
  170.4 21.5 %collective-permute-done.17 = bf16[256,2048]{1,0:T(8,128)(2,1)S(1)} collective-permute-done((bf16[256,2048]{1,0:T(8,128)(2,1)S(1)}, bf16[256,2048]{1,0:T(8,128)(2,1)S(1)}, u32[]{:S(2)}, u32[]{:S(2)}) %collective-permute-start.17) | collective-permute-done | bytes 1048608 | tf_op jit(solution)/shard_map/ppermute | solution.py:572
  198.2 21.8 %collective-permute-done.26.b0.refs_2_ = bf16[256,2048]{1,0:T(8,128)(2,1)S(1)} collective-permute-done((bf16[256,2048]{1,0:T(8,128)(2,1)S(1)}, bf16[256,2048]{1,0:T(8,128)(2,1)S(1)}, u32[]{:S(2)}, u32[]{:S(2)}) %collective-permute-start.26) | collective-permute-done | bytes 1048608 | tf_op jit(solution)/shard_map/ppermute | solution.py:572
  224.2 8.6 %collective-permute-done.30 = bf16[128,2048]{1,0:T(8,128)(2,1)S(1)} collective-permute-done((bf16[128,2048]{1,0:T(8,128)(2,1)}, bf16[128,2048]{1,0:T(8,128)(2,1)S(1)}, u32[]{:S(2)}, u32[]{:S(2)}) %collective-permute-start.30) | collective-permute-done | bytes 524320 | tf_op jit(solution)/shard_map/ppermute | solution.py:572
  269.8 7.1 %down_grad.1 = bf16[512,2048]{1,0:T(8,128)(2,1)S(1)} custom-call(bf16[512,512]{1,0:T(8,128)(2,1)S(1)} %get-tuple-element.176.refs_0_.mixed, bf16[512,512]{1,0:T(8,128)(2,1)S(1)} %get-tuple-element.179.refs_1_.mixed, bf16[512,512]{1,0:T(8,128)(2,1)S(1)} %get-tuple-element.185.refs_2_.mixed, bf16[512,512]{1,0:T(8,128)(2,1)S(1)} %get-tuple-element.182.refs_3_.mixed, ...), custom_call_target="tpu_custom_call" | custom-call | flops 4294967296 | bytes 12582912 | tf_op jit(solution)/shard_map/down_grad/pallas_call | solution.py:338
  285.5 6.1 expert_back.5
  333.5 12.2 %up_grad.1 = bf16[2048,1024]{1,0:T(8,128)(2,1)S(1)} custom-call(bf16[256,2048]{1,0:T(8,128)(2,1)S(1)} %multiply_convert_fusion.1.b0.refs_0_, bf16[256,2048]{1,0:T(8,128)(2,1)} %collective-permute-done.25.b1.refs_1_, bf16[256,2048]{1,0:T(8,128)(2,1)S(1)} %collective-permute-done.26.b0.refs_2_, bf16[256,2048]{1,0:T(8,128)(2,1)} %collective-permute-done.27.b1.refs_3_, ...), custom_call_target="tpu_custom_call" | custom-call | flops 8589934592 | bytes 16777216 | tf_op jit(solution)/shard_map/up_grad/pallas_call | solution.py:338
  348.1 10.1 %collective-permute-done.40 = bf16[272,2048]{1,0:T(8,128)(2,1)} collective-permute-done((bf16[272,2048]{1,0:T(8,128)(2,1)}, bf16[272,2048]{1,0:T(8,128)(2,1)}, u32[]{:S(2)}, u32[]{:S(2)}) %collective-permute-start.40) | collective-permute-done | bytes 1114144 | tf_op jit(solution)/shard_map/ppermute | solution.py:572
  376.8 17.9 %collective-permute-done.51.da0.refs_6_ = bf16[256,2048]{1,0:T(8,128)(2,1)S(1)} collective-permute-done((bf16[256,2048]{1,0:T(8,128)(2,1)S(1)}, bf16[256,2048]{1,0:T(8,128)(2,1)S(1)}, u32[]{:S(2)}, u32[]{:S(2)}) %collective-permute-start.51) | collective-permute-done | bytes 1048608 | tf_op jit(solution)/shard_map/ppermute | solution.py:572
  400.3 7.5 %attend_back.4 = (bf16[256,2048]{1,0:T(8,128)(2,1)S(1)}, bf16[256,2048]{1,0:T(8,128)(2,1)S(1)}, bf16[512,768]{1,0:T(8,128)(2,1)S(1)}, f32[8,128]{1,0:T(8,128)S(1)}) custom-call(bf16[256,2048]{1,0:T(8,128)(2,1)S(1)} %get-tuple-element.239.da0.refs_4_, bf16[256,2048]{1,0:T(8,128)(2,1)S(1)} %collective-permute-done.49.da1.refs_5_, ...), custom_call_target="tpu_custom_call" | custom-call | flops 3221225472 | bytes 13243392 | tf_op jit(solution)/shard_map/attend_back/pallas_call | solution.py:199
  410.5 12.8 %collective-permute-done.56 = bf16[128,2048]{1,0:T(8,128)(2,1)S(1)} collective-permute-done((bf16[128,2048]{1,0:T(8,128)(2,1)S(1)}, bf16[128,2048]{1,0:T(8,128)(2,1)S(1)}, u32[]{:S(2)}, u32[]{:S(2)}) %collective-permute-start.56) | collective-permute-done | bytes 524320 | tf_op jit(solution)/shard_map/ppermute | solution.py:572
  427.5 7.5 %attend_back.6 = (bf16[256,2048]{1,0:T(8,128)(2,1)S(1)}, bf16[256,2048]{1,0:T(8,128)(2,1)S(1)}, bf16[512,768]{1,0:T(8,128)(2,1)S(1)}, f32[8,128]{1,0:T(8,128)S(1)}) custom-call(bf16[256,2048]{1,0:T(8,128)(2,1)S(1)} %constant_dynamic-update-slice_fusion.6.da0.refs_10_, bf16[256,2048]{1,0:T(8,128)(2,1)S(1)} %collective-permute-done.57.da1.refs_11_, ...), custom_call_target="tpu_custom_call" | custom-call | flops 3221225472 | bytes 13243392 | tf_op jit(solution)/shard_map/attend_back/pallas_call | solution.py:199
  436.6 7.8 %attend_back.5 = (bf16[256,2048]{1,0:T(8,128)(2,1)S(1)}, bf16[256,2048]{1,0:T(8,128)(2,1)S(1)}, bf16[512,768]{1,0:T(8,128)(2,1)S(1)}, f32[8,128]{1,0:T(8,128)S(1)}) custom-call(bf16[256,2048]{1,0:T(8,128)(2,1)S(1)} %collective-permute-done.51.da0.refs_6_, bf16[256,2048]{1,0:T(8,128)(2,1)S(1)} %collective-permute-done.52.da1.refs_7_, ...), custom_call_target="tpu_custom_call" | custom-call | flops 3221225472 | bytes 13243392 | tf_op jit(solution)/shard_map/attend_back/pallas_call | solution.py:199
  445.5 8.4 %attend_back.7 = (bf16[256,2048]{1,0:T(8,128)(2,1)S(1)}, bf16[256,2048]{1,0:T(8,128)(2,1)}, bf16[512,768]{1,0:T(8,128)(2,1)S(1)}, f32[8,128]{1,0:T(8,128)S(1)}) custom-call(bf16[256,2048]{1,0:T(8,128)(2,1)S(1)} %collective-permute-done.55.da0.refs_8_, bf16[256,2048]{1,0:T(8,128)(2,1)S(1)} %collective-permute-done.61.da1.refs_9_, ...), custom_call_target="tpu_custom_call" | custom-call | flops 3221225472 | bytes 13243392 | tf_op jit(solution)/shard_map/attend_back/pallas_call | solution.py:199
  458.2 10.5 %attention_grad.1 = (bf16[2048,1024]{1,0:T(8,128)(2,1)S(1)}, f32[2048,1]{1,0:T(8,128)S(1)}) custom-call(bf16[272,2048]{1,0:T(8,128)(2,1)} %pad_maximum_fusion.2.blk0.ids0.refs_0_, bf16[272,2048]{1,0:T(8,128)(2,1)S(1)} %copy-done.27, bf16[272,2048]{1,0:T(8,128)(2,1)} %collective-permute-done.3.blk0.ids0.refs_2_, bf16[272,2048]{1,0:T(8,128)(2,1)S(1)} %copy-done.24, ...), custom_call_target="tpu_custom_call" | custom-call | flops 6442450944 | bytes 16261120 | tf_op jit(solution)/shard_map/attention_grad/pallas_call | solution.py:369
  480.6 9.9 %collective-permute-done.59 = bf16[128,2048]{1,0:T(8,128)(2,1)} collective-permute-done((bf16[128,2048]{1,0:T(8,128)(2,1)}, bf16[128,2048]{1,0:T(8,128)(2,1)}, u32[]{:S(2)}, u32[]{:S(2)}) %collective-permute-start.59) | collective-permute-done | bytes 524320 | tf_op jit(solution)/shard_map/ppermute | solution.py:572
  504.3 15.5 %collective-permute-done.60 = bf16[256,2048]{1,0:T(8,128)(2,1)} collective-permute-done((bf16[256,2048]{1,0:T(8,128)(2,1)}, bf16[256,2048]{1,0:T(8,128)(2,1)}, u32[]{:S(2)}, u32[]{:S(2)}) %collective-permute-start.60) | collective-permute-done | bytes 1048608 | tf_op jit(solution)/shard_map/ppermute | solution.py:572
  541.0 5.4 collective-permute-done.68
  546.4 5.5 collective-permute-done.65.refs_2_
  561.8 23.3 %collective-permute-done.69 = bf16[384,1024]{1,0:T(8,128)(2,1)S(1)} collective-permute-done((bf16[384,1024]{1,0:T(8,128)(2,1)S(1)}, bf16[384,1024]{1,0:T(8,128)(2,1)S(1)}, u32[]{:S(2)}, u32[]{:S(2)}) %collective-permute-start.69) | collective-permute-done | bytes 786464 | tf_op jit(solution)/shard_map/ppermute | solution.py:572
  589.4 22.7 %collective-permute-start.73 = (bf16[512,256]{1,0:T(8,128)(2,1)}, bf16[512,256]{1,0:T(8,128)(2,1)S(1)}, u32[]{:S(2)}, u32[]{:S(2)}) collective-permute-start(bf16[512,256]{1,0:T(8,128)(2,1)} %collective-permute-done.71.refs_0_), channel_id=1, source_target_pairs={{0,8},{4,12},{8,0},{12,4},{16,24},{20,28},{24,16},{28,20},{1,9},{5... | collective-permute-start | bytes 786440 | tf_op jit(solution)/shard_map/ppermute | solution.py:572
  614.8 5.5 place_down.1
  620.4 10.6 %place_units.1 = (f32[4,512,1024]{2,1,0:T(8,128)}, f32[4,512,1024]{2,1,0:T(8,128)}) custom-call(s32[16]{0:T(128)S(1)} %reshape.156.place, bf16[768,1024]{1,0:T(8,128)(2,1)S(1)} %pad_maximum_fusion.1.refs_0_, bf16[768,1024]{1,0:T(8,128)(2,1)S(1)} %copy-done.9, bf16[768,1024]{1,0:T(8,128)(2,1)S(1)} %collective-permute-done.65.refs_2_, ...), custom_call_target="tpu_custom_call" | custom-call | bytes 33554432 | tf_op jit(solution)/shard_map/place_units/pallas_call | solution.py:480
  (581 shorter events, 305.2 us)
Async XLA Ops:
  7.2 84.3 %all-gather.7.cloned.1.call-start = ((), (), s32[]{:S(2)}) async-start(), calls=%async_computation.3 | async-start | bytes 3932160 | tf_op jit(solution)/shard_map/all_gather | solution.py:68
  13.2 119.9 %all-gather.9.cloned.1.call-start = ((), (), s32[]{:S(2)}) async-start(), calls=%async_computation.4 | async-start | bytes 1310720 | tf_op jit(solution)/shard_map/all_gather | solution.py:68
  15.5 27.8 %collective-permute-start.5 = (bf16[272,2048]{1,0:T(8,128)(2,1)}, bf16[272,2048]{1,0:T(8,128)(2,1)}, u32[]{:S(2)}, u32[]{:S(2)}) collective-permute-start(bf16[272,2048]{1,0:T(8,128)(2,1)} %pad_maximum_fusion.2.blk0.ids0.refs_0_), channel_id=1, source_target_pairs={{0,16},{4,20},{8,24},{12,28},{16,0},{20,4},{24,8},{28,12},{1,17},{... | collective-permute-start | bytes 3342344 | tf_op jit(solution)/shard_map/ppermute | solution.py:572
  18.4 26.3 %collective-permute-start.3 = (bf16[272,2048]{1,0:T(8,128)(2,1)}, bf16[272,2048]{1,0:T(8,128)(2,1)}, u32[]{:S(2)}, u32[]{:S(2)}) collective-permute-start(bf16[272,2048]{1,0:T(8,128)(2,1)} %pad_maximum_fusion.2.blk0.ids0.refs_0_), channel_id=1, source_target_pairs={{0,8},{4,12},{8,0},{12,4},{16,24},{20,28},{24,16},{28,20},{1,9},{5... | collective-permute-start | bytes 3342344 | tf_op jit(solution)/shard_map/ppermute | solution.py:572
  63.4 33.5 %collective-permute-start.8 = (bf16[256,2048]{1,0:T(8,128)(2,1)}, bf16[256,2048]{1,0:T(8,128)(2,1)}, u32[]{:S(2)}, u32[]{:S(2)}) collective-permute-start(bf16[256,2048]{1,0:T(8,128)(2,1)} %broadcast_select_fusion.refs_4_.c0), channel_id=1, source_target_pairs={{0,8},{4,12},{8,0},{12,4},{16,24},{20,28},{24,16},{28,20},{1,9},{5... | collective-permute-start | bytes 3145736 | tf_op jit(solution)/shard_map/ppermute | solution.py:572
  64.9 36.6 %collective-permute-start.10 = (bf16[272,2048]{1,0:T(8,128)(2,1)}, bf16[272,2048]{1,0:T(8,128)(2,1)}, u32[]{:S(2)}, u32[]{:S(2)}) collective-permute-start(bf16[272,2048]{1,0:T(8,128)(2,1)} %constant_dynamic-update-slice_fusion.blk0.ids0.refs_6_), channel_id=1, source_target_pairs={{0,4},{4,0},{8,12},{12,8},{16,20},{20,16},{24,28},{28,24},{1,5},{5... | collective-permute-start | bytes 3342344 | tf_op jit(solution)/shard_map/ppermute | solution.py:572
  65.6 34.0 %collective-permute-start.9 = (bf16[256,2048]{1,0:T(8,128)(2,1)}, bf16[256,2048]{1,0:T(8,128)(2,1)}, u32[]{:S(2)}, u32[]{:S(2)}) collective-permute-start(bf16[256,2048]{1,0:T(8,128)(2,1)} %broadcast_select_fusion.refs_4_.c0), channel_id=1, source_target_pairs={{0,16},{4,20},{8,24},{12,28},{16,0},{20,4},{24,8},{28,12},{1,17},{... | collective-permute-start | bytes 3145736 | tf_op jit(solution)/shard_map/ppermute | solution.py:572
  71.0 37.2 %collective-permute-start.4 = (bf16[272,2048]{1,0:T(8,128)(2,1)}, bf16[272,2048]{1,0:T(8,128)(2,1)S(1)}, u32[]{:S(2)}, u32[]{:S(2)}) collective-permute-start(bf16[272,2048]{1,0:T(8,128)(2,1)} %collective-permute-done.3.blk0.ids0.refs_2_), channel_id=1, source_target_pairs={{0,4},{4,0},{8,12},{12,8},{16,20},{20,16},{24,28},{28,24},{1,5},{5... | collective-permute-start | bytes 3342344 | tf_op jit(solution)/shard_map/ppermute | solution.py:572
  71.0 42.7 %collective-permute-start.11 = (bf16[272,2048]{1,0:T(8,128)(2,1)}, bf16[272,2048]{1,0:T(8,128)(2,1)}, u32[]{:S(2)}, u32[]{:S(2)}) collective-permute-start(bf16[272,2048]{1,0:T(8,128)(2,1)} %collective-permute-done.5.blk0.ids0.refs_4_), channel_id=1, source_target_pairs={{0,4},{4,0},{8,12},{12,8},{16,20},{20,16},{24,28},{28,24},{1,5},{5... | collective-permute-start | bytes 3342344 | tf_op jit(solution)/shard_map/ppermute | solution.py:572
  91.5 147.0 %all-gather.11.cloned.1.call-start = ((), (), s32[]{:S(2)}) async-start(), calls=%async_computation.5 | async-start | bytes 5242880 | tf_op jit(solution)/shard_map/all_gather | solution.py:68
  149.0 130.1 %all-gather.13.cloned.1.call-start = ((), (), s32[]{:S(2)}) async-start(), calls=%async_computation.6 | async-start | bytes 2621440 | tf_op jit(solution)/shard_map/all_gather | solution.py:68
  221.9 136.3 %reduce-scatter.4.cloned.1.call-start = ((), (), s32[]{:S(2)}) async-start(), calls=%async_computation.7 | async-start | bytes 2621440 | tf_op jit(solution)/shard_map/reduce_scatter | solution.py:72
  236.4 26.6 %collective-permute-start.25 = (bf16[256,2048]{1,0:T(8,128)(2,1)S(1)}, bf16[256,2048]{1,0:T(8,128)(2,1)}, u32[]{:S(2)}, u32[]{:S(2)}) collective-permute-start(bf16[256,2048]{1,0:T(8,128)(2,1)S(1)} %multiply_convert_fusion.1.b0.refs_0_), channel_id=1, source_target_pairs={{0,4},{4,0},{8,12},{12,8},{16,20},{20,16},{24,28},{28,24},{1,5},{5... | collective-permute-start | bytes 3145736 | tf_op jit(solution)/shard_map/ppermute | solution.py:572
  292.7 179.9 %reduce-scatter.6.cloned.1.call-start = ((), (), s32[]{:S(2)}) async-start(), calls=%async_computation.8 | async-start | bytes 5242880 | tf_op jit(solution)/shard_map/reduce_scatter | solution.py:72
  322.1 26.0 %collective-permute-start.38 = (bf16[272,2048]{1,0:T(8,128)(2,1)}, bf16[272,2048]{1,0:T(8,128)(2,1)}, u32[]{:S(2)}, u32[]{:S(2)}) collective-permute-start(bf16[272,2048]{1,0:T(8,128)(2,1)} %pad_maximum_fusion.3), channel_id=1, source_target_pairs={{0,8},{4,12},{8,0},{12,4},{16,24},{20,28},{24,16},{28,20},{1,9},{5... | collective-permute-start | bytes 3342344 | tf_op jit(solution)/shard_map/ppermute | solution.py:572
  330.9 27.3 %collective-permute-start.40 = (bf16[272,2048]{1,0:T(8,128)(2,1)}, bf16[272,2048]{1,0:T(8,128)(2,1)}, u32[]{:S(2)}, u32[]{:S(2)}) collective-permute-start(bf16[272,2048]{1,0:T(8,128)(2,1)} %pad_maximum_fusion.4), channel_id=1, source_target_pairs={{0,16},{4,20},{8,24},{12,28},{16,0},{20,4},{24,8},{28,12},{1,17},{... | collective-permute-start | bytes 3342344 | tf_op jit(solution)/shard_map/ppermute | solution.py:572
  358.2 197.5 %reduce-scatter.8.cloned.1.call-start = ((), (), s32[]{:S(2)}) async-start(), calls=%async_computation.9 | async-start | bytes 5242880 | tf_op jit(solution)/shard_map/reduce_scatter | solution.py:72
  375.1 33.8 %collective-permute-start.46 = (bf16[256,2048]{1,0:T(8,128)(2,1)S(1)}, bf16[256,2048]{1,0:T(8,128)(2,1)S(1)}, u32[]{:S(2)}, u32[]{:S(2)}) collective-permute-start(bf16[256,2048]{1,0:T(8,128)(2,1)S(1)} %get-tuple-element.187), channel_id=1, source_target_pairs={{0,4},{4,0},{8,12},{12,8},{16,20},{20,16},{24,28},{28,24},{1,5},{5... | collective-permute-start | bytes 3145736 | tf_op jit(solution)/shard_map/ppermute | solution.py:572
  410.5 26.0 %collective-permute-start.52 = (bf16[256,2048]{1,0:T(8,128)(2,1)S(1)}, bf16[256,2048]{1,0:T(8,128)(2,1)S(1)}, u32[]{:S(2)}, u32[]{:S(2)}) collective-permute-start(bf16[256,2048]{1,0:T(8,128)(2,1)S(1)} %collective-permute-done.51.da0.refs_6_), channel_id=1, source_target_pairs={{0,4},{4,0},{8,12},{12,8},{16,20},{20,16},{24,28},{28,24},{1,5},{5... | collective-permute-start | bytes 3145736 | tf_op jit(solution)/shard_map/ppermute | solution.py:572
  424.6 47.1 %collective-permute-start.48 = (bf16[256,2048]{1,0:T(8,128)(2,1)S(1)}, bf16[256,2048]{1,0:T(8,128)(2,1)S(1)}, u32[]{:S(2)}, u32[]{:S(2)}) collective-permute-start(bf16[256,2048]{1,0:T(8,128)(2,1)S(1)} %pad_maximum_fusion.8), channel_id=1, source_target_pairs={{0,16},{4,20},{8,24},{12,28},{16,0},{20,4},{24,8},{28,12},{1,17},{... | collective-permute-start | bytes 3145736 | tf_op jit(solution)/shard_map/ppermute | solution.py:572
  435.3 37.4 %collective-permute-start.45 = (bf16[256,2048]{1,0:T(8,128)(2,1)S(1)}, bf16[256,2048]{1,0:T(8,128)(2,1)}, u32[]{:S(2)}, u32[]{:S(2)}) collective-permute-start(bf16[256,2048]{1,0:T(8,128)(2,1)S(1)} %pad_maximum_fusion.7), channel_id=1, source_target_pairs={{0,8},{4,12},{8,0},{12,4},{16,24},{20,28},{24,16},{28,20},{1,9},{5... | collective-permute-start | bytes 3145736 | tf_op jit(solution)/shard_map/ppermute | solution.py:572
  472.7 172.0 %all-gather.15.cloned.1.call-start = ((), (), s32[]{:S(2)}) async-start(), calls=%async_computation.10 | async-start | bytes 7741440 | tf_op jit(solution)/shard_map/all_gather | solution.py:873
  493.4 26.4 %collective-permute-start.60 = (bf16[256,2048]{1,0:T(8,128)(2,1)}, bf16[256,2048]{1,0:T(8,128)(2,1)}, u32[]{:S(2)}, u32[]{:S(2)}) collective-permute-start(bf16[256,2048]{1,0:T(8,128)(2,1)} %pad_maximum_fusion.9), channel_id=1, source_target_pairs={{0,8},{4,12},{8,0},{12,4},{16,24},{20,28},{24,16},{28,20},{1,9},{5... | collective-permute-start | bytes 3145736 | tf_op jit(solution)/shard_map/ppermute | solution.py:572
  497.3 26.4 %collective-permute-start.64 = (bf16[256,2048]{1,0:T(8,128)(2,1)}, bf16[256,2048]{1,0:T(8,128)(2,1)}, u32[]{:S(2)}, u32[]{:S(2)}) collective-permute-start(bf16[256,2048]{1,0:T(8,128)(2,1)} %pad_maximum_fusion.10), channel_id=1, source_target_pairs={{0,16},{4,20},{8,24},{12,28},{16,0},{20,4},{24,8},{28,12},{1,17},{... | collective-permute-start | bytes 3145736 | tf_op jit(solution)/shard_map/ppermute | solution.py:572
  502.2 49.7 %collective-permute-start.65 = (bf16[768,1024]{1,0:T(8,128)(2,1)S(1)}, bf16[768,1024]{1,0:T(8,128)(2,1)S(1)}, u32[]{:S(2)}, u32[]{:S(2)}) collective-permute-start(bf16[768,1024]{1,0:T(8,128)(2,1)S(1)} %pad_maximum_fusion.1.refs_0_), channel_id=1, source_target_pairs={{0,8},{4,12},{8,0},{12,4},{16,24},{20,28},{24,16},{28,20},{1,9},{5... | collective-permute-start | bytes 4718600 | tf_op jit(solution)/shard_map/ppermute | solution.py:572
  503.1 52.6 %collective-permute-start.66 = (bf16[768,1024]{1,0:T(8,128)(2,1)S(1)}, bf16[768,1024]{1,0:T(8,128)(2,1)}, u32[]{:S(2)}, u32[]{:S(2)}) collective-permute-start(bf16[768,1024]{1,0:T(8,128)(2,1)S(1)} %pad_maximum_fusion.1.refs_0_), channel_id=1, source_target_pairs={{0,16},{4,20},{8,24},{12,28},{16,0},{20,4},{24,8},{28,12},{1,17},{... | collective-permute-start | bytes 4718600 | tf_op jit(solution)/shard_map/ppermute | solution.py:572
  558.0 27.1 %collective-permute-start.69 = (bf16[384,1024]{1,0:T(8,128)(2,1)S(1)}, bf16[384,1024]{1,0:T(8,128)(2,1)S(1)}, u32[]{:S(2)}, u32[]{:S(2)}) collective-permute-start(bf16[384,1024]{1,0:T(8,128)(2,1)S(1)} %slice.503), channel_id=1, source_target_pairs={{0,16},{4,20},{8,24},{12,28},{16,0},{20,4},{24,8},{28,12},{1,17},{... | collective-permute-start | bytes 2359304 | tf_op jit(solution)/shard_map/ppermute | solution.py:572
  560.2 26.8 %collective-permute-start.70 = (bf16[384,1024]{1,0:T(8,128)(2,1)S(1)}, bf16[384,1024]{1,0:T(8,128)(2,1)S(1)}, u32[]{:S(2)}, u32[]{:S(2)}) collective-permute-start(bf16[384,1024]{1,0:T(8,128)(2,1)S(1)} %slice.504), channel_id=1, source_target_pairs={{0,8},{4,12},{8,0},{12,4},{16,24},{20,28},{24,16},{28,20},{1,9},{5... | collective-permute-start | bytes 2359304 | tf_op jit(solution)/shard_map/ppermute | solution.py:572
  561.3 50.8 %collective-permute-start.77 = (bf16[768,1024]{1,0:T(8,128)(2,1)S(1)}, bf16[768,1024]{1,0:T(8,128)(2,1)S(1)}, u32[]{:S(2)}, u32[]{:S(2)}) collective-permute-start(bf16[768,1024]{1,0:T(8,128)(2,1)S(1)} %pad_maximum_fusion.1.refs_0_), channel_id=1, source_target_pairs={{0,4},{4,0},{8,12},{12,8},{16,20},{20,16},{24,28},{28,24},{1,5},{5... | collective-permute-start | bytes 4718600 | tf_op jit(solution)/shard_map/ppermute | solution.py:572
  561.3 52.1 %collective-permute-start.78 = (bf16[768,1024]{1,0:T(8,128)(2,1)S(1)}, bf16[768,1024]{1,0:T(8,128)(2,1)}, u32[]{:S(2)}, u32[]{:S(2)}) collective-permute-start(bf16[768,1024]{1,0:T(8,128)(2,1)S(1)} %collective-permute-done.65.refs_2_), channel_id=1, source_target_pairs={{0,4},{4,0},{8,12},{12,8},{16,20},{20,16},{24,28},{28,24},{1,5},{5... | collective-permute-start | bytes 4718600 | tf_op jit(solution)/shard_map/ppermute | solution.py:572
  561.8 51.6 %collective-permute-start.79 = (bf16[768,1024]{1,0:T(8,128)(2,1)}, bf16[768,1024]{1,0:T(8,128)(2,1)}, u32[]{:S(2)}, u32[]{:S(2)}) collective-permute-start(bf16[768,1024]{1,0:T(8,128)(2,1)} %collective-permute-done.66.refs_4_), channel_id=1, source_target_pairs={{0,4},{4,0},{8,12},{12,8},{16,20},{20,16},{24,28},{28,24},{1,5},{5... | collective-permute-start | bytes 4718600 | tf_op jit(solution)/shard_map/ppermute | solution.py:572
  589.4 41.6 %collective-permute-start.73 = (bf16[512,256]{1,0:T(8,128)(2,1)}, bf16[512,256]{1,0:T(8,128)(2,1)S(1)}, u32[]{:S(2)}, u32[]{:S(2)}) collective-permute-start(bf16[512,256]{1,0:T(8,128)(2,1)} %collective-permute-done.71.refs_0_), channel_id=1, source_target_pairs={{0,8},{4,12},{8,0},{12,4},{16,24},{20,28},{24,16},{28,20},{1,9},{5... | collective-permute-start | bytes 786440 | tf_op jit(solution)/shard_map/ppermute | solution.py:572
  (194 other events, 1738.2 us)
Sparse Core Ops, SparseCore 0:
  13.3 78.1 all-gather.6
  93.6 29.3 all-gather.8
  149.1 80.3 all-gather.10
  230.9 44.5 all-gather.12
  292.9 43.2 reduce-scatter.3
  358.3 75.9 reduce-scatter.5
  472.8 78.7 reduce-scatter.7
  558.1 67.7 all-gather.14

commit v4 on v3

--- a/solution.py
+++ b/solution.py
@@ -695,9 +695,8 @@
             for src in range(shards)
         ]
         back = [(target, source) for source, target in there]
-        first_row = lax.rem(rep, per_plane) * cols + lax.div(rep, per_plane) * out_rows
-        out_piece = lax.dynamic_slice(w_output, (first_row, 0), (out_rows, width))
-        out_piece = lax.ppermute(out_piece, ("rep", "shard"), there)
+        own_rows = lax.dynamic_slice(w_output, (lax.rem(rep, per_plane) * cols, 0), (cols, width))
+        own_rows = jnp.where(lax.axis_index("shard") == lax.div(rep, per_plane), own_rows, jnp.zeros_like(own_rows))
         w_qkv = gather(own_columns((w_query, w_key, w_value), rep, cols), "shard")
 
         stream = tokens.astype(F32)
@@ -722,9 +721,9 @@
         for m in [0] + ring.links:
             first.core(m)
         blocks = first.blocks()
-        w_out = gather(after(out_piece, w_qkv), "shard")
+        w_out = lax.psum(after(own_rows, w_qkv), "shard")
         second = ring.gathering(grad_moe_own)
-        second.near(blocks[ring.links[-1]])
+        second.near(w_qkv)
 
         cosine, sine = rotary_tables(length, head_size)
         cosine = jnp.concatenate([cosine, cosine], axis=1)

time: 670 us -> 666 us (level)
  starting transfers between devices: 89.8 us -> 82.6 us
    psum x0 -> x1, waiting for transfers between devices: none -> 16.1 us  [body(): w_out = lax.psum(after(own_rows, w_qkv), 'shard')]
    ppermute x80, waiting for transfers between devices: 218 us -> 202 us  [swap(): return lax.ppermute(piece, 'rep', [(i, i ^ bit) for i in range(self.reps)])]
    all_gather x4 -> x3, waiting for transfers between devices: 20 us -> 12 us  [gather(): return lax.all_gather(piece, axis, axis=dim, tiled=True)]
    unnamed x271 -> x269, local copies, waits for them, and re-layouts: 73.1 us -> 77.4 us
  transfers between devices with their start and end apart: 92 -> 91, of which waited for: 35 -> 34; matrix products, arithmetic and copies ran while one was open for 10% -> 11% of each run, Pallas kernels for 23% -> 23%
where the time goes in v4:
time: 666 us; the launch traced here: 660 us
  waiting for transfers between devices  243 us (36%)
  Pallas kernels  166 us (25%)
  local copies, waits for them, and re-layouts  97.4 us (15%)
  starting transfers between devices  82.6 us (12%)
  other arithmetic  50.6 us (8%)
  between operations  16.6 us (2%)
    ppermute x80, waiting for transfers between devices, swap(): return lax.ppermute(piece, 'rep', [(i, i ^ bit) for i in range(self.reps)])  202 us
    unnamed x269, local copies, waits for them, and re-layouts  77.4 us
    ppermute x80, starting transfers between devices, swap(): return lax.ppermute(piece, 'rep', [(i, i ^ bit) for i in range(self.reps)])  76.8 us
    pallas_call x4, Pallas kernels, attend_back(): pl.pallas_call(functools.partial(attend_back_kernel, length, score_scale)...  33 us
    pallas_call x3, Pallas kernels, weight_grad(): pl.pallas_call(functools.partial(weight_grad_kernel, len(left)), grid=(ou...  22.4 us
    pallas_call x4, Pallas kernels, attend(): pl.pallas_call(functools.partial(attend_kernel, length, score_scale), gri...  21.9 us
    pallas_call x4, Pallas kernels, expert_back(): pl.pallas_call(functools.partial(expert_back_kernel, length), grid=(1,),...  21.6 us
    pallas_call x4, Pallas kernels, expert_in(): pl.pallas_call(functools.partial(expert_in_kernel, length, experts), grid...  19.2 us
  transfers between devices with their start and end apart: 91, of which 34 were waited for; matrix products, arithmetic and copies ran while one was open for 11% of the time, Pallas kernels for 23%

profile of v4, /device:TPU:0, one launch (start us, length us, event | category | flops | bytes accessed | tf_op | source)
XLA Modules:
  0.0 660.1 jit_solution(6638506815063277661)
XLA Ops:
  29.0 13.6 %collective-permute-done.6.blk0.ids0.refs_4_ = bf16[272,2048]{1,0:T(8,128)(2,1)} collective-permute-done((bf16[272,2048]{1,0:T(8,128)(2,1)S(1)}, bf16[272,2048]{1,0:T(8,128)(2,1)}, u32[]{:S(2)}, u32[]{:S(2)}) %collective-permute-start.6) | collective-permute-done | bytes 1114144 | tf_op jit(solution)/shard_map/ppermute | solution.py:572
  48.8 10.1 %collective-permute-done.7 = bf16[128,2048]{1,0:T(8,128)(2,1)S(1)} collective-permute-done((bf16[128,2048]{1,0:T(8,128)(2,1)}, bf16[128,2048]{1,0:T(8,128)(2,1)S(1)}, u32[]{:S(2)}, u32[]{:S(2)}) %collective-permute-start.7) | collective-permute-done | bytes 524320 | tf_op jit(solution)/shard_map/ppermute | solution.py:572
  67.4 12.0 %all-gather.6.cloned.1.call-done.w_qkv.refs_13_ = bf16[2048,768]{1,0:T(8,128)(2,1)} async-done(((bf16[512,768]{1,0:T(8,128)(2,1)}), bf16[2048,768]{1,0:T(8,128)(2,1)}) %all-gather.6.cloned.1.call-update) | async-done | bytes 3145744 | tf_op jit(solution)/shard_map/all_gather | solution.py:68
  85.4 5.6 attend.6
  92.1 5.4 attend.5
  98.7 5.4 attend.7
  105.3 5.6 attend.4
  116.7 16.1 %all-reduce.6.cloned.1.call-done.w_out = bf16[256,2048]{1,0:T(8,128)(2,1)} async-done(((bf16[256,2048]{1,0:T(8,128)(2,1)}), bf16[256,2048]{1,0:T(8,128)(2,1)}) %all-reduce.6.cloned.1.call-update) | async-done | bytes 1048592 | tf_op jit(solution)/shard_map/psum | solution.py:724
  149.0 8.9 %collective-permute-done.15 = bf16[128,2048]{1,0:T(8,128)(2,1)S(1)} collective-permute-done((bf16[128,2048]{1,0:T(8,128)(2,1)S(1)}, bf16[128,2048]{1,0:T(8,128)(2,1)S(1)}, u32[]{:S(2)}, u32[]{:S(2)}) %collective-permute-start.15) | collective-permute-done | bytes 524320 | tf_op jit(solution)/shard_map/ppermute | solution.py:572
  163.2 20.9 %collective-permute-done.16 = bf16[256,2048]{1,0:T(8,128)(2,1)S(1)} collective-permute-done((bf16[256,2048]{1,0:T(8,128)(2,1)S(1)}, bf16[256,2048]{1,0:T(8,128)(2,1)S(1)}, u32[]{:S(2)}, u32[]{:S(2)}) %collective-permute-start.16) | collective-permute-done | bytes 1048608 | tf_op jit(solution)/shard_map/ppermute | solution.py:572
  191.2 21.7 %collective-permute-done.25.b0.refs_2_ = bf16[256,2048]{1,0:T(8,128)(2,1)} collective-permute-done((bf16[256,2048]{1,0:T(8,128)(2,1)S(1)}, bf16[256,2048]{1,0:T(8,128)(2,1)}, u32[]{:S(2)}, u32[]{:S(2)}) %collective-permute-start.25) | collective-permute-done | bytes 1048608 | tf_op jit(solution)/shard_map/ppermute | solution.py:572
  218.1 8.3 %collective-permute-done.29 = bf16[128,2048]{1,0:T(8,128)(2,1)} collective-permute-done((bf16[128,2048]{1,0:T(8,128)(2,1)}, bf16[128,2048]{1,0:T(8,128)(2,1)}, u32[]{:S(2)}, u32[]{:S(2)}) %collective-permute-start.29) | collective-permute-done | bytes 524320 | tf_op jit(solution)/shard_map/ppermute | solution.py:572
  262.2 7.1 %down_grad.1 = bf16[512,2048]{1,0:T(8,128)(2,1)S(1)} custom-call(bf16[512,512]{1,0:T(8,128)(2,1)S(1)} %get-tuple-element.176.refs_0_.mixed, bf16[512,512]{1,0:T(8,128)(2,1)S(1)} %get-tuple-element.179.refs_1_.mixed, bf16[512,512]{1,0:T(8,128)(2,1)S(1)} %get-tuple-element.185.refs_2_.mixed, bf16[512,512]{1,0:T(8,128)(2,1)S(1)} %get-tuple-element.182.refs_3_.mixed, ...), custom_call_target="tpu_custom_call" | custom-call | flops 4294967296 | bytes 12582912 | tf_op jit(solution)/shard_map/down_grad/pallas_call | solution.py:338
  276.9 6.1 expert_back.5
  291.7 5.2 expert_back.4
  325.8 12.1 %up_grad.1 = bf16[2048,1024]{1,0:T(8,128)(2,1)S(1)} custom-call(bf16[256,2048]{1,0:T(8,128)(2,1)S(1)} %multiply_convert_fusion.1.b0.refs_0_, bf16[256,2048]{1,0:T(8,128)(2,1)} %collective-permute-done.24.b1.refs_1_, bf16[256,2048]{1,0:T(8,128)(2,1)} %collective-permute-done.25.b0.refs_2_, bf16[256,2048]{1,0:T(8,128)(2,1)} %collective-permute-done.26.b1.refs_3_, ...), custom_call_target="tpu_custom_call" | custom-call | flops 8589934592 | bytes 16777216 | tf_op jit(solution)/shard_map/up_grad/pallas_call | solution.py:338
  340.8 10.1 %collective-permute-done.39 = bf16[272,2048]{1,0:T(8,128)(2,1)} collective-permute-done((bf16[272,2048]{1,0:T(8,128)(2,1)}, bf16[272,2048]{1,0:T(8,128)(2,1)}, u32[]{:S(2)}, u32[]{:S(2)}) %collective-permute-start.39) | collective-permute-done | bytes 1114144 | tf_op jit(solution)/shard_map/ppermute | solution.py:572
  369.9 17.9 %collective-permute-done.50.da0.refs_6_ = bf16[256,2048]{1,0:T(8,128)(2,1)S(1)} collective-permute-done((bf16[256,2048]{1,0:T(8,128)(2,1)S(1)}, bf16[256,2048]{1,0:T(8,128)(2,1)S(1)}, u32[]{:S(2)}, u32[]{:S(2)}) %collective-permute-start.50) | collective-permute-done | bytes 1048608 | tf_op jit(solution)/shard_map/ppermute | solution.py:572
  393.5 8.6 %attend_back.4 = (bf16[256,2048]{1,0:T(8,128)(2,1)S(1)}, bf16[256,2048]{1,0:T(8,128)(2,1)}, bf16[512,768]{1,0:T(8,128)(2,1)S(1)}, f32[8,128]{1,0:T(8,128)S(1)}) custom-call(bf16[256,2048]{1,0:T(8,128)(2,1)S(1)} %get-tuple-element.239.da0.refs_4_, bf16[256,2048]{1,0:T(8,128)(2,1)S(1)} %collective-permute-done.48.da1.refs_5_, ...), custom_call_target="tpu_custom_call" | custom-call | flops 3221225472 | bytes 13243392 | tf_op jit(solution)/shard_map/attend_back/pallas_call | solution.py:199
  404.3 11.8 %collective-permute-done.55 = bf16[128,2048]{1,0:T(8,128)(2,1)S(1)} collective-permute-done((bf16[128,2048]{1,0:T(8,128)(2,1)S(1)}, bf16[128,2048]{1,0:T(8,128)(2,1)S(1)}, u32[]{:S(2)}, u32[]{:S(2)}) %collective-permute-start.55) | collective-permute-done | bytes 524320 | tf_op jit(solution)/shard_map/ppermute | solution.py:572
  420.3 7.3 %attend_back.6 = (bf16[256,2048]{1,0:T(8,128)(2,1)S(1)}, bf16[256,2048]{1,0:T(8,128)(2,1)S(1)}, bf16[512,768]{1,0:T(8,128)(2,1)S(1)}, f32[8,128]{1,0:T(8,128)S(1)}) custom-call(bf16[256,2048]{1,0:T(8,128)(2,1)S(1)} %constant_dynamic-update-slice_fusion.6.da0.refs_10_, bf16[256,2048]{1,0:T(8,128)(2,1)S(1)} %collective-permute-done.56.da1.refs_11_, ...), custom_call_target="tpu_custom_call" | custom-call | flops 3221225472 | bytes 13243392 | tf_op jit(solution)/shard_map/attend_back/pallas_call | solution.py:199
  429.4 8.8 %attend_back.5 = (bf16[256,2048]{1,0:T(8,128)(2,1)S(1)}, bf16[256,2048]{1,0:T(8,128)(2,1)}, bf16[512,768]{1,0:T(8,128)(2,1)S(1)}, f32[8,128]{1,0:T(8,128)S(1)}) custom-call(bf16[256,2048]{1,0:T(8,128)(2,1)S(1)} %collective-permute-done.50.da0.refs_6_, bf16[256,2048]{1,0:T(8,128)(2,1)S(1)} %collective-permute-done.51.da1.refs_7_, ...), custom_call_target="tpu_custom_call" | custom-call | flops 3221225472 | bytes 13243392 | tf_op jit(solution)/shard_map/attend_back/pallas_call | solution.py:199
  439.2 8.3 %attend_back.7 = (bf16[256,2048]{1,0:T(8,128)(2,1)S(1)}, bf16[256,2048]{1,0:T(8,128)(2,1)}, bf16[512,768]{1,0:T(8,128)(2,1)S(1)}, f32[8,128]{1,0:T(8,128)S(1)}) custom-call(bf16[256,2048]{1,0:T(8,128)(2,1)S(1)} %collective-permute-done.54.da0.refs_8_, bf16[256,2048]{1,0:T(8,128)(2,1)S(1)} %collective-permute-done.60.da1.refs_9_, ...), custom_call_target="tpu_custom_call" | custom-call | flops 3221225472 | bytes 13243392 | tf_op jit(solution)/shard_map/attend_back/pallas_call | solution.py:199
  452.8 10.7 %attention_grad.1 = (bf16[2048,1024]{1,0:T(8,128)(2,1)S(1)}, f32[2048,1]{1,0:T(8,128)S(1)}) custom-call(bf16[272,2048]{1,0:T(8,128)(2,1)S(1)} %pad_maximum_fusion.2.blk0.ids0.refs_0_, bf16[272,2048]{1,0:T(8,128)(2,1)} %collective-permute-done.blk1.ids1.refs_1_, bf16[272,2048]{1,0:T(8,128)(2,1)} %collective-permute-done.2.blk0.ids0.refs_2_, ...), custom_call_target="tpu_custom_call" | custom-call | flops 6442450944 | bytes 16261120 | tf_op jit(solution)/shard_map/attention_grad/pallas_call | solution.py:369
  476.4 9.0 %collective-permute-done.58 = bf16[128,2048]{1,0:T(8,128)(2,1)S(1)} collective-permute-done((bf16[128,2048]{1,0:T(8,128)(2,1)}, bf16[128,2048]{1,0:T(8,128)(2,1)S(1)}, u32[]{:S(2)}, u32[]{:S(2)}) %collective-permute-start.58) | collective-permute-done | bytes 524320 | tf_op jit(solution)/shard_map/ppermute | solution.py:572
  500.1 15.5 %collective-permute-done.59 = bf16[256,2048]{1,0:T(8,128)(2,1)} collective-permute-done((bf16[256,2048]{1,0:T(8,128)(2,1)}, bf16[256,2048]{1,0:T(8,128)(2,1)}, u32[]{:S(2)}, u32[]{:S(2)}) %collective-permute-start.59) | collective-permute-done | bytes 1048608 | tf_op jit(solution)/shard_map/ppermute | solution.py:572
  536.4 8.2 %collective-permute-done.67 = f32[99,128]{1,0:T(8,128)S(1)} collective-permute-done((f32[99,128]{1,0:T(8,128)S(1)}, f32[99,128]{1,0:T(8,128)S(1)}, u32[]{:S(2)}, u32[]{:S(2)}) %collective-permute-start.67) | collective-permute-done | bytes 50720 | tf_op jit(solution)/shard_map/ppermute | solution.py:62
  557.5 23.5 %collective-permute-done.68 = bf16[384,1024]{1,0:T(8,128)(2,1)S(1)} collective-permute-done((bf16[384,1024]{1,0:T(8,128)(2,1)S(1)}, bf16[384,1024]{1,0:T(8,128)(2,1)S(1)}, u32[]{:S(2)}, u32[]{:S(2)}) %collective-permute-start.68) | collective-permute-done | bytes 786464 | tf_op jit(solution)/shard_map/ppermute | solution.py:572
  585.3 22.2 %collective-permute-start.72 = (bf16[512,256]{1,0:T(8,128)(2,1)}, bf16[512,256]{1,0:T(8,128)(2,1)S(1)}, u32[]{:S(2)}, u32[]{:S(2)}) collective-permute-start(bf16[512,256]{1,0:T(8,128)(2,1)} %collective-permute-done.70.refs_0_), channel_id=1, source_target_pairs={{0,8},{4,12},{8,0},{12,4},{16,24},{20,28},{24,16},{28,20},{1,9},{5... | collective-permute-start | bytes 786440 | tf_op jit(solution)/shard_map/ppermute | solution.py:572
  610.3 5.5 place_down.1
  615.8 10.6 %place_units.1 = (f32[4,512,1024]{2,1,0:T(8,128)}, f32[4,512,1024]{2,1,0:T(8,128)}) custom-call(s32[16]{0:T(128)S(1)} %reshape.156.place, bf16[768,1024]{1,0:T(8,128)(2,1)S(1)} %pad_maximum_fusion.1.refs_0_, bf16[768,1024]{1,0:T(8,128)(2,1)S(1)} %copy-done.6, bf16[768,1024]{1,0:T(8,128)(2,1)S(1)} %collective-permute-done.64.refs_2_, ...), custom_call_target="tpu_custom_call" | custom-call | bytes 33554432 | tf_op jit(solution)/shard_map/place_units/pallas_call | solution.py:480
  644.3 5.2 place_columns.1
  (577 shorter events, 296.2 us)
Async XLA Ops:
  7.2 72.2 %all-gather.6.cloned.1.call-start = ((), (), s32[]{:S(2)}) async-start(), calls=%async_computation.3 | async-start | bytes 3932160 | tf_op jit(solution)/shard_map/all_gather | solution.py:68
  13.0 119.8 %all-reduce.6.cloned.1.call-start = ((), (), s32[]{:S(2)}) async-start(), calls=%async_computation.4 | async-start | bytes 2097152 | tf_op jit(solution)/shard_map/psum | solution.py:724
  14.9 27.7 %collective-permute-start.6 = (bf16[272,2048]{1,0:T(8,128)(2,1)S(1)}, bf16[272,2048]{1,0:T(8,128)(2,1)}, u32[]{:S(2)}, u32[]{:S(2)}) collective-permute-start(bf16[272,2048]{1,0:T(8,128)(2,1)S(1)} %pad_maximum_fusion.2.blk0.ids0.refs_0_), channel_id=1, source_target_pairs={{0,16},{4,20},{8,24},{12,28},{16,0},{20,4},{24,8},{28,12},{1,17},{... | collective-permute-start | bytes 3342344 | tf_op jit(solution)/shard_map/ppermute | solution.py:572
  17.9 26.1 %collective-permute-start.2 = (bf16[272,2048]{1,0:T(8,128)(2,1)S(1)}, bf16[272,2048]{1,0:T(8,128)(2,1)}, u32[]{:S(2)}, u32[]{:S(2)}) collective-permute-start(bf16[272,2048]{1,0:T(8,128)(2,1)S(1)} %pad_maximum_fusion.2.blk0.ids0.refs_0_), channel_id=1, source_target_pairs={{0,8},{4,12},{8,0},{12,4},{16,24},{20,28},{24,16},{28,20},{1,9},{5... | collective-permute-start | bytes 3342344 | tf_op jit(solution)/shard_map/ppermute | solution.py:572
  62.1 43.1 %collective-permute-start = (bf16[272,2048]{1,0:T(8,128)(2,1)S(1)}, bf16[272,2048]{1,0:T(8,128)(2,1)}, u32[]{:S(2)}, u32[]{:S(2)}) collective-permute-start(bf16[272,2048]{1,0:T(8,128)(2,1)S(1)} %pad_maximum_fusion.2.blk0.ids0.refs_0_), channel_id=1, source_target_pairs={{0,4},{4,0},{8,12},{12,8},{16,20},{20,16},{24,28},{28,24},{1,5},{5... | collective-permute-start | bytes 3342344 | tf_op jit(solution)/shard_map/ppermute | solution.py:572
  63.2 28.9 %collective-permute-start.3 = (bf16[272,2048]{1,0:T(8,128)(2,1)}, bf16[272,2048]{1,0:T(8,128)(2,1)}, u32[]{:S(2)}, u32[]{:S(2)}) collective-permute-start(bf16[272,2048]{1,0:T(8,128)(2,1)} %collective-permute-done.2.blk0.ids0.refs_2_), channel_id=1, source_target_pairs={{0,4},{4,0},{8,12},{12,8},{16,20},{20,16},{24,28},{28,24},{1,5},{5... | collective-permute-start | bytes 3342344 | tf_op jit(solution)/shard_map/ppermute | solution.py:572
  64.4 34.3 %collective-permute-start.10 = (bf16[272,2048]{1,0:T(8,128)(2,1)}, bf16[272,2048]{1,0:T(8,128)(2,1)}, u32[]{:S(2)}, u32[]{:S(2)}) collective-permute-start(bf16[272,2048]{1,0:T(8,128)(2,1)} %collective-permute-done.6.blk0.ids0.refs_4_), channel_id=1, source_target_pairs={{0,4},{4,0},{8,12},{12,8},{16,20},{20,16},{24,28},{28,24},{1,5},{5... | collective-permute-start | bytes 3342344 | tf_op jit(solution)/shard_map/ppermute | solution.py:572
  79.4 33.3 %collective-permute-start.4 = (bf16[256,2048]{1,0:T(8,128)(2,1)}, bf16[256,2048]{1,0:T(8,128)(2,1)}, u32[]{:S(2)}, u32[]{:S(2)}) collective-permute-start(bf16[256,2048]{1,0:T(8,128)(2,1)} %broadcast_select_fusion.refs_4_.c0), channel_id=1, source_target_pairs={{0,8},{4,12},{8,0},{12,4},{16,24},{20,28},{24,16},{28,20},{1,9},{5... | collective-permute-start | bytes 3145736 | tf_op jit(solution)/shard_map/ppermute | solution.py:572
  80.9 33.7 %collective-permute-start.5 = (bf16[256,2048]{1,0:T(8,128)(2,1)}, bf16[256,2048]{1,0:T(8,128)(2,1)}, u32[]{:S(2)}, u32[]{:S(2)}) collective-permute-start(bf16[256,2048]{1,0:T(8,128)(2,1)} %broadcast_select_fusion.refs_4_.c0), channel_id=1, source_target_pairs={{0,16},{4,20},{8,24},{12,28},{16,0},{20,4},{24,8},{28,12},{1,17},{... | collective-permute-start | bytes 3145736 | tf_op jit(solution)/shard_map/ppermute | solution.py:572
  82.9 148.5 %all-gather.8.cloned.1.call-start = ((), (), s32[]{:S(2)}) async-start(), calls=%async_computation.5 | async-start | bytes 5242880 | tf_op jit(solution)/shard_map/all_gather | solution.py:68
  141.8 129.7 %all-gather.10.cloned.1.call-start = ((), (), s32[]{:S(2)}) async-start(), calls=%async_computation.6 | async-start | bytes 2621440 | tf_op jit(solution)/shard_map/all_gather | solution.py:68
  215.4 135.6 %reduce-scatter.4.cloned.1.call-start = ((), (), s32[]{:S(2)}) async-start(), calls=%async_computation.7 | async-start | bytes 2621440 | tf_op jit(solution)/shard_map/reduce_scatter | solution.py:72
  229.2 26.0 %collective-permute-start.24 = (bf16[256,2048]{1,0:T(8,128)(2,1)S(1)}, bf16[256,2048]{1,0:T(8,128)(2,1)}, u32[]{:S(2)}, u32[]{:S(2)}) collective-permute-start(bf16[256,2048]{1,0:T(8,128)(2,1)S(1)} %multiply_convert_fusion.1.b0.refs_0_), channel_id=1, source_target_pairs={{0,4},{4,0},{8,12},{12,8},{16,20},{20,16},{24,28},{28,24},{1,5},{5... | collective-permute-start | bytes 3145736 | tf_op jit(solution)/shard_map/ppermute | solution.py:572
  285.2 182.2 %reduce-scatter.6.cloned.1.call-start = ((), (), s32[]{:S(2)}) async-start(), calls=%async_computation.8 | async-start | bytes 5242880 | tf_op jit(solution)/shard_map/reduce_scatter | solution.py:72
  314.2 26.7 %collective-permute-start.37 = (bf16[272,2048]{1,0:T(8,128)(2,1)}, bf16[272,2048]{1,0:T(8,128)(2,1)}, u32[]{:S(2)}, u32[]{:S(2)}) collective-permute-start(bf16[272,2048]{1,0:T(8,128)(2,1)} %pad_maximum_fusion.3), channel_id=1, source_target_pairs={{0,8},{4,12},{8,0},{12,4},{16,24},{20,28},{24,16},{28,20},{1,9},{5... | collective-permute-start | bytes 3342344 | tf_op jit(solution)/shard_map/ppermute | solution.py:572
  323.6 27.3 %collective-permute-start.39 = (bf16[272,2048]{1,0:T(8,128)(2,1)}, bf16[272,2048]{1,0:T(8,128)(2,1)}, u32[]{:S(2)}, u32[]{:S(2)}) collective-permute-start(bf16[272,2048]{1,0:T(8,128)(2,1)} %pad_maximum_fusion.4), channel_id=1, source_target_pairs={{0,16},{4,20},{8,24},{12,28},{16,0},{20,4},{24,8},{28,12},{1,17},{... | collective-permute-start | bytes 3342344 | tf_op jit(solution)/shard_map/ppermute | solution.py:572
  350.9 200.8 %reduce-scatter.8.cloned.1.call-start = ((), (), s32[]{:S(2)}) async-start(), calls=%async_computation.9 | async-start | bytes 5242880 | tf_op jit(solution)/shard_map/reduce_scatter | solution.py:72
  368.2 34.8 %collective-permute-start.45 = (bf16[256,2048]{1,0:T(8,128)(2,1)S(1)}, bf16[256,2048]{1,0:T(8,128)(2,1)S(1)}, u32[]{:S(2)}, u32[]{:S(2)}) collective-permute-start(bf16[256,2048]{1,0:T(8,128)(2,1)S(1)} %get-tuple-element.187), channel_id=1, source_target_pairs={{0,4},{4,0},{8,12},{12,8},{16,20},{20,16},{24,28},{28,24},{1,5},{5... | collective-permute-start | bytes 3145736 | tf_op jit(solution)/shard_map/ppermute | solution.py:572
  417.4 49.1 %collective-permute-start.47 = (bf16[256,2048]{1,0:T(8,128)(2,1)S(1)}, bf16[256,2048]{1,0:T(8,128)(2,1)S(1)}, u32[]{:S(2)}, u32[]{:S(2)}) collective-permute-start(bf16[256,2048]{1,0:T(8,128)(2,1)S(1)} %pad_maximum_fusion.8), channel_id=1, source_target_pairs={{0,16},{4,20},{8,24},{12,28},{16,0},{20,4},{24,8},{28,12},{1,17},{... | collective-permute-start | bytes 3145736 | tf_op jit(solution)/shard_map/ppermute | solution.py:572
  427.9 39.5 %collective-permute-start.44 = (bf16[256,2048]{1,0:T(8,128)(2,1)S(1)}, bf16[256,2048]{1,0:T(8,128)(2,1)}, u32[]{:S(2)}, u32[]{:S(2)}) collective-permute-start(bf16[256,2048]{1,0:T(8,128)(2,1)S(1)} %pad_maximum_fusion.7), channel_id=1, source_target_pairs={{0,8},{4,12},{8,0},{12,4},{16,24},{20,28},{24,16},{28,20},{1,9},{5... | collective-permute-start | bytes 3145736 | tf_op jit(solution)/shard_map/ppermute | solution.py:572
  467.5 172.6 %all-gather.12.cloned.1.call-start = ((), (), s32[]{:S(2)}) async-start(), calls=%async_computation.10 | async-start | bytes 7741440 | tf_op jit(solution)/shard_map/all_gather | solution.py:872
  474.5 25.6 %collective-permute-start.49 = (bf16[256,2048]{1,0:T(8,128)(2,1)}, bf16[256,2048]{1,0:T(8,128)(2,1)}, u32[]{:S(2)}, u32[]{:S(2)}) collective-permute-start(bf16[256,2048]{1,0:T(8,128)(2,1)} %get-tuple-element.191), channel_id=1, source_target_pairs={{0,4},{4,0},{8,12},{12,8},{16,20},{20,16},{24,28},{28,24},{1,5},{5... | collective-permute-start | bytes 3145736 | tf_op jit(solution)/shard_map/ppermute | solution.py:572
  489.2 26.4 %collective-permute-start.59 = (bf16[256,2048]{1,0:T(8,128)(2,1)}, bf16[256,2048]{1,0:T(8,128)(2,1)}, u32[]{:S(2)}, u32[]{:S(2)}) collective-permute-start(bf16[256,2048]{1,0:T(8,128)(2,1)} %pad_maximum_fusion.9), channel_id=1, source_target_pairs={{0,8},{4,12},{8,0},{12,4},{16,24},{20,28},{24,16},{28,20},{1,9},{5... | collective-permute-start | bytes 3145736 | tf_op jit(solution)/shard_map/ppermute | solution.py:572
  493.5 26.4 %collective-permute-start.63 = (bf16[256,2048]{1,0:T(8,128)(2,1)}, bf16[256,2048]{1,0:T(8,128)(2,1)}, u32[]{:S(2)}, u32[]{:S(2)}) collective-permute-start(bf16[256,2048]{1,0:T(8,128)(2,1)} %pad_maximum_fusion.10), channel_id=1, source_target_pairs={{0,16},{4,20},{8,24},{12,28},{16,0},{20,4},{24,8},{28,12},{1,17},{... | collective-permute-start | bytes 3145736 | tf_op jit(solution)/shard_map/ppermute | solution.py:572
  498.4 49.2 %collective-permute-start.64 = (bf16[768,1024]{1,0:T(8,128)(2,1)S(1)}, bf16[768,1024]{1,0:T(8,128)(2,1)S(1)}, u32[]{:S(2)}, u32[]{:S(2)}) collective-permute-start(bf16[768,1024]{1,0:T(8,128)(2,1)S(1)} %pad_maximum_fusion.1.refs_0_), channel_id=1, source_target_pairs={{0,8},{4,12},{8,0},{12,4},{16,24},{20,28},{24,16},{28,20},{1,9},{5... | collective-permute-start | bytes 4718600 | tf_op jit(solution)/shard_map/ppermute | solution.py:572
  499.1 52.6 %collective-permute-start.65 = (bf16[768,1024]{1,0:T(8,128)(2,1)S(1)}, bf16[768,1024]{1,0:T(8,128)(2,1)}, u32[]{:S(2)}, u32[]{:S(2)}) collective-permute-start(bf16[768,1024]{1,0:T(8,128)(2,1)S(1)} %pad_maximum_fusion.1.refs_0_), channel_id=1, source_target_pairs={{0,16},{4,20},{8,24},{12,28},{16,0},{20,4},{24,8},{28,12},{1,17},{... | collective-permute-start | bytes 4718600 | tf_op jit(solution)/shard_map/ppermute | solution.py:572
  554.1 26.9 %collective-permute-start.68 = (bf16[384,1024]{1,0:T(8,128)(2,1)S(1)}, bf16[384,1024]{1,0:T(8,128)(2,1)S(1)}, u32[]{:S(2)}, u32[]{:S(2)}) collective-permute-start(bf16[384,1024]{1,0:T(8,128)(2,1)S(1)} %slice.503), channel_id=1, source_target_pairs={{0,16},{4,20},{8,24},{12,28},{16,0},{20,4},{24,8},{28,12},{1,17},{... | collective-permute-start | bytes 2359304 | tf_op jit(solution)/shard_map/ppermute | solution.py:572
  556.3 26.6 %collective-permute-start.69 = (bf16[384,1024]{1,0:T(8,128)(2,1)S(1)}, bf16[384,1024]{1,0:T(8,128)(2,1)S(1)}, u32[]{:S(2)}, u32[]{:S(2)}) collective-permute-start(bf16[384,1024]{1,0:T(8,128)(2,1)S(1)} %slice.504), channel_id=1, source_target_pairs={{0,8},{4,12},{8,0},{12,4},{16,24},{20,28},{24,16},{28,20},{1,9},{5... | collective-permute-start | bytes 2359304 | tf_op jit(solution)/shard_map/ppermute | solution.py:572
  557.0 50.5 %collective-permute-start.76 = (bf16[768,1024]{1,0:T(8,128)(2,1)S(1)}, bf16[768,1024]{1,0:T(8,128)(2,1)S(1)}, u32[]{:S(2)}, u32[]{:S(2)}) collective-permute-start(bf16[768,1024]{1,0:T(8,128)(2,1)S(1)} %pad_maximum_fusion.1.refs_0_), channel_id=1, source_target_pairs={{0,4},{4,0},{8,12},{12,8},{16,20},{20,16},{24,28},{28,24},{1,5},{5... | collective-permute-start | bytes 4718600 | tf_op jit(solution)/shard_map/ppermute | solution.py:572
  557.0 51.9 %collective-permute-start.77 = (bf16[768,1024]{1,0:T(8,128)(2,1)S(1)}, bf16[768,1024]{1,0:T(8,128)(2,1)}, u32[]{:S(2)}, u32[]{:S(2)}) collective-permute-start(bf16[768,1024]{1,0:T(8,128)(2,1)S(1)} %collective-permute-done.64.refs_2_), channel_id=1, source_target_pairs={{0,4},{4,0},{8,12},{12,8},{16,20},{20,16},{24,28},{28,24},{1,5},{5... | collective-permute-start | bytes 4718600 | tf_op jit(solution)/shard_map/ppermute | solution.py:572
  557.5 51.4 %collective-permute-start.78 = (bf16[768,1024]{1,0:T(8,128)(2,1)}, bf16[768,1024]{1,0:T(8,128)(2,1)}, u32[]{:S(2)}, u32[]{:S(2)}) collective-permute-start(bf16[768,1024]{1,0:T(8,128)(2,1)} %collective-permute-done.65.refs_4_), channel_id=1, source_target_pairs={{0,4},{4,0},{8,12},{12,8},{16,20},{20,16},{24,28},{28,24},{1,5},{5... | collective-permute-start | bytes 4718600 | tf_op jit(solution)/shard_map/ppermute | solution.py:572
  585.3 41.1 %collective-permute-start.72 = (bf16[512,256]{1,0:T(8,128)(2,1)}, bf16[512,256]{1,0:T(8,128)(2,1)S(1)}, u32[]{:S(2)}, u32[]{:S(2)}) collective-permute-start(bf16[512,256]{1,0:T(8,128)(2,1)} %collective-permute-done.70.refs_0_), channel_id=1, source_target_pairs={{0,8},{4,12},{8,0},{12,4},{16,24},{20,28},{24,16},{28,20},{1,9},{5... | collective-permute-start | bytes 786440 | tf_op jit(solution)/shard_map/ppermute | solution.py:572
  (192 other events, 1557.6 us)
Sparse Core Ops, SparseCore 0:
  13.2 66.1 all-gather.5
  83.0 49.7 all-reduce.5
  141.9 80.1 all-gather.7
  223.6 44.4 all-gather.9
  285.3 43.6 reduce-scatter.3
  351.1 75.6 reduce-scatter.5
  467.6 78.7 reduce-scatter.7
  554.1 67.1 all-gather.11
